TPU v7x, 32 devices: a whole 2x2x4 slice. The times are simulated.
32 devices in a mesh: ref: 2 (over x), dp: 16 (over z, y, core).
Axes of the slice: x: 2, y: 2, z: 4, core: 2. Of those that a mesh axis runs over, the one named last changes fastest.
Arguments:
- particles: bfloat16 [32, 64, 4096], P(('ref', 'dp')), may hold values from -8 to 8
- references: bfloat16 [2, 64, 4096], P(None, 'dp'), may hold values from -6 to 6
- orient: int32 [16, 6], replicated, may hold values from 0 to 2, as said below
- allowed: int32 [32, 2], P(('ref', 'dp')), may hold values from 0 to 1, as said below
Outputs:
- sums: float32 [16, 64, 4096], P('ref', 'dp')
- log_evidence: float32 [32], P(('ref', 'dp'))
Inputs may be any that keep to these rules, and one draw needn't show every extreme that they name: `orient`: the first three entries of each row are a permutation of 0, 1, 2; the last three are 0 or 1. Every particle has at least one allowed class.
All inputs are finite; a program needn't handle non-finite values.
Results may differ from a plain program's by a relative error of at most 0.0027.
Values may be sent and summed in bfloat16 or wider, within the bound.
No kernel may reach another device: no remote copies, remote signals or barrier semaphores. Data moves between devices by JAX's collectives and lax.ppermute only.
A program may use at most 128 MiB of HBM per device.

v0:
```python
import math

import jax
import jax.numpy as jnp
from jax import lax
from jax.sharding import PartitionSpec as P

ORI = 8


MOVES = [(0, 0, 0), (1, 0, 0), (-1, 0, 0), (0, 1, 0), (0, -1, 0), (0, 0, 1), (0, 0, -1)]
ORDERS = [(0, 1, 2), (0, 2, 1), (1, 0, 2), (1, 2, 0), (2, 0, 1), (2, 1, 0)]


def as_sent(shard):

    def short(part):
        return part.astype(jnp.bfloat16) if part.dtype == jnp.float32 else part

    return jax.tree.map(short, shard)


def make_turn(order):

    def turn(volume):
        return jnp.transpose(volume, order)

    return turn


def rotate_flat(volume, code):
    edge = volume.shape[0]
    cube = volume.reshape(edge, edge, edge)
    which = jnp.int32(0)
    for number in range(len(ORDERS)):
        order = ORDERS[number]
        hit = (code[0] == order[0]) & (code[1] == order[1]) & (code[2] == order[2])
        which = which + hit.astype(jnp.int32) * number
    cube = lax.switch(which, [make_turn(order) for order in ORDERS], cube)
    for axis in range(3):
        cube = jnp.where(code[3 + axis] == 1, jnp.flip(cube, axis), cube)
    return cube.reshape(edge, edge * edge)


def rotate_many(whole, picks, codes):

    def single(pair):
        return rotate_flat(whole[pair[0]], pair[1])

    return lax.map(single, (picks, codes))


def roll_plane(volume, edge, step_y, step_z):
    moved = volume
    if step_y != 0:
        moved = jnp.roll(moved, -step_y * edge, axis=-1)
    if step_z != 0:
        column = jnp.arange(moved.shape[-1], dtype=jnp.int32) % edge
        if step_z == 1:
            moved = jnp.where(
                column == edge - 1, jnp.roll(moved, edge - 1, axis=-1), jnp.roll(moved, -1, axis=-1)
            )
        else:
            moved = jnp.where(
                column == 0, jnp.roll(moved, -(edge - 1), axis=-1), jnp.roll(moved, 1, axis=-1)
            )
    return moved


def posterior(logits, permit):
    logits = jnp.where(permit, logits, jnp.float32(-1e30))
    top = jnp.max(logits, axis=(0, 2))
    expo = jnp.exp(logits - top[None, :, None])
    total = jnp.sum(expo, axis=(0, 2))
    weights = (expo / total[None, :, None]).astype(jnp.bfloat16)
    return (weights, top + jnp.log(total))


def per_device(particles, references, orient, allowed):
    count, edge = (particles.shape[0], particles.shape[1])
    voxels = edge**3
    total_orient = orient.shape[0]
    scale = 3.0 / math.sqrt(voxels)
    classes = jnp.arange(total_orient, dtype=jnp.int32) // ORI
    whole = lax.all_gather(references, "dp", axis=1, tiled=True)
    owned = total_orient // lax.axis_size("ref")
    first = lax.axis_index("ref") * owned
    codes = lax.dynamic_slice_in_dim(orient, first, owned, 0)
    mine_classes = (first + jnp.arange(owned, dtype=jnp.int32)) // ORI
    mine = rotate_many(whole, mine_classes, codes)
    rotated = lax.all_gather(as_sent(mine), "ref", axis=0, tiled=True).astype(mine.dtype)
    flat_refs = rotated.reshape(total_orient, voxels)
    pieces = []
    for move in MOVES:
        piece = jnp.roll(particles, -move[0], axis=1) if move[0] != 0 else particles
        piece = roll_plane(piece, edge, move[1], move[2])
        pieces.append(piece.reshape(count, voxels))
    stacked = jnp.stack(pieces).reshape(len(MOVES) * count, voxels)
    logits = jnp.dot(stacked, flat_refs.T, preferred_element_type=jnp.float32) * scale
    logits = logits.reshape(len(MOVES), count, total_orient)
    permit = jnp.take(allowed, classes, axis=1)[None] == 1
    weights, log_evidence = posterior(logits, permit)
    flat_weights = weights.reshape(len(MOVES) * count, total_orient)
    partial_sums = jnp.dot(flat_weights.T, stacked, preferred_element_type=jnp.float32)
    partial_sums = partial_sums.reshape(total_orient, edge, edge * edge)
    slabs = lax.psum_scatter(partial_sums, "dp", scatter_dimension=1, tiled=True)
    sums = lax.psum_scatter(slabs, "ref", scatter_dimension=0, tiled=True)
    return (sums, log_evidence)


def solution(mesh):
    return jax.shard_map(
        per_device,
        mesh=mesh,
        in_specs=(P(("ref", "dp"), None, None), P(None, "dp", None), P(), P(("ref", "dp"), None)),
        out_specs=(P("ref", "dp", None), P(("ref", "dp"))),
        check_vma=False,
    )
```

profile of v0, /device:TPU:0, one launch (start us, length us, event | category | flops | bytes accessed | tf_op | source)
XLA Modules:
  0.0 544.6 jit_solution(4700597883820961579)
XLA Ops:
  7.2 1.5 copy.29
  9.0 42.4 %all-gather.3.cloned.1.call-done = bf16[2,64,4096]{2,0,1:T(2,128)(2,1)} async-done(((bf16[2,4,4096]{2,0,1:T(2,128)(2,1)}), bf16[2,64,4096]{2,0,1:T(2,128)(2,1)}) %all-gather.3.cloned.1.call-update) | async-done | bytes 1048592 | tf_op jit(solution)/shard_map/all_gather | solution.py:85
  51.4 2.8 copy.30
  54.2 150.2 %while.10 = (s32[]{:T(128)}, bf16[8,64,4096]{2,1,0:T(8,128)(2,1)}, s32[8,6]{1,0:T(8,128)S(1)}, s32[8]{0:T(128)S(1)}, bf16[2,64,4096]{2,1,0:T(8,128)(2,1)}, /*ind...) while((s32[]{:T(128)}, bf16[8,64,4096]{2,1,0:T(8,128)(2,1)}, ...), condition=%wide.region_7.8_spmd, body=%wide.region_0.7_spmd.sunk | while | flops 1048613 | bytes 14680630 | solution.py:50
  62.9 1.1 constant_dynamic-slice_fusion.6
  64.0 1.1 squeeze.22
  81.2 1.1 constant_dynamic-slice_fusion.6
  82.3 1.1 squeeze.22
  83.5 2.3 conditional.2
  83.6 2.2 copy.25
  102.1 1.1 squeeze.22
  103.3 1.4 conditional.2
  103.4 1.2 copy.23
  119.8 1.1 constant_dynamic-slice_fusion.6
  120.9 1.1 squeeze.22
  122.1 2.3 conditional.2
  122.2 2.2 copy.25
  139.6 1.1 constant_dynamic-slice_fusion.6
  140.7 1.1 squeeze.22
  157.9 1.1 constant_dynamic-slice_fusion.6
  158.9 1.1 squeeze.22
  176.1 1.1 constant_dynamic-slice_fusion.6
  177.2 1.1 squeeze.22
  194.3 1.1 constant_dynamic-slice_fusion.6
  195.4 1.1 squeeze.22
  196.6 1.4 conditional.2
  196.7 1.2 copy.23
  205.4 1.7 stack_reshape.17
  207.4 1.7 stack_reshape.18
  209.1 1.6 stack_reshape.19
  211.3 1.7 stack_reshape.20
  213.0 1.6 stack_reshape.21
  216.1 1.6 concatenate.53
  218.3 1.6 concatenate.55
  220.9 1.7 concatenate.57
  222.6 1.6 concatenate.59
  224.2 4.6 select_n.132
  228.8 3.3 select_n.133
  232.1 21.0 %stack.3 = bf16[7,1,262144]{2,0,1:T(8,128)(2,1)} concatenate(bf16[1,1,262144]{2,0,1:T(2,128)(2,1)S(1)} %copy-done.6, bf16[1,1,262144]{2,0,1:T(2,128)(2,1)} %stack_reshape.18, bf16[1,1,262144]{2,0,1:T(2,128)(2,1)} %stack_reshape.19, bf16[1,1,262144]{2,0,1:T(2,128)(2,1)} %stack_reshape.20, bf16[1,1,262144]{2,0,1:T(2,128)(2,1)} %stack_reshape.21, bf16[1,1,262144]{2,0,1:T(2,128)(2,1)} %select_n.132, ...), dimensions={0} | concatenate | bytes 7340032 | tf_op jit(solution)/shard_map/stack | solution.py:98
  253.7 1.3 fusion.18
  255.0 51.6 %all-gather.5.cloned.1.call-done = bf16[16,64,4096]{2,1,0:T(8,128)(2,1)} async-done(((bf16[8,64,4096]{2,1,0:T(8,128)(2,1)}), bf16[16,64,4096]{2,1,0:T(8,128)(2,1)}) %all-gather.5.cloned.1.call-update) | async-done | bytes 8388624 | tf_op jit(solution)/shard_map/all_gather | solution.py:91
  306.6 11.3 %copy.33 = bf16[2,8,64,4096]{3,1,2,0:T(8,128)(2,1)} copy(bf16[2,8,64,4096]{3,2,1,0:T(8,128)(2,1)} %bitcast.58) | data formatting | bytes 16777216
  317.9 7.3 %fusion.29 = (f32[]{:T(128)}, f32[7,16]{1,0:T(8,128)S(1)}) fusion(bf16[16,262144]{1,0:T(8,128)(2,1)} %bitcast.57, bf16[7,1,262144]{2,0,1:T(8,128)(2,1)S(1)} %copy-done.3, pred[16]{0:T(512)(128)(4,1)S(1)} %fusion.18), kind=kOutput, calls=%fused_computation.61 | convolution fusion | flops 58720592 | bytes 12059092 | tf_op jit(solution)/shard_map/dot_general | solution.py:99
  325.3 1.3 fusion.13
  326.5 8.0 %fusion.14 = f32[16,64,4096]{2,0,1:T(8,128)} fusion(bf16[64,4096,7]{1,2,0:T(8,128)(2,1)S(1)} %bitcast.56, f32[7,16]{1,0:T(8,128)S(1)} %get-tuple-element.89, f32[]{:T(128)} %fusion.13, f32[]{:T(128)} %get-tuple-element.88), kind=kOutput, calls=%fused_computation.31 | convolution fusion | flops 58720592 | bytes 20447688 | tf_op jit(solution)/shard_map/dot_general | solution.py:104
  334.7 178.7 %reduce-scatter.3.cloned.1.call-done = f32[16,4,4096]{2,0,1:T(8,128)} async-done(((f32[16,64,4096]{2,0,1:T(8,128)}), f32[16,4,4096]{2,0,1:T(8,128)}) %reduce-scatter.3.cloned.1.call-update) | async-done | bytes 1048592 | tf_op jit(solution)/shard_map/reduce_scatter | solution.py:106
  514.7 20.1 %reduce-scatter.5.cloned.1.call-done = f32[8,4,4096]{2,0,1:T(8,128)} async-done(((f32[16,4,4096]{2,0,1:T(8,128)}), f32[8,4,4096]{2,0,1:T(8,128)}) %reduce-scatter.5.cloned.1.call-update) | async-done | bytes 524304 | tf_op jit(solution)/shard_map/reduce_scatter | solution.py:107
  534.8 2.2 copy.31
  (160 shorter events, 60.2 us)
Async XLA Ops:
  7.2 1.7 copy-start
  7.2 44.2 %all-gather.3.cloned.1.call-start = ((), (), s32[]{:S(2)}) async-start(), calls=%async_computation.2 | async-start | bytes 1114112 | tf_op jit(solution)/shard_map/all_gather | solution.py:85
  8.8 297.8 %all-gather.5.cloned.1.call-start = ((), (), s32[]{:S(2)}) async-start(), calls=%async_computation.3 | async-start | bytes 12582912 | tf_op jit(solution)/shard_map/all_gather | solution.py:91
  204.4 1.0 copy-start.2
  204.4 308.9 %reduce-scatter.3.cloned.1.call-start = ((), (), s32[]{:S(2)}) async-start(), calls=%async_computation.4 | async-start | bytes 17825792 | tf_op jit(solution)/shard_map/reduce_scatter | solution.py:106
  224.2 4.6 copy-start.4
  224.2 4.6 copy-start.5
  228.8 3.3 copy-start.6
  232.1 21.0 %copy-start.7 = (s32[1,2]{1,0:T(1,128)S(1)}, s32[1,2]{1,0:T(1,128)}, u32[]{:S(2)}) copy-start(s32[1,2]{1,0:T(1,128)} %param.15) | copy-start | bytes 28
  306.6 11.3 %copy-start.3 = (bf16[7,1,262144]{2,0,1:T(8,128)(2,1)S(1)}, bf16[7,1,262144]{2,0,1:T(8,128)(2,1)}, u32[]{:S(2)}) copy-start(bf16[7,1,262144]{2,0,1:T(8,128)(2,1)} %stack.3) | copy-start | bytes 11010052
  334.6 202.4 %copy-start.1 = (s32[16,6]{0,1:T(8,128)S(1)}, s32[16,6]{0,1:T(8,128)}, u32[]{:S(2)}) copy-start(s32[16,6]{0,1:T(8,128)} %param.14) | copy-start | bytes 1156
  334.6 200.2 %reduce-scatter.5.cloned.1.call-start = ((), (), s32[]{:S(2)}) async-start(), calls=%async_computation.5 | async-start | bytes 1572864 | tf_op jit(solution)/shard_map/reduce_scatter | solution.py:107
Sparse Core Ops, SparseCore 0:
  10.7 40.6 all-gather.2
  204.5 102.0 all-gather.4
  334.7 178.5 reduce-scatter.2
  515.5 19.3 reduce-scatter.4
where the time goes:
time: 547 us; the launch traced here: 545 us
  waiting for transfers between devices  293 us (54%)
  local copies, waits for them, and re-layouts  126 us (23%)
  loops' own time  75.4 us (14%)
  other arithmetic  18.8 us (3%)
  between operations  16.4 us (3%)
  matrix products  15.4 us (3%)
    reduce_scatter x1, waiting for transfers between devices, per_device(): lax.psum_scatter(partial_sums, 'dp', scatter_dimension=1, tiled=True)  179 us
    another operation x1, loops' own time, rotate_many(): return lax.map(single, (picks, codes))  75 us
    all_gather x1, waiting for transfers between devices, per_device(): lax.all_gather(as_sent(mine), 'ref', axis=0, tiled=True).astype(mine.dtype)  51.6 us
    all_gather x1, waiting for transfers between devices, per_device(): whole = lax.all_gather(references, 'dp', axis=1, tiled=True)  42.4 us
    another operation x6, local copies, waits for them, and re-layouts, per_device(): stacked = jnp.stack(pieces).reshape(len(MOVES) * count, voxels)  29.3 us
    reduce_scatter x1, waiting for transfers between devices, per_device(): sums = lax.psum_scatter(slabs, 'ref', scatter_dimension=0, tiled=True)  20.1 us
    unnamed x20, local copies, waits for them, and re-layouts  16 us
  transfers between devices with their start and end apart: 4, of which 4 were waited for; matrix products, arithmetic and copies ran while one was open for 9% of the time, Pallas kernels for 0%

commit v1 on v0

v1 whole, which is shorter than its diff:
```python
import functools
import math

import jax
import jax.numpy as jnp
from jax import lax
from jax.experimental import pallas as pl
from jax.experimental.pallas import tpu as pltpu
from jax.sharding import PartitionSpec as P

ORI = 8
LANES = 128
ROWS = 8
MOVES = [(0, 0, 0), (1, 0, 0), (-1, 0, 0), (0, 1, 0), (0, -1, 0), (0, 0, 1), (0, 0, -1)]
FLAT = [(0, 0), (1, 0), (-1, 0), (0, 1), (0, -1)]
SLOTS = 8
BARRED = -1e30
VMEM_BYTES = 48 * 1024 * 1024


def lane_iota(shape):
    return lax.broadcasted_iota(jnp.int32, shape, len(shape) - 1)


def swap_halves(x):
    return pltpu.roll(x, LANES // 2, 1)


def transpose_planes(source, target, planes, edge):
    for n in range(0, planes, 2):
        turned = source[n * edge : (n + 2) * edge, :].T[:edge, :]
        target[n * edge : (n + 1) * edge, :] = turned
        target[(n + 1) * edge : (n + 2) * edge, :] = swap_halves(turned)


def flatten_planes(source, planes, edge, store):
    low = lane_iota((planes, LANES)) < edge
    for m in range(edge // 2):
        even = source[pl.ds(2 * m, planes, stride=edge), :]
        odd = source[pl.ds(2 * m + 1, planes, stride=edge), :]
        store(m, jnp.where(low, even, swap_halves(odd)))


def pack_kernel(edge, parts, part_ref, refs_ref, out_ref, both_ref, ring, stage, x, z, flat, turned):
    h = edge // parts
    planes = 2 * h
    wide = edge * edge
    spare = ROWS - h - 2
    span = 4 * h * edge
    ring[ROWS : ROWS + edge, :] = part_ref[...].astype(jnp.float32)
    ring[ROWS - 1 : ROWS, :] = ring[ROWS + edge - 1 : ROWS + edge, :]
    ring[ROWS + edge : ROWS + edge + 1, :] = ring[ROWS : ROWS + 1, :]
    for c in range(2):
        x[c * h : (c + 1) * h, :] = refs_ref[c].astype(jnp.float32)
    for m in range(edge // 2):
        piece = x[:planes, m * LANES : (m + 1) * LANES]
        flat[pl.ds(2 * m, planes, stride=edge), :] = piece
        flat[pl.ds(2 * m + 1, planes, stride=edge), :] = swap_halves(piece)
    transpose_planes(flat, turned, planes, edge)

    def store(m, value):
        z[:planes, m * LANES : (m + 1) * LANES] = value

    flatten_planes(turned, planes, edge, store)
    if planes // spare * span < wide:
        stage[...] = jnp.zeros_like(stage)
    slab = h * edge
    for s in range(parts):
        top = s * ROWS
        stage[top : top + h + 2, :] = ring[ROWS + h * s - 1 : ROWS + h * s + h + 1, :]
        mirror = parts - 1 - s
        for q in range(planes // spare):
            rows = slice(q * spare, (q + 1) * spare)
            for number, (array, place) in enumerate(((x, s), (x, mirror), (z, s), (z, mirror))):
                left = q * span + number * slab
                stage[top + h + 2 : top + ROWS, left : left + slab] = array[rows, place * slab : (place + 1) * slab]
    out_ref[...] = stage[...].astype(jnp.bfloat16)
    both_ref[...] = jnp.concatenate([x[:planes, :], z[:planes, :]], axis=0).astype(jnp.bfloat16)


def logits_kernel(
    edge, parts, total, devices, scale,
    orient_ref, allowed_ref, got_ref, own_ref, far_ref, out_ref,
    wide_f32, flat, turned, kinds, rotated, shifted,
):
    h = edge // parts
    planes = 2 * h
    wide = edge * edge
    columns = wide // LANES
    spare = ROWS - h - 2
    span = 4 * h * edge
    me = lax.axis_index("dp")
    for j in range(columns):
        wide_f32[j] = got_ref[:, j * LANES : (j + 1) * LANES].astype(jnp.float32)
    own = own_ref[...].astype(jnp.float32)
    far = far_ref[...].astype(jnp.float32)
    for turn in range(2):
        kinds[2 * turn, :planes, :] = own[turn * planes : (turn + 1) * planes, :]
        for c in range(2):
            for l in range(h):
                row = turn * planes + c * h + h - 1 - l
                kinds[2 * turn + 1, c * h + l : c * h + l + 1, :] = far[row : row + 1, :]
    for axis in (1, 2):
        for side in range(2):
            for c in range(2):
                for jl in range(h):
                    q, e = divmod(c * h + jl, spare)
                    for pair in range(h // 2):
                        left = q * span + (axis - 1) * 2 * h * edge + side * h * edge + pair * LANES
                        for s in range(0, parts, ROWS):
                            block = wide_f32[left // LANES, pl.ds(s * ROWS + h + 2 + e, ROWS, stride=ROWS), :]
                            for parity in range(2):
                                l = 2 * pair + parity
                                if side == 1:
                                    l = h - 1 - l
                                base = (c * h + l) * edge + s * h + jl
                                flat[pl.ds(base, ROWS, stride=h), :] = swap_halves(block) if parity else block
            transpose_planes(flat, turned, planes, edge)
            for turn, planar in enumerate((flat, turned)):
                kind = axis * 4 + turn * 2 + side

                def store(m, value, kind=kind):
                    kinds[kind, :planes, m * LANES : (m + 1) * LANES] = value

                flatten_planes(planar, planes, edge, store)
    lane = lane_iota((ROWS, LANES))
    for o in range(total):
        c = o // ORI
        axis, first, second = (orient_ref[o, k] for k in range(3))
        flips = [orient_ref[o, 3 + k] for k in range(3)]
        turn = (first > second).astype(jnp.int32)
        kind = axis * 4 + turn * 2 + flips[0]
        index = lane ^ (flips[1] * edge + flips[2] * (edge - 1))
        for j in range(columns):
            at = j + flips[1] * (columns - 1 - 2 * j)
            value = kinds[kind, :, pl.ds(pl.multiple_of(at * LANES, LANES), LANES)]
            value = jnp.take_along_axis(value, index, axis=1, mode="promise_in_bounds")
            rotated[o * h : (o + 1) * h, j * LANES : (j + 1) * LANES] = value[c * h : (c + 1) * h, :]
    rows = total * h
    lane = lane_iota((rows, LANES))
    low = lane < edge
    after = (lane // edge) * edge + (lane + 1) % edge
    before = (lane // edge) * edge + (lane + edge - 1) % edge

    def swapped(j):
        j = j % columns
        return swap_halves(rotated[:, j * LANES : (j + 1) * LANES])

    for j in range(columns):
        at = slice(j * LANES, (j + 1) * LANES)
        value = rotated[:, at]
        here = swapped(j)
        results = [
            value,
            jnp.where(low, swapped(j - 1), here),
            jnp.where(low, here, swapped(j + 1)),
            jnp.take_along_axis(value, before, axis=1, mode="promise_in_bounds"),
            jnp.take_along_axis(value, after, axis=1, mode="promise_in_bounds"),
        ]
        for number, result in enumerate(results):
            shifted[number * rows : (number + 1) * rows, at] = result.astype(jnp.bfloat16)
    gram = lax.dot_general(
        shifted[...], got_ref[...], (((1,), (1,)), ((), ())), preferred_element_type=jnp.float32
    )
    many = parts * ROWS
    plane = lax.broadcasted_iota(jnp.int32, (rows, many), 0) % h
    mate = lax.broadcasted_iota(jnp.int32, (rows, many), 1) % ROWS
    kept = []
    for t, move in enumerate(MOVES):
        source = FLAT.index((move[1], move[2]))
        block = gram[source * rows : (source + 1) * rows, :]
        kept.append(jnp.where(mate == plane + 1 + move[0], block, 0.0))
    kept = jnp.concatenate(kept, axis=1)
    tall = lax.broadcasted_iota(jnp.int32, (total, rows), 1) // h
    adder = (tall == lax.broadcasted_iota(jnp.int32, (total, rows), 0)).astype(jnp.float32)
    shape = (len(MOVES) * many, SLOTS * parts)
    source = lax.broadcasted_iota(jnp.int32, shape, 0) // ROWS
    picker = (source == lax.broadcasted_iota(jnp.int32, shape, 1)).astype(jnp.float32)
    exact = functools.partial(jnp.dot, preferred_element_type=jnp.float32, precision=lax.Precision.HIGHEST)
    result = exact(exact(adder, kept), picker) * scale
    where = lax.broadcasted_iota(jnp.int32, result.shape, 1)
    kin = lax.broadcasted_iota(jnp.int32, result.shape, 0) // ORI
    permit = jnp.zeros(result.shape, jnp.int32)
    for c in range(total // ORI):
        permit = jnp.where(kin == c, allowed_ref[0, c], permit)
    barred = (where % parts == me) & (permit == 0)
    result = result + jnp.where(barred, jnp.float32(BARRED), jnp.float32(0.0))
    for d in range(devices):
        out_ref[d * total : (d + 1) * total, :] = result


def sums_kernel(edge, parts, total, groups, *refs):
    parts_in = refs[1 : 1 + groups]
    logits_ref = refs[0]
    out_ref, log_ref, chances, table = refs[1 + groups :]
    h = edge // parts
    wide = edge * edge
    columns = wide // LANES
    owned = total // groups
    rows = owned * h
    many = parts * ROWS
    span = SLOTS * parts
    mine, me = lax.axis_index("ref"), lax.axis_index("dp")
    lane = lane_iota((total, span))
    log_evidence = jnp.zeros((1, span), jnp.float32)
    for g in range(groups):
        score = logits_ref[g * parts * total : (g * parts + 1) * total, :]
        for s in range(1, parts):
            top = (g * parts + s) * total
            score = score + logits_ref[top : top + total, :]
        score = jnp.where(lane >= len(MOVES) * parts, jnp.float32(-3e38), score)
        peak = jnp.max(score, axis=0, keepdims=True)
        for step in (1, 2, 4):
            peak = jnp.maximum(peak, pltpu.roll(peak, step * parts, 1))
        expo = jnp.exp(score - peak)
        mass = jnp.sum(expo, axis=0, keepdims=True)
        for step in (1, 2, 4):
            mass = mass + pltpu.roll(mass, step * parts, 1)
        chances[g] = (expo / mass).astype(jnp.bfloat16)
        log_evidence = jnp.where(mine == g, peak + jnp.log(mass), log_evidence)
    log_ref[...] = jnp.sum(jnp.where(lane_iota((1, span)) == me, log_evidence, 0.0), axis=1, keepdims=True)
    at = mine * owned + lax.broadcasted_iota(jnp.int32, (rows, total), 0) // h
    chooser = (at == lax.broadcasted_iota(jnp.int32, (rows, total), 1)).astype(jnp.bfloat16)
    shape = (span, len(MOVES) * many)
    target = lax.broadcasted_iota(jnp.int32, shape, 1) // ROWS
    spread = (target == lax.broadcasted_iota(jnp.int32, shape, 0)).astype(jnp.bfloat16)
    plane = lax.broadcasted_iota(jnp.int32, (rows, many), 0) % h
    mate = lax.broadcasted_iota(jnp.int32, (rows, many), 1) % ROWS
    dot = functools.partial(jnp.dot, preferred_element_type=jnp.float32)
    total_sums = None
    for k in range(groups):
        g = lax.rem(mine + groups - k, groups)
        chosen = dot(chooser, chances[g]).astype(jnp.bfloat16)
        laid = dot(chosen, spread)
        blocks = [jnp.zeros((rows, many), jnp.float32)] * len(FLAT)
        for t, move in enumerate(MOVES):
            slot = FLAT.index((move[1], move[2]))
            block = laid[:, t * many : (t + 1) * many]
            blocks[slot] = jnp.where(mate == plane + 1 + move[0], block, blocks[slot])
        weights = jnp.concatenate(blocks, axis=0).astype(jnp.bfloat16)
        part = dot(weights, parts_in[k][...])
        if k == 0:
            table[...] = part
        else:
            table[...] += part
    lane = lane_iota((rows, LANES))
    low = lane < edge
    after = (lane // edge) * edge + (lane + 1) % edge
    before = (lane // edge) * edge + (lane + edge - 1) % edge

    def cut(slot, j):
        j = j % columns
        return table[slot * rows : (slot + 1) * rows, j * LANES : (j + 1) * LANES]

    for j in range(columns):
        value = cut(0, j)
        value = value + jnp.where(low, swap_halves(cut(1, j)), swap_halves(cut(1, j + 1)))
        value = value + jnp.where(low, swap_halves(cut(2, j - 1)), swap_halves(cut(2, j)))
        value = value + jnp.take_along_axis(cut(3, j), after, axis=1, mode="promise_in_bounds")
        value = value + jnp.take_along_axis(cut(4, j), before, axis=1, mode="promise_in_bounds")
        for o in range(owned):
            out_ref[o, :, j * LANES : (j + 1) * LANES] = value[o * h : (o + 1) * h, :]


def in_vmem():
    return pl.BlockSpec(memory_space=pltpu.VMEM)


def in_smem():
    return pl.BlockSpec(memory_space=pltpu.SMEM)


def per_device(particles, references, orient, allowed):
    edge = particles.shape[1]
    wide = edge * edge
    total = orient.shape[0]
    parts = lax.axis_size("dp")
    groups = lax.axis_size("ref")
    devices = parts * groups
    h = edge // parts
    planes = 2 * h
    scale = 3.0 / math.sqrt(edge**3)
    params = pltpu.CompilerParams(vmem_limit_bytes=VMEM_BYTES)
    f32, bf16 = jnp.float32, jnp.bfloat16
    sent, both = pl.pallas_call(
        functools.partial(pack_kernel, edge, parts),
        out_shape=(
            jax.ShapeDtypeStruct((parts * ROWS, wide), bf16),
            jax.ShapeDtypeStruct((2 * planes, wide), bf16),
        ),
        in_specs=[in_vmem()] * 2,
        out_specs=(in_vmem(), in_vmem()),
        scratch_shapes=[
            pltpu.VMEM((edge + 2 * ROWS, wide), f32),
            pltpu.VMEM((parts * ROWS, wide), f32),
            pltpu.VMEM((ROWS, wide), f32),
            pltpu.VMEM((ROWS, wide), f32),
            pltpu.VMEM((planes * edge, LANES), f32),
            pltpu.VMEM((planes * edge, LANES), f32),
        ],
        compiler_params=params,
        name="pack",
    )(particles.reshape(edge, wide), references)
    far = lax.ppermute(both, "dp", [(i, parts - 1 - i) for i in range(parts)])
    got = lax.all_to_all(sent, "dp", 0, 0, tiled=True)
    others = [
        lax.ppermute(got, "ref", [(i, (i + k) % groups) for i in range(groups)]) for k in range(1, groups)
    ]
    rows = total * h
    partial = pl.pallas_call(
        functools.partial(logits_kernel, edge, parts, total, devices, scale),
        out_shape=jax.ShapeDtypeStruct((devices * total, SLOTS * parts), f32),
        in_specs=[in_smem(), in_smem(), in_vmem(), in_vmem(), in_vmem()],
        out_specs=in_vmem(),
        scratch_shapes=[
            pltpu.VMEM((wide // LANES, parts * ROWS, LANES), f32),
            pltpu.VMEM((planes * edge, LANES), f32),
            pltpu.VMEM((planes * edge, LANES), f32),
            pltpu.VMEM((12, ROWS, wide), f32),
            pltpu.VMEM((rows, wide), f32),
            pltpu.VMEM((len(FLAT) * rows, wide), bf16),
        ],
        compiler_params=params,
        name="logits",
    )(orient, allowed, got, both, far)
    logits = lax.all_to_all(partial, ("ref", "dp"), 0, 0, tiled=True)
    owned = total // groups
    sums, log_evidence = pl.pallas_call(
        functools.partial(sums_kernel, edge, parts, total, groups),
        out_shape=(
            jax.ShapeDtypeStruct((owned, h, wide), f32),
            jax.ShapeDtypeStruct((1, 1), f32),
        ),
        in_specs=[in_vmem()] * (1 + groups),
        out_specs=(in_vmem(), in_vmem()),
        scratch_shapes=[
            pltpu.VMEM((groups, total, SLOTS * parts), bf16),
            pltpu.VMEM((len(FLAT) * owned * h, wide), f32),
        ],
        compiler_params=params,
        name="sums",
    )(logits, got, *others)
    return (sums, log_evidence.reshape(1))


def solution(mesh):
    return jax.shard_map(
        per_device,
        mesh=mesh,
        in_specs=(P(("ref", "dp"), None, None), P(None, "dp", None), P(), P(("ref", "dp"), None)),
        out_specs=(P("ref", "dp", None), P(("ref", "dp"))),
        check_vma=False,
    )
```

time: 547 us -> 69 us (0.13)
  waiting for transfers between devices: 293 us -> 4.66 us
  local copies, waits for them, and re-layouts: 126 us -> 1.97 us
  loops' own time: 75.4 us -> 0 us
  blocking collectives: 0 us -> 46.5 us
  other arithmetic: 18.8 us -> 0 us
  between operations: 16.4 us -> 0.67 us
  matrix products: 15.4 us -> 0 us
  Pallas kernels: 0 us -> 10.2 us
    reduce_scatter x2 -> x0, waiting for transfers between devices: 199 us -> none  [the longest x1 179 us: per_device(): lax.psum_scatter(partial_sums, 'dp', scatter_dimension=1, tiled=True)]
    all_gather x2 -> x0, waiting for transfers between devices: 93.9 us -> none  [the longest x1 51.6 us: per_device(): lax.all_gather(as_sent(mine), 'ref', axis=0, tiled=True).astype(mine.dtype)]
    another operation x9 -> x0, loops' own time: 75.4 us -> none  [the longest x1 75 us: rotate_many(): return lax.map(single, (picks, codes))]
    all_to_all x0 -> x2, blocking collectives: none -> 46.5 us  [the longest x1 32 us: per_device(): got = lax.all_to_all(sent, 'dp', 0, 0, tiled=True)]
    another operation x6 -> x0, local copies, waits for them, and re-layouts: 29.3 us -> none  [per_device(): stacked = jnp.stack(pieces).reshape(len(MOVES) * count, voxels)]
    squeeze x16 -> x0, local copies, waits for them, and re-layouts: 18.6 us -> none
    select_n x27 -> x0, other arithmetic: 15.4 us -> none  [the longest x24 7.49 us: rotate_flat(): cube = jnp.where(code[3 + axis] == 1, jnp.flip(cube, axis), cube)]
    dot_general x2 -> x0, matrix products: 15.4 us -> none  [the longest x1 8.05 us: per_device(): jnp.dot(flat_weights.T, stacked, preferred_element_type=jnp.float32)]
  transfers between devices with their start and end apart: 4 -> 2, of which waited for: 4 -> 1; matrix products, arithmetic and copies ran while one was open for 9% -> 0% of each run, Pallas kernels for 0% -> 8%
where the time goes in v1:
time: 69 us; the launch traced here: 68.7 us
  blocking collectives  46.5 us (67%)
  Pallas kernels  10.2 us (15%)
  starting transfers between devices  4.72 us (7%)
  waiting for transfers between devices  4.66 us (7%)
  local copies, waits for them, and re-layouts  1.97 us (3%)
    all_to_all x1, blocking collectives, per_device(): got = lax.all_to_all(sent, 'dp', 0, 0, tiled=True)  32 us
    all_to_all x1, blocking collectives, per_device(): logits = lax.all_to_all(partial, ('ref', 'dp'), 0, 0, tiled=True)  14.5 us
    pallas_call x1, Pallas kernels, per_device(): pl.pallas_call(functools.partial(logits_kernel, edge, parts, total, devic...  5.75 us
    ppermute x1, waiting for transfers between devices, per_device(): far = lax.ppermute(both, 'dp', [(i, parts - 1 - i) for i in range(parts)])  4.66 us
    pallas_call x1, Pallas kernels, per_device(): pl.pallas_call(functools.partial(sums_kernel, edge, parts, total, groups)...  3.25 us
    ppermute x1, starting transfers between devices, per_device(): far = lax.ppermute(both, 'dp', [(i, parts - 1 - i) for i in range(parts)])  3.23 us
    unnamed x9, local copies, waits for them, and re-layouts  1.97 us
    ppermute x1, starting transfers between devices, per_device(): lax.ppermute(got, 'ref', [(i, (i + k) % groups) for i in range(groups)])  1.49 us
  transfers between devices with their start and end apart: 2, of which 1 were waited for; matrix products, arithmetic and copies ran while one was open for 0% of the time, Pallas kernels for 8%

profile of v1, /device:TPU:0, one launch (start us, length us, event | category | flops | bytes accessed | tf_op | source)
XLA Modules:
  0.0 68.7 jit_solution(12687321125155822878)
XLA Ops:
  0.6 0.0 copy-start
  0.6 1.0 %copy-done = bf16[1,64,4096]{2,1,0:T(8,128)(2,1)S(1)} copy-done((bf16[1,64,4096]{2,1,0:T(8,128)(2,1)S(1)}, bf16[1,64,4096]{2,1,0:T(8,128)(2,1)}, u32[]{:S(2)}) %copy-start) | copy-done | bytes 524312
  1.7 0.0 copy-start.1
  1.7 0.8 %copy-done.1 = bf16[2,4,4096]{2,1,0:T(4,128)(2,1)S(1)} copy-done((bf16[2,4,4096]{2,1,0:T(4,128)(2,1)S(1)}, bf16[2,4,4096]{2,1,0:T(4,128)(2,1)}, u32[]{:S(2)}) %copy-start.1) | copy-done | bytes 65560
  2.5 1.2 %pack.1 = (bf16[128,4096]{1,0:T(8,128)(2,1)S(1)}, bf16[16,4096]{1,0:T(8,128)(2,1)S(1)}) custom-call(bf16[64,4096]{1,0:T(8,128)(2,1)S(1)} %bitcast.12, bf16[2,4,4096]{2,1,0:T(4,128)(2,1)S(1)} %copy-done.1), custom_call_target="tpu_custom_call" | custom-call | tf_op jit(solution)/shard_map/pack/pallas_call | solution.py:285
  3.7 0.0 copy-start.3
  3.7 32.0 %all_to_all.22 = bf16[16,8,4096]{2,1,0:T(8,128)(2,1)S(1)} all-to-all(bf16[16,8,4096]{2,1,0:T(8,128)(2,1)S(1)} %bitcast.10), channel_id=1, replica_groups=mesh['ref'=2,'dp'=16] {'dp'}, dimensions={0} | all-to-all | bytes 2097152 | tf_op jit(solution)/shard_map/all_to_all | solution.py:305
  35.7 1.5 %collective-permute-start.1 = (bf16[128,4096]{1,0:T(8,128)(2,1)S(1)}, bf16[128,4096]{1,0:T(8,128)(2,1)S(1)}, u32[]{:S(2)}, u32[]{:S(2)}) collective-permute-start(bf16[128,4096]{1,0:T(8,128)(2,1)S(1)} %bitcast.6), channel_id=1, source_target_pairs={{0,16},{16,0},{1,17},{17,1},{2,18},{18,2},{3,19},{19,3},{4,20},{20... | collective-permute-start | bytes 3145736 | tf_op jit(solution)/shard_map/ppermute | solution.py:307
  37.2 0.0 copy-start.2
  37.2 3.2 %collective-permute-start = (bf16[16,4096]{1,0:T(8,128)(2,1)S(1)}, bf16[16,4096]{1,0:T(8,128)(2,1)S(1)}, u32[]{:S(2)}, u32[]{:S(2)}) collective-permute-start(bf16[16,4096]{1,0:T(8,128)(2,1)S(1)} %get-tuple-element.7.own_ref), channel_id=1, source_target_pairs={{0,15},{1,14},{2,13},{3,12},{4,11},{5,10},{6,9},{7,8},{8,7},{9,6},... | collective-permute-start | bytes 393224 | tf_op jit(solution)/shard_map/ppermute | solution.py:304
  40.5 0.0 copy-done.3
  40.5 0.1 copy.6.orient_ref
  40.6 4.7 %collective-permute-done.far_ref = bf16[16,4096]{1,0:T(8,128)(2,1)S(1)} collective-permute-done((bf16[16,4096]{1,0:T(8,128)(2,1)S(1)}, bf16[16,4096]{1,0:T(8,128)(2,1)S(1)}, u32[]{:S(2)}, u32[]{:S(2)}) %collective-permute-start) | collective-permute-done | bytes 131104 | tf_op jit(solution)/shard_map/ppermute | solution.py:304
  45.2 0.0 copy-done.2
  45.2 5.8 %logits.1 = f32[512,128]{1,0:T(8,128)S(1)} custom-call(s32[16,6]{1,0:T(8,128)S(1)} %copy.6.orient_ref, s32[1,2]{1,0:T(1,128)S(1)} %copy-done.2, bf16[128,4096]{1,0:T(8,128)(2,1)S(1)} %bitcast.7, bf16[16,4096]{1,0:T(8,128)(2,1)S(1)} %get-tuple-element.7.own_ref, bf16[16,4096]{1,0:T(8,128)(2,1)S(1)} %collective-permute-done.far_ref), custom_call_target="tpu_custom_call" | custom-call | tf_op jit(solution)/shard_map/logits/pallas_call | solution.py:310
  51.0 14.5 %all_to_all.23 = f32[32,16,128]{2,1,0:T(8,128)S(1)} all-to-all(f32[32,16,128]{2,1,0:T(8,128)S(1)} %bitcast.11), channel_id=1, replica_groups=mesh['ref'=2,'dp'=16] {'ref','dp'}, dimensions={0} | all-to-all | bytes 524288 | tf_op jit(solution)/shard_map/all_to_all | solution.py:326
  65.5 0.0 collective-permute-done.1.refs_2_
  65.5 3.3 %sums.1 = (f32[8,4,4096]{2,1,0:T(4,128)}, f32[1,1]{1,0:T(1,128)}) custom-call(f32[512,128]{1,0:T(8,128)S(1)} %bitcast.9, bf16[128,4096]{1,0:T(8,128)(2,1)S(1)} %bitcast.8, bf16[128,4096]{1,0:T(8,128)(2,1)S(1)} %collective-permute-done.1.refs_2_), custom_call_target="tpu_custom_call" | custom-call | tf_op jit(solution)/shard_map/sums/pallas_call | solution.py:328
Async XLA Ops:
  0.6 1.0 %copy-start = (bf16[1,64,4096]{2,1,0:T(8,128)(2,1)S(1)}, bf16[1,64,4096]{2,1,0:T(8,128)(2,1)}, u32[]{:S(2)}) copy-start(bf16[1,64,4096]{2,1,0:T(8,128)(2,1)} %param.4) | copy-start | bytes 1572868
  1.7 0.8 %copy-start.1 = (bf16[2,4,4096]{2,1,0:T(4,128)(2,1)S(1)}, bf16[2,4,4096]{2,1,0:T(4,128)(2,1)}, u32[]{:S(2)}) copy-start(bf16[2,4,4096]{2,1,0:T(4,128)(2,1)} %refs_ref.1) | copy-start | bytes 196612
  3.7 36.8 %copy-start.3 = (s32[16,6]{0,1:T(8,128)S(1)}, s32[16,6]{0,1:T(8,128)}, u32[]{:S(2)}) copy-start(s32[16,6]{0,1:T(8,128)} %param.6) | copy-start | bytes 1156
  35.7 29.7 %collective-permute-start.1 = (bf16[128,4096]{1,0:T(8,128)(2,1)S(1)}, bf16[128,4096]{1,0:T(8,128)(2,1)S(1)}, u32[]{:S(2)}, u32[]{:S(2)}) collective-permute-start(bf16[128,4096]{1,0:T(8,128)(2,1)S(1)} %bitcast.6), channel_id=1, source_target_pairs={{0,16},{16,0},{1,17},{17,1},{2,18},{18,2},{3,19},{19,3},{4,20},{20... | collective-permute-start | bytes 3145736 | tf_op jit(solution)/shard_map/ppermute | solution.py:307
  37.2 8.0 %copy-start.2 = (s32[1,2]{1,0:T(1,128)S(1)}, s32[1,2]{1,0:T(1,128)}, u32[]{:S(2)}) copy-start(s32[1,2]{1,0:T(1,128)} %allowed_ref.1) | copy-start | bytes 28
  37.2 8.0 %collective-permute-start = (bf16[16,4096]{1,0:T(8,128)(2,1)S(1)}, bf16[16,4096]{1,0:T(8,128)(2,1)S(1)}, u32[]{:S(2)}, u32[]{:S(2)}) collective-permute-start(bf16[16,4096]{1,0:T(8,128)(2,1)S(1)} %get-tuple-element.7.own_ref), channel_id=1, source_target_pairs={{0,15},{1,14},{2,13},{3,12},{4,11},{5,10},{6,9},{7,8},{8,7},{9,6},... | collective-permute-start | bytes 393224 | tf_op jit(solution)/shard_map/ppermute | solution.py:304

commit v2 on v1

--- a/solution.py
+++ b/solution.py
@@ -16,6 +16,7 @@
 SLOTS = 8
 BARRED = -1e30
 VMEM_BYTES = 48 * 1024 * 1024
+MOST_VMEM = 62 * 1024 * 1024
 
 
 def lane_iota(shape):
@@ -41,27 +42,39 @@
         store(m, jnp.where(low, even, swap_halves(odd)))
 
 
-def pack_kernel(edge, parts, part_ref, refs_ref, out_ref, both_ref, ring, stage, x, z, flat, turned):
+def turn_rows(edge, planes, x, z, flat, turned):
+    for m in range(edge // 2):
+        piece = x[:planes, m * LANES : (m + 1) * LANES]
+        flat[pl.ds(2 * m, planes, stride=edge), :] = piece
+        flat[pl.ds(2 * m + 1, planes, stride=edge), :] = swap_halves(piece)
+    transpose_planes(flat, turned, planes, edge)
+
+    def store(m, value):
+        z[:planes, m * LANES : (m + 1) * LANES] = value
+
+    flatten_planes(turned, planes, edge, store)
+
+
+def pack_kernel(
+    edge, parts, part_hbm, refs_hbm, out_ref, both_ref, part_ref, refs_ref, sems, ring, stage, x, z, flat, turned
+):
     h = edge // parts
     planes = 2 * h
     wide = edge * edge
     spare = ROWS - h - 2
     span = 4 * h * edge
+    refs_copy = pltpu.make_async_copy(refs_hbm, refs_ref, sems.at[0])
+    part_copy = pltpu.make_async_copy(part_hbm, part_ref, sems.at[1])
+    refs_copy.start()
+    part_copy.start()
+    refs_copy.wait()
+    for c in range(2):
+        x[c * h : (c + 1) * h, :] = refs_ref[c].astype(jnp.float32)
+    turn_rows(edge, planes, x, z, flat, turned)
+    part_copy.wait()
     ring[ROWS : ROWS + edge, :] = part_ref[...].astype(jnp.float32)
     ring[ROWS - 1 : ROWS, :] = ring[ROWS + edge - 1 : ROWS + edge, :]
     ring[ROWS + edge : ROWS + edge + 1, :] = ring[ROWS : ROWS + 1, :]
-    for c in range(2):
-        x[c * h : (c + 1) * h, :] = refs_ref[c].astype(jnp.float32)
-    for m in range(edge // 2):
-        piece = x[:planes, m * LANES : (m + 1) * LANES]
-        flat[pl.ds(2 * m, planes, stride=edge), :] = piece
-        flat[pl.ds(2 * m + 1, planes, stride=edge), :] = swap_halves(piece)
-    transpose_planes(flat, turned, planes, edge)
-
-    def store(m, value):
-        z[:planes, m * LANES : (m + 1) * LANES] = value
-
-    flatten_planes(turned, planes, edge, store)
     if planes // spare * span < wide:
         stage[...] = jnp.zeros_like(stage)
     slab = h * edge
@@ -78,9 +91,23 @@
     both_ref[...] = jnp.concatenate([x[:planes, :], z[:planes, :]], axis=0).astype(jnp.bfloat16)
 
 
+def near_kernel(h, edge, own_ref, far_ref, out_ref, x, z, flat, turned):
+    planes = 2 * h
+    own = own_ref[...].astype(jnp.float32)
+    for c in range(2):
+        far = far_ref[c].astype(jnp.float32)
+        for l in range(h):
+            x[c * h + l : c * h + l + 1, :] = far[h - 1 - l : h - l, :]
+    turn_rows(edge, planes, x, z, flat, turned)
+    for turn in range(2):
+        out_ref[2 * turn, :planes, :] = own[turn * planes : (turn + 1) * planes, :]
+    out_ref[1, :planes, :] = x[:planes, :]
+    out_ref[3, :planes, :] = z[:planes, :]
+
+
 def logits_kernel(
     edge, parts, total, devices, scale,
-    orient_ref, allowed_ref, got_ref, own_ref, far_ref, out_ref,
+    orient_ref, allowed_ref, got_ref, near_ref, out_ref,
     wide_f32, flat, turned, kinds, rotated, shifted,
 ):
     h = edge // parts
@@ -92,14 +119,7 @@
     me = lax.axis_index("dp")
     for j in range(columns):
         wide_f32[j] = got_ref[:, j * LANES : (j + 1) * LANES].astype(jnp.float32)
-    own = own_ref[...].astype(jnp.float32)
-    far = far_ref[...].astype(jnp.float32)
-    for turn in range(2):
-        kinds[2 * turn, :planes, :] = own[turn * planes : (turn + 1) * planes, :]
-        for c in range(2):
-            for l in range(h):
-                row = turn * planes + c * h + h - 1 - l
-                kinds[2 * turn + 1, c * h + l : c * h + l + 1, :] = far[row : row + 1, :]
+    kinds[:4] = near_ref[...]
     for axis in (1, 2):
         for side in range(2):
             for c in range(2):
@@ -198,7 +218,6 @@
     columns = wide // LANES
     owned = total // groups
     rows = owned * h
-    many = parts * ROWS
     span = SLOTS * parts
     mine, me = lax.axis_index("ref"), lax.axis_index("dp")
     lane = lane_iota((total, span))
@@ -221,22 +240,27 @@
     log_ref[...] = jnp.sum(jnp.where(lane_iota((1, span)) == me, log_evidence, 0.0), axis=1, keepdims=True)
     at = mine * owned + lax.broadcasted_iota(jnp.int32, (rows, total), 0) // h
     chooser = (at == lax.broadcasted_iota(jnp.int32, (rows, total), 1)).astype(jnp.bfloat16)
-    shape = (span, len(MOVES) * many)
-    target = lax.broadcasted_iota(jnp.int32, shape, 1) // ROWS
-    spread = (target == lax.broadcasted_iota(jnp.int32, shape, 0)).astype(jnp.bfloat16)
-    plane = lax.broadcasted_iota(jnp.int32, (rows, many), 0) % h
-    mate = lax.broadcasted_iota(jnp.int32, (rows, many), 1) % ROWS
+
+    def tables(each):
+        many = parts * each
+        shape = (span, len(MOVES) * many)
+        target = lax.broadcasted_iota(jnp.int32, shape, 1) // each
+        spread = (target == lax.broadcasted_iota(jnp.int32, shape, 0)).astype(jnp.bfloat16)
+        plane = lax.broadcasted_iota(jnp.int32, (rows, many), 0) % h
+        mate = lax.broadcasted_iota(jnp.int32, (rows, many), 1) % each
+        return many, spread, mate - plane
+
     dot = functools.partial(jnp.dot, preferred_element_type=jnp.float32)
-    total_sums = None
     for k in range(groups):
         g = lax.rem(mine + groups - k, groups)
+        many, spread, offset = tables(ROWS if k == 0 else h + 2)
         chosen = dot(chooser, chances[g]).astype(jnp.bfloat16)
         laid = dot(chosen, spread)
         blocks = [jnp.zeros((rows, many), jnp.float32)] * len(FLAT)
         for t, move in enumerate(MOVES):
             slot = FLAT.index((move[1], move[2]))
             block = laid[:, t * many : (t + 1) * many]
-            blocks[slot] = jnp.where(mate == plane + 1 + move[0], block, blocks[slot])
+            blocks[slot] = jnp.where(offset == 1 + move[0], block, blocks[slot])
         weights = jnp.concatenate(blocks, axis=0).astype(jnp.bfloat16)
         part = dot(weights, parts_in[k][...])
         if k == 0:
@@ -260,6 +284,12 @@
         value = value + jnp.take_along_axis(cut(4, j), before, axis=1, mode="promise_in_bounds")
         for o in range(owned):
             out_ref[o, :, j * LANES : (j + 1) * LANES] = value[o * h : (o + 1) * h, :]
+
+
+def trim_kernel(h, got_ref, out_ref):
+    count, wide = got_ref.shape[0] // ROWS, got_ref.shape[1]
+    whole = got_ref[...].reshape(count, ROWS, wide)
+    out_ref[...] = whole[:, : h + 2, :].reshape(count * (h + 2), wide)
 
 
 def in_vmem():
@@ -282,15 +312,19 @@
     scale = 3.0 / math.sqrt(edge**3)
     params = pltpu.CompilerParams(vmem_limit_bytes=VMEM_BYTES)
     f32, bf16 = jnp.float32, jnp.bfloat16
+    far = lax.ppermute(references, "dp", [(i, parts - 1 - i) for i in range(parts)])
     sent, both = pl.pallas_call(
         functools.partial(pack_kernel, edge, parts),
         out_shape=(
             jax.ShapeDtypeStruct((parts * ROWS, wide), bf16),
             jax.ShapeDtypeStruct((2 * planes, wide), bf16),
         ),
-        in_specs=[in_vmem()] * 2,
+        in_specs=[pl.BlockSpec(memory_space=pl.ANY)] * 2,
         out_specs=(in_vmem(), in_vmem()),
         scratch_shapes=[
+            pltpu.VMEM((edge, wide), bf16),
+            pltpu.VMEM(references.shape, bf16),
+            pltpu.SemaphoreType.DMA((2,)),
             pltpu.VMEM((edge + 2 * ROWS, wide), f32),
             pltpu.VMEM((parts * ROWS, wide), f32),
             pltpu.VMEM((ROWS, wide), f32),
@@ -298,19 +332,42 @@
             pltpu.VMEM((planes * edge, LANES), f32),
             pltpu.VMEM((planes * edge, LANES), f32),
         ],
-        compiler_params=params,
+        compiler_params=pltpu.CompilerParams(vmem_limit_bytes=MOST_VMEM),
         name="pack",
     )(particles.reshape(edge, wide), references)
-    far = lax.ppermute(both, "dp", [(i, parts - 1 - i) for i in range(parts)])
+    near = pl.pallas_call(
+        functools.partial(near_kernel, h, edge),
+        out_shape=jax.ShapeDtypeStruct((4, ROWS, wide), f32),
+        in_specs=[in_vmem()] * 2,
+        out_specs=in_vmem(),
+        scratch_shapes=[
+            pltpu.VMEM((ROWS, wide), f32),
+            pltpu.VMEM((ROWS, wide), f32),
+            pltpu.VMEM((planes * edge, LANES), f32),
+            pltpu.VMEM((planes * edge, LANES), f32),
+        ],
+        compiler_params=params,
+        cost_estimate=pl.CostEstimate(flops=0, bytes_accessed=16 * 1024 * 1024, transcendentals=0),
+        name="near",
+    )(both, far)
     got = lax.all_to_all(sent, "dp", 0, 0, tiled=True)
+    got, near = lax.optimization_barrier((got, near))
+    trimmed = pl.pallas_call(
+        functools.partial(trim_kernel, h),
+        out_shape=jax.ShapeDtypeStruct((parts * (h + 2), wide), bf16),
+        in_specs=[in_vmem()],
+        out_specs=in_vmem(),
+        compiler_params=params,
+        name="trim",
+    )(got)
     others = [
-        lax.ppermute(got, "ref", [(i, (i + k) % groups) for i in range(groups)]) for k in range(1, groups)
+        lax.ppermute(trimmed, "ref", [(i, (i + k) % groups) for i in range(groups)]) for k in range(1, groups)
     ]
     rows = total * h
     partial = pl.pallas_call(
         functools.partial(logits_kernel, edge, parts, total, devices, scale),
         out_shape=jax.ShapeDtypeStruct((devices * total, SLOTS * parts), f32),
-        in_specs=[in_smem(), in_smem(), in_vmem(), in_vmem(), in_vmem()],
+        in_specs=[in_smem(), in_smem(), in_vmem(), in_vmem()],
         out_specs=in_vmem(),
         scratch_shapes=[
             pltpu.VMEM((wide // LANES, parts * ROWS, LANES), f32),
@@ -322,7 +379,7 @@
         ],
         compiler_params=params,
         name="logits",
-    )(orient, allowed, got, both, far)
+    )(orient, allowed, got, near)
     logits = lax.all_to_all(partial, ("ref", "dp"), 0, 0, tiled=True)
     owned = total // groups
     sums, log_evidence = pl.pallas_call(

time: 69 us -> 65.5 us (0.949)
  the two profiles are of different devices: /device:TPU:0 before, /device:TPU:10 now
where the time goes in v2:
time: 65.5 us; the launch traced here: 65.3 us
  waiting for transfers between devices  26.3 us (40%)
  blocking collectives  16.2 us (25%)
  Pallas kernels  12.8 us (20%)
  starting transfers between devices  9.22 us (14%)
  between operations  0.71 us (1%)
    ppermute x1, waiting for transfers between devices, per_device(): lax.ppermute(references, 'dp', [(i, parts - 1 - i) for i in range(parts)])  26.2 us
    all_to_all x1, blocking collectives, per_device(): logits = lax.all_to_all(partial, ('ref', 'dp'), 0, 0, tiled=True)  16.2 us
    all_to_all x1, starting transfers between devices, per_device(): got = lax.all_to_all(sent, 'dp', 0, 0, tiled=True)  6.44 us
    pallas_call x1, Pallas kernels, per_device(): pl.pallas_call(functools.partial(logits_kernel, edge, parts, total, devic...  5.72 us
    pallas_call x1, Pallas kernels, per_device(): pl.pallas_call(functools.partial(sums_kernel, edge, parts, total, groups)...  3.33 us
    pallas_call x1, Pallas kernels, per_device(): pl.pallas_call(functools.partial(pack_kernel, edge, parts), out_shape=(ja...  3.08 us
    ppermute x1, starting transfers between devices, per_device(): lax.ppermute(references, 'dp', [(i, parts - 1 - i) for i in range(parts)])  2.18 us
  transfers between devices with their start and end apart: 3, of which 1 were waited for; matrix products, arithmetic and copies ran while one was open for 0% of the time, Pallas kernels for 10%

profile of v2, /device:TPU:10, one launch (start us, length us, event | category | flops | bytes accessed | tf_op | source)
XLA Modules:
  0.0 65.3 jit_solution(1541970835484036563)
XLA Ops:
  0.6 3.1 %pack.1 = (bf16[128,4096]{1,0:T(8,128)(2,1)}, bf16[16,4096]{1,0:T(8,128)(2,1)}) custom-call(bf16[64,4096]{1,0:T(8,128)(2,1)} %bitcast.12, bf16[2,4,4096]{2,1,0:T(4,128)(2,1)} %refs_hbm.1), custom_call_target="tpu_custom_call" | custom-call | tf_op jit(solution)/shard_map/pack/pallas_call | solution.py:316
  3.7 0.0 copy-start.2
  3.7 0.0 copy-start
  3.7 6.4 %all-to-all-start = ((bf16[16,8,4096]{2,1,0:T(8,128)(2,1)}), bf16[16,8,4096]{2,1,0:T(8,128)(2,1)S(1)}, u32[]{:S(2)}, u32[]{:S(2)}) async-start(bf16[16,8,4096]{2,1,0:T(8,128)(2,1)} %bitcast.11), calls=%async_computation | async-start | bytes 2097152 | tf_op jit(solution)/shard_map/all_to_all | solution.py:353
  10.2 0.0 copy-done.2
  10.2 2.2 %collective-permute-start = (bf16[2,4,4096]{2,1,0:T(4,128)(2,1)S(1)}, bf16[2,4,4096]{2,1,0:T(4,128)(2,1)S(1)}, u32[]{:S(2)}, u32[]{:S(2)}) collective-permute-start(bf16[2,4,4096]{2,1,0:T(4,128)(2,1)S(1)} %copy-done.2), channel_id=1, source_target_pairs={{0,15},{1,14},{2,13},{3,12},{4,11},{5,10},{6,9},{7,8},{8,7},{9,6},... | collective-permute-start | bytes 196616 | tf_op jit(solution)/shard_map/ppermute | solution.py:315
  12.4 26.2 %collective-permute-done.far_ref = bf16[2,4,4096]{2,1,0:T(4,128)(2,1)S(1)} collective-permute-done((bf16[2,4,4096]{2,1,0:T(4,128)(2,1)S(1)}, bf16[2,4,4096]{2,1,0:T(4,128)(2,1)S(1)}, u32[]{:S(2)}, u32[]{:S(2)}) %collective-permute-start) | collective-permute-done | bytes 65568 | tf_op jit(solution)/shard_map/ppermute | solution.py:315
  38.6 0.0 copy-done
  38.6 0.5 near.1.near_ref
  39.1 0.0 all-to-all-done
  39.2 0.0 copy-start.3
  39.2 0.2 trim.1
  39.3 0.0 copy-start.1
  39.4 0.6 collective-permute-start.1
  40.0 0.0 copy-done.3
  40.0 0.1 copy.6.orient_ref
  40.0 0.0 copy-done.1
  40.0 5.7 %logits.1 = f32[512,128]{1,0:T(8,128)S(1)} custom-call(s32[16,6]{1,0:T(8,128)S(1)} %copy.6.orient_ref, s32[1,2]{1,0:T(1,128)S(1)} %copy-done.1, bf16[128,4096]{1,0:T(8,128)(2,1)S(1)} %bitcast.7, f32[4,8,4096]{2,1,0:T(8,128)S(1)} %near.1.near_ref), custom_call_target="tpu_custom_call" | custom-call | tf_op jit(solution)/shard_map/logits/pallas_call | solution.py:367
  45.8 16.2 %all_to_all.23 = f32[32,16,128]{2,1,0:T(8,128)S(1)} all-to-all(f32[32,16,128]{2,1,0:T(8,128)S(1)} %bitcast.9), channel_id=1, replica_groups=mesh['ref'=2,'dp'=16] {'ref','dp'}, dimensions={0} | all-to-all | bytes 524288 | tf_op jit(solution)/shard_map/all_to_all | solution.py:383
  62.0 0.0 collective-permute-done.1.refs_2_
  62.0 3.3 %sums.1 = (f32[8,4,4096]{2,1,0:T(4,128)}, f32[1,1]{1,0:T(1,128)}) custom-call(f32[512,128]{1,0:T(8,128)S(1)} %bitcast.10, bf16[128,4096]{1,0:T(8,128)(2,1)S(1)} %bitcast.8, bf16[96,4096]{1,0:T(8,128)(2,1)S(1)} %collective-permute-done.1.refs_2_), custom_call_target="tpu_custom_call" | custom-call | tf_op jit(solution)/shard_map/sums/pallas_call | solution.py:385
Async XLA Ops:
  3.7 6.5 %copy-start.2 = (bf16[2,4,4096]{2,1,0:T(4,128)(2,1)S(1)}, bf16[2,4,4096]{2,1,0:T(4,128)(2,1)}, u32[]{:S(2)}) copy-start(bf16[2,4,4096]{2,1,0:T(4,128)(2,1)} %refs_hbm.1) | copy-start | bytes 196612
  3.7 34.9 %copy-start = (bf16[16,4096]{1,0:T(8,128)(2,1)S(1)}, bf16[16,4096]{1,0:T(8,128)(2,1)}, u32[]{:S(2)}) copy-start(bf16[16,4096]{1,0:T(8,128)(2,1)} %get-tuple-element.9.own_ref) | copy-start | bytes 393220
  3.7 35.4 %all-to-all-start = ((bf16[16,8,4096]{2,1,0:T(8,128)(2,1)}), bf16[16,8,4096]{2,1,0:T(8,128)(2,1)S(1)}, u32[]{:S(2)}, u32[]{:S(2)}) async-start(bf16[16,8,4096]{2,1,0:T(8,128)(2,1)} %bitcast.11), calls=%async_computation | async-start | bytes 2097152 | tf_op jit(solution)/shard_map/all_to_all | solution.py:353
  10.2 28.4 %collective-permute-start = (bf16[2,4,4096]{2,1,0:T(4,128)(2,1)S(1)}, bf16[2,4,4096]{2,1,0:T(4,128)(2,1)S(1)}, u32[]{:S(2)}, u32[]{:S(2)}) collective-permute-start(bf16[2,4,4096]{2,1,0:T(4,128)(2,1)S(1)} %copy-done.2), channel_id=1, source_target_pairs={{0,15},{1,14},{2,13},{3,12},{4,11},{5,10},{6,9},{7,8},{8,7},{9,6},... | collective-permute-start | bytes 196616 | tf_op jit(solution)/shard_map/ppermute | solution.py:315
  39.2 0.8 %copy-start.3 = (s32[16,6]{0,1:T(8,128)S(1)}, s32[16,6]{0,1:T(8,128)}, u32[]{:S(2)}) copy-start(s32[16,6]{0,1:T(8,128)} %param.6) | copy-start | bytes 1156
  39.3 0.7 %copy-start.1 = (s32[1,2]{1,0:T(1,128)S(1)}, s32[1,2]{1,0:T(1,128)}, u32[]{:S(2)}) copy-start(s32[1,2]{1,0:T(1,128)} %allowed_ref.1) | copy-start | bytes 28
  39.4 22.6 %collective-permute-start.1 = (bf16[96,4096]{1,0:T(8,128)(2,1)S(1)}, bf16[96,4096]{1,0:T(8,128)(2,1)S(1)}, u32[]{:S(2)}, u32[]{:S(2)}) collective-permute-start(bf16[96,4096]{1,0:T(8,128)(2,1)S(1)} %trim.1), channel_id=1, source_target_pairs={{0,16},{16,0},{1,17},{17,1},{2,18},{18,2},{3,19},{19,3},{4,20},{20... | collective-permute-start | bytes 2359304 | tf_op jit(solution)/shard_map/ppermute | solution.py:364

commit v3 on v2

v3 whole, which is shorter than its diff:
```python
import functools
import math

import jax
import jax.numpy as jnp
from jax import lax
from jax.experimental import pallas as pl
from jax.experimental.pallas import tpu as pltpu
from jax.sharding import PartitionSpec as P

ORI = 8
LANES = 128
ROWS = 8
MOVES = [(0, 0, 0), (1, 0, 0), (-1, 0, 0), (0, 1, 0), (0, -1, 0), (0, 0, 1), (0, 0, -1)]
FLAT = [(0, 0), (1, 0), (-1, 0), (0, 1), (0, -1)]
SLOTS = 8
BARRED = -1e30
VMEM_BYTES = 24 * 1024 * 1024
MOST_VMEM = 62 * 1024 * 1024


def lane_iota(shape):
    return lax.broadcasted_iota(jnp.int32, shape, len(shape) - 1)


def row_iota(shape):
    return lax.broadcasted_iota(jnp.int32, shape, 0)


def swap_halves(x):
    return pltpu.roll(x, LANES // 2, 1)


def pick_lanes(x, index):
    return jnp.take_along_axis(x, index, axis=1, mode="promise_in_bounds")


def tile(m):
    return slice(m * LANES, (m + 1) * LANES)


def outer_inner(h, me):
    outer = (me % 2) * (h + 1)
    return outer, h + 1 - outer


def turn_rows(edge, planes, x, z, flat, turned):
    low = lane_iota((planes, LANES)) < edge
    for m in range(edge // 2):
        piece = x[:planes, tile(m)]
        flat[pl.ds(2 * m, planes, stride=edge), :] = piece
        flat[pl.ds(2 * m + 1, planes, stride=edge), :] = swap_halves(piece)
    for n in range(0, planes, 2):
        block = flat[n * edge : (n + 2) * edge, :].T[:edge, :]
        turned[n * edge : (n + 1) * edge, :] = block
        turned[(n + 1) * edge : (n + 2) * edge, :] = swap_halves(block)
    for m in range(edge // 2):
        even = turned[pl.ds(2 * m, planes, stride=edge), :]
        odd = turned[pl.ds(2 * m + 1, planes, stride=edge), :]
        z[:planes, tile(m)] = jnp.where(low, even, swap_halves(odd))


def pack_kernel(
    edge, parts, part_hbm, refs_hbm, out_ref, both_ref, part_ref, refs_ref, sems, ring, stage, x, z, flat, turned
):
    h = edge // parts
    planes = 2 * h
    wide = edge * edge
    spare = ROWS - h - 2
    span = 4 * h * edge
    chunk = 2 * ROWS
    refs_copy = pltpu.make_async_copy(refs_hbm, refs_ref, sems.at[0])
    refs_copy.start()
    copies = []
    for i in range(edge // chunk):
        rows = pl.ds(i * chunk, chunk)
        copies.append(pltpu.make_async_copy(part_hbm.at[rows], part_ref.at[rows], sems.at[1 + i]))
        copies[-1].start()
    refs_copy.wait()
    for c in range(2):
        x[c * h : (c + 1) * h, :] = refs_ref[c].astype(jnp.float32)
    turn_rows(edge, planes, x, z, flat, turned)
    both_ref[...] = jnp.concatenate([x[:planes, :], z[:planes, :]], axis=0).astype(jnp.bfloat16)
    if planes // spare * span < wide:
        stage[...] = jnp.zeros_like(stage)
    slab = h * edge
    for s in range(parts):
        top = s * ROWS
        mirror = parts - 1 - s
        for q in range(planes // spare):
            rows = slice(q * spare, (q + 1) * spare)
            for number, (array, place) in enumerate(((x, s), (x, mirror), (z, s), (z, mirror))):
                left = q * span + number * slab
                stage[top + h + 2 : top + ROWS, left : left + slab] = array[rows, place * slab : (place + 1) * slab]
    last = len(copies) - 1
    done = 0
    for i in [last] + list(range(last)):
        copies[i].wait()
        rows = slice(i * chunk, (i + 1) * chunk)
        ring[ROWS + i * chunk : ROWS + (i + 1) * chunk, :] = part_ref[rows, :].astype(jnp.float32)
        if i == last:
            ring[ROWS - 1 : ROWS, :] = ring[ROWS + edge - 1 : ROWS + edge, :]
        if i == 0:
            ring[ROWS + edge : ROWS + edge + 1, :] = ring[ROWS : ROWS + 1, :]
        ready = 0 if i == last else (parts if i == last - 1 else ((i + 1) * chunk - 1) // h)
        while done + 2 <= ready:
            for s in (done, done + 1):
                top, first = s * ROWS, ROWS + h * s
                stage[top : top + h, :] = ring[first : first + h, :]
                ends = (first - 1, first + h) if s % 2 == 0 else (first + h, first - 1)
                for number, end in enumerate(ends):
                    stage[top + h + number : top + h + number + 1, :] = ring[end : end + 1, :]
            both = slice(done * ROWS, (done + 2) * ROWS)
            out_ref[both, :] = stage[both, :].astype(jnp.bfloat16)
            done += 2


def near_kernel(edge, h, own_ref, far_ref, out_ref, x, z, flat, turned):
    planes = 2 * h
    columns = edge * edge // LANES
    own = own_ref[...].astype(jnp.float32)
    for c in range(2):
        far = far_ref[c].astype(jnp.float32)
        for l in range(h):
            x[c * h + l : c * h + l + 1, :] = far[h - 1 - l : h - l, :]
    turn_rows(edge, planes, x, z, flat, turned)
    for turn in range(2):
        far = (x, z)[turn]
        for c in range(2):
            for copy in range(ROWS // h):
                rows = slice(copy * h, (copy + 1) * h)
                top = turn * planes + c * h
                for m in range(columns):
                    out_ref[(turn * 4 + c) * columns + m, rows, :] = own[top : top + h, tile(m)]
                    out_ref[(turn * 4 + 2 + c) * columns + m, rows, :] = far[c * h : (c + 1) * h, tile(m)]


def logits_kernel(
    edge, parts, total, devices, scale,
    orient_ref, allowed_ref, got_ref, near_ref, out_ref,
    wide_f32, flat, turned, kinds, shifted, gram,
):
    h = edge // parts
    planes = 2 * h
    wide = edge * edge
    columns = wide // LANES
    spare = ROWS - h - 2
    span = 4 * h * edge
    rows = total * h
    me = lax.axis_index("dp")
    low = lane_iota((ROWS, LANES)) < edge
    for j in range(columns):
        wide_f32[j] = got_ref[:, tile(j)].astype(jnp.float32)
    kinds[: 8 * columns] = near_ref[...]

    def keep(first, second, value, m):
        if planes == ROWS:
            upper = row_iota((ROWS, LANES)) < h
            other = pltpu.roll(value, h, 0)
            kinds[first * columns + m] = jnp.where(upper, value, other)
            kinds[second * columns + m] = jnp.where(upper, other, value)
        else:
            for number, kind in enumerate((first, second)):
                for copy in range(ROWS // h):
                    kinds[kind * columns + m, copy * h : (copy + 1) * h, :] = value[number * h : (number + 1) * h, :]

    for axis in (1, 2):
        for c in range(2):
            for jl in range(h):
                q, e = divmod(c * h + jl, spare)
                first = (q * span + (axis - 1) * 2 * h * edge) // LANES
                for s in range(0, parts, ROWS):
                    tiles = [
                        wide_f32[first + i, pl.ds(s * ROWS + h + 2 + e, ROWS, stride=ROWS), :] for i in range(h)
                    ]
                    for l in range(h):
                        plain, mirrored = tiles[l // 2], tiles[h // 2 + (h - 1 - l) // 2]
                        if l % 2 == 0:
                            value = jnp.where(low, plain, mirrored)
                        else:
                            value = swap_halves(jnp.where(low, mirrored, plain))
                        flat[pl.ds((c * h + l) * edge + s * h + jl, ROWS, stride=h), :] = value
        for l in range(h):
            block = jnp.concatenate(
                [flat[(c * h + l) * edge : (c * h + l + 1) * edge, :] for c in range(2)], axis=0
            ).T
            for side in range(2):
                turned[(side * h + l) * edge : (side * h + l + 1) * edge, :] = block[side * edge : (side + 1) * edge, :]
        part = lane_iota((planes, LANES)) < edge
        for m in range(edge // 2):
            even = flat[pl.ds(2 * m, planes, stride=edge), :]
            odd = flat[pl.ds(2 * m + 1, planes, stride=edge), :]
            keep(axis * 8, axis * 8 + 1, jnp.where(part, even, swap_halves(odd)), m)
            keep(axis * 8 + 2, axis * 8 + 3, jnp.where(part, swap_halves(even), odd), m)
            even = turned[pl.ds(2 * m, planes, stride=edge), :]
            odd = turned[pl.ds(2 * m + 1, planes, stride=edge), :]
            keep(axis * 8 + 4, axis * 8 + 6, jnp.where(part, even, swap_halves(odd)), m)
            keep(axis * 8 + 5, axis * 8 + 7, jnp.where(part, swap_halves(even), odd), m)

    lane = lane_iota((ROWS, LANES))
    slot = row_iota((ROWS, LANES)) // h
    per = ROWS // h
    lows = lane < edge
    after = (lane // edge) * edge + (lane + 1) % edge
    before = (lane // edge) * edge + (lane + edge - 1) % edge
    start, step, index = [], [], []
    for b in range(total // per):
        xor = jnp.zeros((ROWS, LANES), jnp.int32)
        for i in range(per):
            o = b * per + i
            turn = (orient_ref[o, 1] > orient_ref[o, 2]).astype(jnp.int32)
            kind = orient_ref[o, 0] * 8 + turn * 4 + orient_ref[o, 3] * 2 + o // ORI
            start.append(kind * columns + orient_ref[o, 4] * (columns - 1))
            step.append(1 - 2 * orient_ref[o, 4])
            xor = jnp.where(slot == i, orient_ref[o, 4] * edge + orient_ref[o, 5] * (edge - 1), xor)
        index.append([lane ^ xor, (lane ^ edge) ^ xor, before ^ xor, after ^ xor])

    def column(j):
        found = []
        for b in range(total // per):
            value = kinds[start[b * per] + j * step[b * per]]
            for i in range(1, per):
                value = jnp.where(slot == i, kinds[start[b * per + i] + j * step[b * per + i]], value)
            found.append([pick_lanes(value, way) for way in index[b]])
        return [list(way) for way in zip(*found, strict=True)]

    behind = column(columns - 1)[1]
    here = column(0)
    for j in range(columns):
        ahead = column((j + 1) % columns)
        results = [
            here[0],
            [jnp.where(lows, x, y) for x, y in zip(behind, here[1], strict=True)],
            [jnp.where(lows, x, y) for x, y in zip(here[1], ahead[1], strict=True)],
            here[2],
            here[3],
        ]
        for number, result in enumerate(results):
            shifted[number * rows : (number + 1) * rows, tile(j)] = jnp.concatenate(result, axis=0).astype(jnp.bfloat16)
        behind, here = here[1], ahead
    gram[...] = lax.dot_general(
        shifted[...], got_ref[...], (((1,), (1,)), ((), ())), preferred_element_type=jnp.float32
    )
    many = parts * ROWS
    place = lane_iota((total, many)) % ROWS
    outer, inner = outer_inner(h, me)
    mate = jnp.where(place < h, place + 1, jnp.where(place == h, outer, jnp.where(place == h + 1, inner, -h)))
    kept = []
    for t, move in enumerate(MOVES):
        source = FLAT.index((move[1], move[2]))
        total_t = None
        for l in range(h):
            if many == LANES:
                block = gram[pl.ds(source * rows + l, total, stride=h), :]
            else:
                block = jnp.concatenate(
                    [gram[source * rows + o * h + l : source * rows + o * h + l + 1, :] for o in range(total)], axis=0
                )
            block = jnp.where(mate == l + 1 + move[0], block, 0.0)
            total_t = block if total_t is None else total_t + block
        kept.append(total_t)
    if many == LANES:
        lane = lane_iota((total, LANES))
        result = jnp.zeros((total, LANES), jnp.float32)
        for t in range(len(MOVES)):
            value = kept[t]
            for step in (1, 2, 4):
                value = value + pltpu.roll(value, LANES - step, 1)
            result = jnp.where(lane // parts == t, pick_lanes(value, (lane % parts) * ROWS), result)
    else:
        shape = (len(MOVES) * many, SLOTS * parts)
        picker = (row_iota(shape) // ROWS == lane_iota(shape)).astype(jnp.float32)
        result = jnp.dot(
            jnp.concatenate(kept, axis=1), picker,
            preferred_element_type=jnp.float32, precision=lax.Precision.HIGHEST,
        )
    result = result * scale
    kin = row_iota(result.shape) // ORI
    permit = jnp.zeros(result.shape, jnp.int32)
    for c in range(total // ORI):
        permit = jnp.where(kin == c, allowed_ref[0, c], permit)
    barred = (lane_iota(result.shape) % parts == me) & (permit != 1)
    result = result + jnp.where(barred, jnp.float32(BARRED), jnp.float32(0.0))
    for d in range(devices):
        out_ref[d * total : (d + 1) * total, :] = result


def trim_kernel(h, got_ref, core_ref, outer_ref):
    count, wide = got_ref.shape[0] // ROWS, got_ref.shape[1]
    whole = got_ref[...].reshape(count, ROWS, wide)
    core_ref[...] = whole[:, :h, :].reshape(count * h, wide)
    outer_ref[...] = whole[:, h, :]


def edge_kernel(h, core_ref, out_ref, *tables):
    parts = core_ref.shape[0] // h
    whole = core_ref[...].reshape(parts, h, core_ref.shape[1])
    even = lax.axis_index("dp") % 2 == 0

    @pl.when(even)
    def _():
        out_ref[...] = whole[:, h - 1, :]

    @pl.when(jnp.logical_not(even))
    def _():
        out_ref[...] = whole[:, 0, :]

    for table, own in zip(tables, (True, False)):
        table[...] = spread_table(h, parts, own)


def far_columns(h, parts):
    return -(-parts * (h + 2) // LANES) * LANES


def spread_table(h, parts, own):
    many = parts * ROWS if own else far_columns(h, parts)
    shape = (SLOTS * parts, len(MOVES) * many)
    column = lane_iota(shape) % many
    if own:
        particle = column // ROWS
    else:
        particle = jnp.where(column < parts * h, column // h, column % parts)
    return ((lane_iota(shape) // many) * parts + particle == row_iota(shape)).astype(jnp.bfloat16)


def mate_row(h, parts, own, me):
    outer, inner = outer_inner(h, me)
    if own:
        place = lane_iota((ROWS, parts * ROWS)) % ROWS
        return jnp.where(place < h, place + 1, jnp.where(place == h, outer, jnp.where(place == h + 1, inner, -h)))
    column = lane_iota((ROWS, far_columns(h, parts)))
    mate = jnp.where(column < parts * h, column % h + 1, jnp.where(column < parts * (h + 1), outer, inner))
    return jnp.where(column < parts * (h + 2), mate, -h)


def sums_kernel(edge, parts, total, groups, logits_ref, own_table, far_table, got_ref, *refs):
    pieces, refs = refs[: 3 * (groups - 1)], refs[3 * (groups - 1) :]
    out_hbm, log_ref, out_ref, sems, in_sems, chances, weights, table, merged = refs
    h = edge // parts
    wide = edge * edge
    columns = wide // LANES
    owned = total // groups
    rows = owned * h
    span = SLOTS * parts
    mine, me = lax.axis_index("ref"), lax.axis_index("dp")
    incoming = []
    for number, piece in enumerate(pieces):
        if number % 3 == 0:
            top = got_ref.shape[0] + number // 3 * far_columns(h, parts)
        rows_here = pl.ds(top, piece.shape[0])
        incoming.append(pltpu.make_async_copy(piece, merged.at[rows_here], in_sems.at[number]))
        top += piece.shape[0]
        rest = far_columns(h, parts) - parts * (h + 2)
        if number % 3 == 2 and rest:
            merged[top : top + rest, :] = jnp.zeros((rest, wide), merged.dtype)
    for copy in incoming:
        copy.start()
    merged[: got_ref.shape[0], :] = got_ref[...]
    dot = functools.partial(jnp.dot, preferred_element_type=jnp.float32)
    lane = lane_iota((total, span))
    log_evidence = jnp.zeros((1, span), jnp.float32)
    for g in range(groups):
        scores = [logits_ref[(g * parts + s) * total : (g * parts + s + 1) * total, :] for s in range(parts)]
        while len(scores) > 1:
            scores = [sum(scores[i : i + 2]) for i in range(0, len(scores), 2)]
        score = jnp.where(lane >= len(MOVES) * parts, jnp.float32(-3e38), scores[0])
        peak = jnp.max(score, axis=0, keepdims=True)
        for step in (1, 2, 4):
            peak = jnp.maximum(peak, pltpu.roll(peak, step * parts, 1))
        expo = jnp.exp(score - peak)
        mass = jnp.sum(expo, axis=0, keepdims=True)
        for step in (1, 2, 4):
            mass = mass + pltpu.roll(mass, step * parts, 1)
        chances[g] = expo / mass
        log_evidence = jnp.where(mine == g, peak + jnp.log(mass), log_evidence)
    log_ref[...] = jnp.sum(jnp.where(lane_iota((1, span)) == me, log_evidence, 0.0), axis=1, keepdims=True)
    left = 0
    for k in range(groups):
        g = lax.rem(mine + groups - k, groups)
        if owned % ROWS == 0:
            chosen = chances[g, pl.ds(pl.multiple_of(mine * owned, ROWS), owned), :].astype(jnp.bfloat16)
        else:
            at = mine * owned + row_iota((owned, total))
            chooser = (at == lane_iota((owned, total))).astype(jnp.bfloat16)
            chosen = dot(chooser, chances[g].astype(jnp.bfloat16)).astype(jnp.bfloat16)
        laid = dot(chosen, (own_table if k == 0 else far_table)[...])
        mate = mate_row(h, parts, k == 0, me)[:owned]
        many = mate.shape[1]
        for slot in range(len(FLAT)):
            for l in range(h):
                value = jnp.zeros((owned, many), jnp.float32)
                for t, move in enumerate(MOVES):
                    if FLAT.index((move[1], move[2])) == slot:
                        value = jnp.where(mate == l + 1 + move[0], laid[:, t * many : (t + 1) * many], value)
                for m in range(many // LANES):
                    weights[left // LANES + m, pl.ds(slot * rows + l, owned, stride=h), :] = value[:, tile(m)]
        left += many
    both = jnp.concatenate([weights[m] for m in range(left // LANES)], axis=1).astype(jnp.bfloat16)
    for copy in incoming:
        copy.wait()
    table[...] = dot(both, merged[...])
    lane = lane_iota((rows, LANES))
    low = lane < edge
    after = (lane // edge) * edge + (lane + 1) % edge
    before = (lane // edge) * edge + (lane + edge - 1) % edge

    def cut(slot, j):
        return table[slot * rows : (slot + 1) * rows, tile(j % columns)]

    pieces = sems.shape[0]
    copies = []
    up = swap_halves(cut(1, 0))
    down = swap_halves(cut(2, columns - 1))
    for j in range(columns):
        up_next, down_next = swap_halves(cut(1, j + 1)), swap_halves(cut(2, j))
        value = cut(0, j) + jnp.where(low, up, up_next) + jnp.where(low, down, down_next)
        value = value + pick_lanes(cut(3, j), after) + pick_lanes(cut(4, j), before)
        up, down = up_next, down_next
        for o in range(owned):
            out_ref[o, :, tile(j)] = value[o * h : (o + 1) * h, :]
        if (j + 1) % (columns // pieces) == 0:
            number = len(copies)
            part = pl.ds(number * (wide // pieces), wide // pieces)
            copies.append(
                pltpu.make_async_copy(out_ref.at[:, :, part], out_hbm.at[:, :, part], sems.at[number])
            )
            copies[-1].start()
    for copy in copies:
        copy.wait()


def in_vmem():
    return pl.BlockSpec(memory_space=pltpu.VMEM)


def in_smem():
    return pl.BlockSpec(memory_space=pltpu.SMEM)


def anywhere():
    return pl.BlockSpec(memory_space=pl.ANY)


def per_device(particles, references, orient, allowed):
    edge = particles.shape[1]
    wide = edge * edge
    total = orient.shape[0]
    parts = lax.axis_size("dp")
    groups = lax.axis_size("ref")
    devices = parts * groups
    h = edge // parts
    planes = 2 * h
    rows = total * h
    owned = total // groups
    scale = 3.0 / math.sqrt(edge**3)
    params = pltpu.CompilerParams(vmem_limit_bytes=VMEM_BYTES)
    f32, bf16 = jnp.float32, jnp.bfloat16
    array = jax.ShapeDtypeStruct
    turning = [
        pltpu.VMEM((ROWS, wide), f32),
        pltpu.VMEM((ROWS, wide), f32),
        pltpu.VMEM((planes * edge, LANES), f32),
        pltpu.VMEM((planes * edge, LANES), f32),
    ]
    far = lax.ppermute(references, "dp", [(i, parts - 1 - i) for i in range(parts)])
    sent, both = pl.pallas_call(
        functools.partial(pack_kernel, edge, parts),
        out_shape=(array((parts * ROWS, wide), bf16), array((2 * planes, wide), bf16)),
        in_specs=[anywhere()] * 2,
        out_specs=(in_vmem(), in_vmem()),
        scratch_shapes=[
            pltpu.VMEM((edge, wide), bf16),
            pltpu.VMEM(references.shape, bf16),
            pltpu.SemaphoreType.DMA((1 + edge // (2 * ROWS),)),
            pltpu.VMEM((edge + 2 * ROWS, wide), f32),
            pltpu.VMEM((parts * ROWS, wide), f32),
            *turning,
        ],
        compiler_params=pltpu.CompilerParams(vmem_limit_bytes=MOST_VMEM),
        name="pack",
    )(particles.reshape(edge, wide), references)
    near = pl.pallas_call(
        functools.partial(near_kernel, edge, h),
        out_shape=array((8 * wide // LANES, ROWS, LANES), f32),
        in_specs=[in_vmem()] * 2,
        out_specs=in_vmem(),
        scratch_shapes=turning,
        compiler_params=params,
        cost_estimate=pl.CostEstimate(flops=0, bytes_accessed=16 * 1024 * 1024, transcendentals=0),
        name="near",
    )(both, far)
    got = lax.all_to_all(sent, "dp", 0, 0, tiled=True)
    got, near = lax.optimization_barrier((got, near))
    core, outer = pl.pallas_call(
        functools.partial(trim_kernel, h),
        out_shape=(array((parts * h, wide), bf16), array((parts, wide), bf16)),
        in_specs=[in_vmem()],
        out_specs=(in_vmem(), in_vmem()),
        compiler_params=params,
        name="trim",
    )(got)
    steps = [[(i, (i + k) % groups) for i in range(groups)] for k in range(1, groups)]
    cores = [lax.ppermute(core, "ref", step) for step in steps]
    partial = pl.pallas_call(
        functools.partial(logits_kernel, edge, parts, total, devices, scale),
        out_shape=array((devices * total, SLOTS * parts), f32),
        in_specs=[in_smem(), in_smem(), in_vmem(), in_vmem()],
        out_specs=in_vmem(),
        scratch_shapes=[
            pltpu.VMEM((wide // LANES, parts * ROWS, LANES), f32),
            pltpu.VMEM((planes * edge, LANES), f32),
            pltpu.VMEM((planes * edge, LANES), f32),
            pltpu.VMEM((24 * wide // LANES, ROWS, LANES), f32),
            pltpu.VMEM((len(FLAT) * rows, wide), bf16),
            pltpu.VMEM((len(FLAT) * rows, parts * ROWS), f32),
        ],
        compiler_params=params,
        name="logits",
    )(orient, allowed, got, near)
    partial, outer = lax.optimization_barrier((partial, outer))
    logits = lax.all_to_all(partial, ("ref", "dp"), 0, 0, tiled=True)
    span = SLOTS * parts
    tables = [array((span, len(MOVES) * n), bf16) for n in (parts * ROWS, far_columns(h, parts))]
    pieces = []
    for core, step in zip(cores, steps, strict=True):
        lacking, *laid = pl.pallas_call(
            functools.partial(edge_kernel, h),
            out_shape=(array((parts, wide), bf16), *tables),
            in_specs=[in_vmem()],
            out_specs=(in_vmem(),) * (1 + len(tables)),
            compiler_params=params,
            cost_estimate=pl.CostEstimate(flops=0, bytes_accessed=16 * 1024 * 1024, transcendentals=0),
            name="edges",
        )(core)
        if not pieces:
            spreads = laid
        pieces += [
            core,
            lax.ppermute(outer, "ref", step),
            lax.ppermute(lacking, "dp", [(i, i ^ 1) for i in range(parts)]),
        ]
        tables = []
    merged_rows = got.shape[0] + (groups - 1) * far_columns(h, parts)
    sums, log_evidence = pl.pallas_call(
        functools.partial(sums_kernel, edge, parts, total, groups),
        out_shape=(array((owned, h, wide), f32), array((1, 1), f32)),
        in_specs=[in_vmem()] * 4 + [anywhere()] * len(pieces),
        out_specs=(anywhere(), in_vmem()),
        scratch_shapes=[
            pltpu.VMEM((owned, h, wide), f32),
            pltpu.SemaphoreType.DMA((4,)),
            pltpu.SemaphoreType.DMA((len(pieces),)),
            pltpu.VMEM((groups, total, span), f32),
            pltpu.VMEM((merged_rows // LANES, len(FLAT) * owned * h, LANES), f32),
            pltpu.VMEM((len(FLAT) * owned * h, wide), f32),
            pltpu.VMEM((merged_rows, wide), bf16),
        ],
        compiler_params=params,
        name="sums",
    )(logits, *spreads, got, *pieces)
    return (sums, log_evidence.reshape(1))


def solution(mesh):
    return jax.shard_map(
        per_device,
        mesh=mesh,
        in_specs=(P(("ref", "dp"), None, None), P(None, "dp", None), P(), P(("ref", "dp"), None)),
        out_specs=(P("ref", "dp", None), P(("ref", "dp"))),
        check_vma=False,
    )
```

time: 65.5 us -> 63.4 us (0.968)
  the two profiles are of different devices: /device:TPU:10 before, /device:TPU:0 now
where the time goes in v3:
time: 63.4 us; the launch traced here: 63.1 us
  waiting for transfers between devices  27.4 us (43%)
  starting transfers between devices  22.3 us (35%)
  Pallas kernels  12.6 us (20%)
  between operations  0.74 us (1%)
    ppermute x1, waiting for transfers between devices, per_device(): lax.ppermute(references, 'dp', [(i, parts - 1 - i) for i in range(parts)])  19.4 us
    all_to_all x1, starting transfers between devices, per_device(): got = lax.all_to_all(sent, 'dp', 0, 0, tiled=True)  7.53 us
    all_to_all x1, starting transfers between devices, per_device(): logits = lax.all_to_all(partial, ('ref', 'dp'), 0, 0, tiled=True)  6.86 us
    ppermute x1, waiting for transfers between devices, per_device(): lax.ppermute(outer, 'ref', step)  5.53 us
    pallas_call x1, Pallas kernels, per_device(): pl.pallas_call(functools.partial(logits_kernel, edge, parts, total, devic...  5.1 us
    ppermute x1, starting transfers between devices, per_device(): lax.ppermute(references, 'dp', [(i, parts - 1 - i) for i in range(parts)])  4.44 us
    pallas_call x1, Pallas kernels, per_device(): pl.pallas_call(functools.partial(sums_kernel, edge, parts, total, groups)...  3.24 us
    pallas_call x1, Pallas kernels, per_device(): pl.pallas_call(functools.partial(pack_kernel, edge, parts), out_shape=(ar...  3.03 us
  transfers between devices with their start and end apart: 6, of which 3 were waited for; matrix products, arithmetic and copies ran while one was open for 0% of the time, Pallas kernels for 10%

profile of v3, /device:TPU:0, one launch (start us, length us, event | category | flops | bytes accessed | tf_op | source)
XLA Modules:
  0.0 63.1 jit_solution(11760378589379155021)
XLA Ops:
  0.6 3.0 %pack.1 = (bf16[128,4096]{1,0:T(8,128)(2,1)}, bf16[16,4096]{1,0:T(8,128)(2,1)}) custom-call(bf16[64,4096]{1,0:T(8,128)(2,1)} %bitcast.11, bf16[2,4,4096]{2,1,0:T(4,128)(2,1)} %refs_hbm.1), custom_call_target="tpu_custom_call" | custom-call | tf_op jit(solution)/shard_map/pack/pallas_call | solution.py:467
  3.7 0.0 copy-start.2
  3.7 0.0 copy-start
  3.7 7.5 %all-to-all-start = ((bf16[16,8,4096]{2,1,0:T(8,128)(2,1)}), bf16[16,8,4096]{2,1,0:T(8,128)(2,1)S(1)}, u32[]{:S(2)}, u32[]{:S(2)}) async-start(bf16[16,8,4096]{2,1,0:T(8,128)(2,1)} %bitcast.10), calls=%async_computation | async-start | bytes 2097152 | tf_op jit(solution)/shard_map/all_to_all | solution.py:493
  11.2 0.0 copy-done.2
  11.2 4.4 %collective-permute-start = (bf16[2,4,4096]{2,1,0:T(4,128)(2,1)S(1)}, bf16[2,4,4096]{2,1,0:T(4,128)(2,1)S(1)}, u32[]{:S(2)}, u32[]{:S(2)}) collective-permute-start(bf16[2,4,4096]{2,1,0:T(4,128)(2,1)S(1)} %copy-done.2), channel_id=1, source_target_pairs={{0,15},{1,14},{2,13},{3,12},{4,11},{5,10},{6,9},{7,8},{8,7},{9,6},... | collective-permute-start | bytes 196616 | tf_op jit(solution)/shard_map/ppermute | solution.py:466
  15.7 19.4 %collective-permute-done.far_ref = bf16[2,4,4096]{2,1,0:T(4,128)(2,1)S(1)} collective-permute-done((bf16[2,4,4096]{2,1,0:T(4,128)(2,1)S(1)}, bf16[2,4,4096]{2,1,0:T(4,128)(2,1)S(1)}, u32[]{:S(2)}, u32[]{:S(2)}) %collective-permute-start) | collective-permute-done | bytes 65568 | tf_op jit(solution)/shard_map/ppermute | solution.py:466
  35.1 0.0 copy-done
  35.1 0.6 near.1.near_ref
  35.7 0.0 all-to-all-done
  35.7 0.0 copy-start.3
  35.7 0.2 trim.1
  36.0 0.0 copy-start.1
  36.0 1.6 %collective-permute-start.1 = (bf16[64,4096]{1,0:T(8,128)(2,1)S(1)}, bf16[64,4096]{1,0:T(8,128)(2,1)S(1)}, u32[]{:S(2)}, u32[]{:S(2)}) collective-permute-start(bf16[64,4096]{1,0:T(8,128)(2,1)S(1)} %get-tuple-element.21), channel_id=1, source_target_pairs={{0,16},{16,0},{1,17},{17,1},{2,18},{18,2},{3,19},{19,3},{4,20},{20... | collective-permute-start | bytes 1572872 | tf_op jit(solution)/shard_map/ppermute | solution.py:504
  37.6 0.0 copy-done.3
  37.6 0.1 copy.6.orient_ref
  37.6 0.0 copy-done.1
  37.6 5.1 %logits.1 = f32[512,128]{1,0:T(8,128)} custom-call(s32[16,6]{1,0:T(8,128)S(1)} %copy.6.orient_ref, s32[1,2]{1,0:T(1,128)S(1)} %copy-done.1, bf16[128,4096]{1,0:T(8,128)(2,1)S(1)} %bitcast.7, f32[256,8,128]{2,1,0:T(8,128)S(1)} %near.1.near_ref), custom_call_target="tpu_custom_call" | custom-call | tf_op jit(solution)/shard_map/logits/pallas_call | solution.py:505
  42.7 6.9 %all-to-all-start.1 = ((f32[32,16,128]{2,1,0:T(8,128)}), f32[32,16,128]{2,1,0:T(8,128)S(1)}, u32[]{:S(2)}, u32[]{:S(2)}) async-start(f32[32,16,128]{2,1,0:T(8,128)} %bitcast.3), calls=%async_computation.1 | async-start | bytes 524288 | tf_op jit(solution)/shard_map/all_to_all | solution.py:522
  49.6 1.8 %collective-permute-start.2 = (bf16[16,4096]{1,0:T(8,128)(2,1)S(1)}, bf16[16,4096]{1,0:T(8,128)(2,1)S(1)}, u32[]{:S(2)}, u32[]{:S(2)}) collective-permute-start(bf16[16,4096]{1,0:T(8,128)(2,1)S(1)} %get-tuple-element.24), channel_id=1, source_target_pairs={{0,16},{16,0},{1,17},{17,1},{2,18},{18,2},{3,19},{19,3},{4,20},{20... | collective-permute-start | bytes 393224 | tf_op jit(solution)/shard_map/ppermute | solution.py:540
  51.4 0.0 collective-permute-done.1.core_ref.refs_0_
  51.4 0.4 edges.1
  51.9 0.1 collective-permute-start.3
  51.9 5.5 %collective-permute-done.2.refs_1_ = bf16[16,4096]{1,0:T(8,128)(2,1)S(1)} collective-permute-done((bf16[16,4096]{1,0:T(8,128)(2,1)S(1)}, bf16[16,4096]{1,0:T(8,128)(2,1)S(1)}, u32[]{:S(2)}, u32[]{:S(2)}) %collective-permute-start.2) | collective-permute-done | bytes 131104 | tf_op jit(solution)/shard_map/ppermute | solution.py:540
  57.5 2.4 %all-to-all-done.1 = f32[32,16,128]{2,1,0:T(8,128)S(1)} async-done(((f32[32,16,128]{2,1,0:T(8,128)}), f32[32,16,128]{2,1,0:T(8,128)S(1)}, u32[]{:S(2)}, u32[]{:S(2)}) %all-to-all-start.1) | async-done | bytes 262176 | tf_op jit(solution)/shard_map/all_to_all | solution.py:522
  59.9 0.0 collective-permute-done.3.refs_2_
  59.9 3.2 %sums.1 = (f32[8,4,4096]{2,1,0:T(4,128)}, f32[1,1]{1,0:T(1,128)}) custom-call(f32[512,128]{1,0:T(8,128)S(1)} %bitcast.9, bf16[128,896]{1,0:T(8,128)(2,1)S(1)} %get-tuple-element.22.own_table, bf16[128,896]{1,0:T(8,128)(2,1)S(1)} %get-tuple-element.23.far_table, bf16[128,4096]{1,0:T(8,128)(2,1)S(1)} %bitcast.8, ...), custom_call_target="tpu_custom_call" | custom-call | tf_op jit(solution)/shard_map/sums/pallas_call | solution.py:545
Async XLA Ops:
  3.7 7.6 %copy-start.2 = (bf16[2,4,4096]{2,1,0:T(4,128)(2,1)S(1)}, bf16[2,4,4096]{2,1,0:T(4,128)(2,1)}, u32[]{:S(2)}) copy-start(bf16[2,4,4096]{2,1,0:T(4,128)(2,1)} %refs_hbm.1) | copy-start | bytes 196612
  3.7 31.4 %copy-start = (bf16[16,4096]{1,0:T(8,128)(2,1)S(1)}, bf16[16,4096]{1,0:T(8,128)(2,1)}, u32[]{:S(2)}) copy-start(bf16[16,4096]{1,0:T(8,128)(2,1)} %get-tuple-element.16.own_ref) | copy-start | bytes 393220
  3.7 32.0 %all-to-all-start = ((bf16[16,8,4096]{2,1,0:T(8,128)(2,1)}), bf16[16,8,4096]{2,1,0:T(8,128)(2,1)S(1)}, u32[]{:S(2)}, u32[]{:S(2)}) async-start(bf16[16,8,4096]{2,1,0:T(8,128)(2,1)} %bitcast.10), calls=%async_computation | async-start | bytes 2097152 | tf_op jit(solution)/shard_map/all_to_all | solution.py:493
  11.2 23.9 %collective-permute-start = (bf16[2,4,4096]{2,1,0:T(4,128)(2,1)S(1)}, bf16[2,4,4096]{2,1,0:T(4,128)(2,1)S(1)}, u32[]{:S(2)}, u32[]{:S(2)}) collective-permute-start(bf16[2,4,4096]{2,1,0:T(4,128)(2,1)S(1)} %copy-done.2), channel_id=1, source_target_pairs={{0,15},{1,14},{2,13},{3,12},{4,11},{5,10},{6,9},{7,8},{8,7},{9,6},... | collective-permute-start | bytes 196616 | tf_op jit(solution)/shard_map/ppermute | solution.py:466
  35.7 1.8 %copy-start.3 = (s32[16,6]{0,1:T(8,128)S(1)}, s32[16,6]{0,1:T(8,128)}, u32[]{:S(2)}) copy-start(s32[16,6]{0,1:T(8,128)} %param.6) | copy-start | bytes 1156
  36.0 1.7 %copy-start.1 = (s32[1,2]{1,0:T(1,128)S(1)}, s32[1,2]{1,0:T(1,128)}, u32[]{:S(2)}) copy-start(s32[1,2]{1,0:T(1,128)} %allowed_ref.1) | copy-start | bytes 28
  36.0 15.4 %collective-permute-start.1 = (bf16[64,4096]{1,0:T(8,128)(2,1)S(1)}, bf16[64,4096]{1,0:T(8,128)(2,1)S(1)}, u32[]{:S(2)}, u32[]{:S(2)}) collective-permute-start(bf16[64,4096]{1,0:T(8,128)(2,1)S(1)} %get-tuple-element.21), channel_id=1, source_target_pairs={{0,16},{16,0},{1,17},{17,1},{2,18},{18,2},{3,19},{19,3},{4,20},{20... | collective-permute-start | bytes 1572872 | tf_op jit(solution)/shard_map/ppermute | solution.py:504
  42.7 17.1 %all-to-all-start.1 = ((f32[32,16,128]{2,1,0:T(8,128)}), f32[32,16,128]{2,1,0:T(8,128)S(1)}, u32[]{:S(2)}, u32[]{:S(2)}) async-start(f32[32,16,128]{2,1,0:T(8,128)} %bitcast.3), calls=%async_computation.1 | async-start | bytes 524288 | tf_op jit(solution)/shard_map/all_to_all | solution.py:522
  49.6 7.9 %collective-permute-start.2 = (bf16[16,4096]{1,0:T(8,128)(2,1)S(1)}, bf16[16,4096]{1,0:T(8,128)(2,1)S(1)}, u32[]{:S(2)}, u32[]{:S(2)}) collective-permute-start(bf16[16,4096]{1,0:T(8,128)(2,1)S(1)} %get-tuple-element.24), channel_id=1, source_target_pairs={{0,16},{16,0},{1,17},{17,1},{2,18},{18,2},{3,19},{19,3},{4,20},{20... | collective-permute-start | bytes 393224 | tf_op jit(solution)/shard_map/ppermute | solution.py:540
  51.9 8.0 %collective-permute-start.3 = (bf16[16,4096]{1,0:T(8,128)(2,1)S(1)}, bf16[16,4096]{1,0:T(8,128)(2,1)S(1)}, u32[]{:S(2)}, u32[]{:S(2)}) collective-permute-start(bf16[16,4096]{1,0:T(8,128)(2,1)S(1)} %get-tuple-element.25), channel_id=1, source_target_pairs={{0,1},{1,0},{2,3},{3,2},{4,5},{5,4},{6,7},{7,6},{8,9},{9,8},{10,11... | collective-permute-start | bytes 393224 | tf_op jit(solution)/shard_map/ppermute | solution.py:541

commit v4 on v3

v4 whole, which is shorter than its diff:
```python
import functools
import math

import jax
import jax.numpy as jnp
from jax import lax
from jax.experimental import pallas as pl
from jax.experimental.pallas import tpu as pltpu
from jax.sharding import PartitionSpec as P

ORI = 8
LANES = 128
ROWS = 8
MOVES = [(0, 0, 0), (1, 0, 0), (-1, 0, 0), (0, 1, 0), (0, -1, 0), (0, 0, 1), (0, 0, -1)]
FLAT = [(0, 0), (1, 0), (-1, 0), (0, 1), (0, -1)]
SLOTS = 8
BARRED = -1e30
VMEM_BYTES = 24 * 1024 * 1024
MOST_VMEM = 62 * 1024 * 1024


def lane_iota(shape):
    return lax.broadcasted_iota(jnp.int32, shape, len(shape) - 1)


def row_iota(shape):
    return lax.broadcasted_iota(jnp.int32, shape, 0)


def swap_halves(x):
    return pltpu.roll(x, LANES // 2, 1)


def rows_by_rows(a, b):
    return lax.dot_general(a, b, (((1,), (1,)), ((), ())), preferred_element_type=jnp.float32)


def pick_lanes(x, index):
    return jnp.take_along_axis(x, index, axis=1, mode="promise_in_bounds")


def tile(m):
    return slice(m * LANES, (m + 1) * LANES)


def lanes_of(edge, parts):
    h = edge // parts
    return edge * edge * h // ROWS, edge * edge // ROWS, 4 * h * edge


def turn_rows(edge, planes, x, z, flat, turned):
    low = lane_iota((planes, LANES)) < edge
    for m in range(edge // 2):
        piece = x[:planes, tile(m)]
        flat[pl.ds(2 * m, planes, stride=edge), :] = piece
        flat[pl.ds(2 * m + 1, planes, stride=edge), :] = swap_halves(piece)
    for n in range(0, planes, 2):
        block = flat[n * edge : (n + 2) * edge, :].T[:edge, :]
        turned[n * edge : (n + 1) * edge, :] = block
        turned[(n + 1) * edge : (n + 2) * edge, :] = swap_halves(block)
    for m in range(edge // 2):
        even = turned[pl.ds(2 * m, planes, stride=edge), :]
        odd = turned[pl.ds(2 * m + 1, planes, stride=edge), :]
        z[:planes, tile(m)] = jnp.where(low, even, swap_halves(odd))


def pack_kernel(
    edge, parts, part_hbm, refs_hbm, out_ref, both_ref, part_ref, refs_ref, sems, ring, stage, x, z, flat, turned
):
    h = edge // parts
    planes = 2 * h
    core, outer, _ = lanes_of(edge, parts)
    chunk = 2 * ROWS
    refs_copy = pltpu.make_async_copy(refs_hbm, refs_ref, sems.at[0])
    refs_copy.start()
    copies = []
    for i in range(edge // chunk):
        rows = pl.ds(i * chunk, chunk)
        copies.append(pltpu.make_async_copy(part_hbm.at[rows], part_ref.at[rows], sems.at[1 + i]))
        copies[-1].start()
    refs_copy.wait()
    for c in range(2):
        x[c * h : (c + 1) * h, :] = refs_ref[c].astype(jnp.float32)
    turn_rows(edge, planes, x, z, flat, turned)
    both_ref[...] = jnp.concatenate([x[:planes, :], z[:planes, :]], axis=0).astype(jnp.bfloat16)
    if planes < ROWS:
        stage[...] = jnp.zeros_like(stage)
    slab = h * edge
    for s in range(parts):
        top = s * ROWS
        mirror = parts - 1 - s
        for number, (array, place) in enumerate(((x, s), (x, mirror), (z, s), (z, mirror))):
            left = core + outer + number * slab
            stage[top : top + planes, left : left + slab] = array[:planes, place * slab : (place + 1) * slab]
    last = len(copies) - 1
    done = 0
    for i in [last] + list(range(last)):
        copies[i].wait()
        rows = slice(i * chunk, (i + 1) * chunk)
        ring[ROWS + i * chunk : ROWS + (i + 1) * chunk, :] = part_ref[rows, :].astype(jnp.float32)
        if i == last:
            ring[ROWS - 1 : ROWS, :] = ring[ROWS + edge - 1 : ROWS + edge, :]
        if i == 0:
            ring[ROWS + edge : ROWS + edge + 1, :] = ring[ROWS : ROWS + 1, :]
        ready = 0 if i == last else (parts if i == last - 1 else ((i + 1) * chunk - 1) // h)
        while done + 2 <= ready:
            for s in (done, done + 1):
                top, first = s * ROWS, ROWS + h * s
                for f in range(ROWS // h):
                    stage[top + f * h : top + (f + 1) * h, :core] = ring[first : first + h, f * core : (f + 1) * core]
                end = first - 1 if s % 2 == 0 else first + h
                for e in range(ROWS):
                    stage[top + e : top + e + 1, core : core + outer] = ring[end : end + 1, e * outer : (e + 1) * outer]
            both = slice(done * ROWS, (done + 2) * ROWS)
            out_ref[both, :] = stage[both, :].astype(jnp.bfloat16)
            done += 2


def own_kernel(h, columns, both_ref, out_ref):
    planes = 2 * h
    own = both_ref[...].astype(jnp.float32)
    for turn in range(2):
        for c in range(2):
            top = turn * planes + c * h
            for copy in range(ROWS // h):
                for m in range(columns):
                    out_ref[(turn * 2 + c) * columns + m, copy * h : (copy + 1) * h, :] = own[top : top + h, tile(m)]


def logits_kernel(
    edge, parts, total, orient_any, allowed_any, got_ref, own_ref, far_ref, out_ref, base_ref, bar_ref,
    orient_ref, allowed_ref, sems, x, z, far_flat, far_turned, wide_f32, flat, turned, kinds, shifted, gram,
):
    h = edge // parts
    wide = edge * edge
    columns = wide // LANES
    rows = total * h
    core, outer, extra = lanes_of(edge, parts)
    planes = 2 * h
    me = lax.axis_index("dp")
    scalars = [
        pltpu.make_async_copy(orient_any, orient_ref, sems.at[0]),
        pltpu.make_async_copy(allowed_any, allowed_ref, sems.at[1]),
    ]
    for copy in scalars:
        copy.start()
    low = lane_iota((ROWS, LANES)) < edge
    for j in range(extra // LANES):
        wide_f32[j] = got_ref[:, tile((core + outer) // LANES + j)].astype(jnp.float32)

    def keep(first, second, value, m):
        if planes == ROWS:
            upper = row_iota((ROWS, LANES)) < h
            other = pltpu.roll(value, h, 0)
            kinds[first * columns + m] = jnp.where(upper, value, other)
            kinds[second * columns + m] = jnp.where(upper, other, value)
        else:
            for number, kind in enumerate((first, second)):
                for copy in range(ROWS // h):
                    kinds[kind * columns + m, copy * h : (copy + 1) * h, :] = value[number * h : (number + 1) * h, :]

    for turn in range(2):
        for c in range(2):
            source, target = (turn * 2 + c) * columns, (turn * 4 + c) * columns
            kinds[target : target + columns] = own_ref[source : source + columns]
    for c in range(2):
        far = far_ref[c].astype(jnp.float32)
        for l in range(h):
            x[c * h + l : c * h + l + 1, :] = far[h - 1 - l : h - l, :]
    turn_rows(edge, planes, x, z, far_flat, far_turned)
    for m in range(columns):
        keep(2, 3, x[:planes, tile(m)], m)
        keep(6, 7, z[:planes, tile(m)], m)
    for axis in (1, 2):
        for c in range(2):
            for jl in range(h):
                first = (axis - 1) * 2 * h * edge // LANES
                for s in range(0, parts, ROWS):
                    tiles = [
                        wide_f32[first + i, pl.ds(s * ROWS + c * h + jl, ROWS, stride=ROWS), :] for i in range(h)
                    ]
                    for l in range(h):
                        plain, mirrored = tiles[l // 2], tiles[h // 2 + (h - 1 - l) // 2]
                        if l % 2 == 0:
                            value = jnp.where(low, plain, mirrored)
                        else:
                            value = swap_halves(jnp.where(low, mirrored, plain))
                        flat[pl.ds((c * h + l) * edge + s * h + jl, ROWS, stride=h), :] = value
        for l in range(h):
            block = jnp.concatenate(
                [flat[(c * h + l) * edge : (c * h + l + 1) * edge, :] for c in range(2)], axis=0
            ).T
            for side in range(2):
                turned[(side * h + l) * edge : (side * h + l + 1) * edge, :] = block[side * edge : (side + 1) * edge, :]
        part = lane_iota((planes, LANES)) < edge
        for m in range(edge // 2):
            even = flat[pl.ds(2 * m, planes, stride=edge), :]
            odd = flat[pl.ds(2 * m + 1, planes, stride=edge), :]
            keep(axis * 8, axis * 8 + 1, jnp.where(part, even, swap_halves(odd)), m)
            keep(axis * 8 + 2, axis * 8 + 3, jnp.where(part, swap_halves(even), odd), m)
            even = turned[pl.ds(2 * m, planes, stride=edge), :]
            odd = turned[pl.ds(2 * m + 1, planes, stride=edge), :]
            keep(axis * 8 + 4, axis * 8 + 6, jnp.where(part, even, swap_halves(odd)), m)
            keep(axis * 8 + 5, axis * 8 + 7, jnp.where(part, swap_halves(even), odd), m)
    for copy in scalars:
        copy.wait()
    lane = lane_iota((ROWS, LANES))
    slot = row_iota((ROWS, LANES)) // h
    per = ROWS // h
    lows = lane < edge
    after = (lane // edge) * edge + (lane + 1) % edge
    before = (lane // edge) * edge + (lane + edge - 1) % edge
    start, step, index = [], [], []
    for b in range(total // per):
        xor = jnp.zeros((ROWS, LANES), jnp.int32)
        for i in range(per):
            o = b * per + i
            turn = (orient_ref[o, 1] > orient_ref[o, 2]).astype(jnp.int32)
            kind = orient_ref[o, 0] * 8 + turn * 4 + orient_ref[o, 3] * 2 + o // ORI
            start.append(kind * columns + orient_ref[o, 4] * (columns - 1))
            step.append(1 - 2 * orient_ref[o, 4])
            xor = jnp.where(slot == i, orient_ref[o, 4] * edge + orient_ref[o, 5] * (edge - 1), xor)
        index.append([lane ^ xor, (lane ^ edge) ^ xor, before ^ xor, after ^ xor])

    def piece(o, j):
        return kinds[start[o] + j * step[o]]

    def column(j):
        found = []
        for b in range(total // per):
            value = piece(b * per, j)
            for i in range(1, per):
                value = jnp.where(slot == i, piece(b * per + i, j), value)
            found.append([pick_lanes(value, way) for way in index[b]])
        return [list(way) for way in zip(*found, strict=True)]

    behind = column(columns - 1)[1]
    here = column(0)
    for j in range(columns):
        ahead = column((j + 1) % columns)
        results = [
            here[0],
            [jnp.where(lows, x, y) for x, y in zip(behind, here[1], strict=True)],
            [jnp.where(lows, x, y) for x, y in zip(here[1], ahead[1], strict=True)],
            here[2],
            here[3],
        ]
        for number, result in enumerate(results):
            result = jnp.concatenate(result, axis=0).astype(jnp.bfloat16)
            shifted[number * rows : (number + 1) * rows, tile(j)] = result
            if number == 0:
                base_ref[:, tile(j)] = result
        behind, here = here[1], ahead
    many = parts * ROWS
    fraction = lane_iota((len(FLAT) * rows, many)) % ROWS // h
    found = None
    for f in range(ROWS // h):
        block = rows_by_rows(shifted[:, f * core : (f + 1) * core], got_ref[:, :core])
        found = block if found is None else jnp.where(fraction == f, block, found)
    gram[...] = found
    place = lane_iota((total, many)) % h
    kept = []
    for t, move in enumerate(MOVES):
        source = FLAT.index((move[1], move[2]))
        total_t = None
        for l in range(h):
            if many == LANES:
                block = gram[pl.ds(source * rows + l, total, stride=h), :]
            else:
                block = jnp.concatenate(
                    [gram[source * rows + o * h + l : source * rows + o * h + l + 1, :] for o in range(total)], axis=0
                )
            block = jnp.where(place == l + move[0], block, 0.0)
            total_t = block if total_t is None else total_t + block
        kept.append(total_t)
    if many == LANES:
        lane = lane_iota((total, LANES))
        result = jnp.zeros((total, LANES), jnp.float32)
        for t in range(len(MOVES)):
            value = kept[t]
            for step in (1, 2, 4):
                value = value + pltpu.roll(value, LANES - step, 1)
            result = jnp.where(lane // parts == t, pick_lanes(value, (lane % parts) * ROWS), result)
    else:
        shape = (len(MOVES) * many, SLOTS * parts)
        picker = (row_iota(shape) // ROWS == lane_iota(shape)).astype(jnp.float32)
        result = exactly(jnp.concatenate(kept, axis=1), picker)
    out_ref[...] = result
    kin = row_iota(result.shape) // ORI
    permit = jnp.zeros(result.shape, jnp.int32)
    for c in range(total // ORI):
        permit = jnp.where(kin == c, allowed_ref[0, c], permit)
    barred = (lane_iota(result.shape) % parts == me) & (permit != 1)
    bar_ref[...] = jnp.where(barred, jnp.float32(BARRED), jnp.float32(0.0))


def exactly(a, b):
    return jnp.dot(a, b, preferred_element_type=jnp.float32, precision=lax.Precision.HIGHEST)


def finish_kernel(
    h, parts, devices, scale, part_ref, base_ref, bar_ref, outer_ref, inner_ref, out_ref, ends
):
    me = lax.axis_index("dp")
    total = part_ref.shape[0]
    ends[:, : 2 * parts] = rows_by_rows(base_ref[...], jnp.concatenate([outer_ref[...], inner_ref[...]], axis=0))
    beyond = {1: (h - 1, parts * (1 - me % 2)), -1: (0, parts * (me % 2))}
    result = part_ref[...]
    lane = lane_iota(result.shape)
    for t, move in enumerate(MOVES):
        if not move[0]:
            continue
        l, left = beyond[move[0]]
        if result.shape[1] == LANES:
            value = pick_lanes(ends[pl.ds(l, total, stride=h), :], lane % parts + left)
            result = result + jnp.where(lane // parts == t, value, 0.0)
        else:
            shape = (2 * parts, SLOTS * parts)
            block = jnp.concatenate([ends[o * h + l : o * h + l + 1, : 2 * parts] for o in range(total)], axis=0)
            chosen = (row_iota(shape) == lane_iota(shape) % parts + left) & (lane_iota(shape) // parts == t)
            result = result + exactly(block, chosen.astype(jnp.float32))
    result = result * scale
    result = result + bar_ref[...]
    for d in range(devices):
        out_ref[d * total : (d + 1) * total, :] = result


def trim_kernel(edge, parts, got_ref, core_ref, outer_ref, lacking_ref):
    h = edge // parts
    core, outer, _ = lanes_of(edge, parts)
    core_ref[...] = got_ref[:, :core]
    whole = got_ref[:, core : core + outer].reshape(parts, ROWS, outer)
    for e in range(ROWS):
        outer_ref[:, e * outer : (e + 1) * outer] = whole[:, e, :]
    own_end(h, got_ref[:, :core].reshape(parts, ROWS, core), lacking_ref)


def own_end(h, whole, out_ref):
    core = whole.shape[2]
    even = lax.axis_index("dp") % 2 == 0

    @pl.when(even)
    def _():
        for f in range(ROWS // h):
            out_ref[:, f * core : (f + 1) * core] = whole[:, f * h + h - 1, :]

    @pl.when(jnp.logical_not(even))
    def _():
        for f in range(ROWS // h):
            out_ref[:, f * core : (f + 1) * core] = whole[:, f * h, :]


def far_ends_kernel(h, core_ref, out_ref, *tables):
    parts = core_ref.shape[0] // ROWS
    own_end(h, core_ref[...].reshape(parts, ROWS, core_ref.shape[1]), out_ref)
    for table in tables:
        many = parts * ROWS
        column = lane_iota(table.shape)
        particle = column % many // ROWS
        table[...] = (column // many * parts + particle == row_iota(table.shape)).astype(table.dtype)


def sums_kernel(edge, parts, total, groups, logits_ref, spread_ref, got_ref, *refs):
    pieces, refs = refs[: 3 * groups - 1], refs[3 * groups - 1 :]
    out_hbm, log_ref, out_ref, sems, in_sems, chances, weights, end_weights, table, merged, ends = refs
    h = edge // parts
    wide = edge * edge
    columns = wide // LANES
    owned = total // groups
    rows = owned * h
    span = SLOTS * parts
    many = parts * ROWS
    core, _, _ = lanes_of(edge, parts)
    mine, me = lax.axis_index("ref"), lax.axis_index("dp")
    incoming = []
    at_core, at_end = many, 0
    for number, piece in enumerate(pieces):
        if piece.shape[0] == many:
            target = merged.at[pl.ds(at_core, many)]
            at_core += many
        else:
            target = ends.at[pl.ds(at_end, parts)]
            at_end += parts
        incoming.append(pltpu.make_async_copy(piece, target, in_sems.at[number]))
        incoming[-1].start()
    merged[:many, :] = got_ref[:, :core]
    dot = functools.partial(jnp.dot, preferred_element_type=jnp.float32)
    lane = lane_iota((total, span))
    log_evidence = jnp.zeros((1, span), jnp.float32)
    for g in range(groups):
        scores = [logits_ref[(g * parts + s) * total : (g * parts + s + 1) * total, :] for s in range(parts)]
        while len(scores) > 1:
            scores = [sum(scores[i : i + 2]) for i in range(0, len(scores), 2)]
        score = jnp.where(lane >= len(MOVES) * parts, jnp.float32(-3e38), scores[0])
        peak = jnp.max(score, axis=0, keepdims=True)
        for step in (1, 2, 4):
            peak = jnp.maximum(peak, pltpu.roll(peak, step * parts, 1))
        expo = jnp.exp(score - peak)
        mass = jnp.sum(expo, axis=0, keepdims=True)
        for step in (1, 2, 4):
            mass = mass + pltpu.roll(mass, step * parts, 1)
        chances[g] = expo / mass
        log_evidence = jnp.where(mine == g, peak + jnp.log(mass), log_evidence)
    log_ref[...] = jnp.sum(jnp.where(lane_iota((1, span)) == me, log_evidence, 0.0), axis=1, keepdims=True)
    every = ends.shape[0]
    place, fraction = lane_iota((owned, many)) % h, lane_iota((owned, many)) % ROWS // h
    laid_ends = jnp.zeros((owned, 2 * every), jnp.float32)
    for k in range(groups):
        g = lax.rem(mine + groups - k, groups)
        if owned % ROWS == 0:
            chosen = chances[g, pl.ds(pl.multiple_of(mine * owned, ROWS), owned), :].astype(jnp.bfloat16)
        else:
            at = mine * owned + row_iota((owned, total))
            chooser = (at == lane_iota((owned, total))).astype(jnp.bfloat16)
            chosen = dot(chooser, chances[g].astype(jnp.bfloat16)).astype(jnp.bfloat16)
        laid = dot(chosen, spread_ref[...])
        for slot in range(len(FLAT)):
            for l in range(h):
                value = jnp.zeros((owned, many), jnp.float32)
                for t, move in enumerate(MOVES):
                    if FLAT.index((move[1], move[2])) == slot:
                        value = jnp.where(place == l + move[0], laid[:, t * many : (t + 1) * many], value)
                for f in range(ROWS // h):
                    part = jnp.where(fraction == f, value, 0.0)
                    for m in range(many // LANES):
                        at = (f * groups + k) * (many // LANES) + m
                        weights[at, pl.ds(slot * rows + l, owned, stride=h), :] = part[:, tile(m)]
        shape = (span, 2 * every)
        column = lane_iota(shape)
        up, down = MOVES.index((1, 0, 0)), MOVES.index((-1, 0, 0))
        shift = jnp.where(column < every, up, down)
        here = (column % every // (2 * parts) == k) & (row_iota(shape) == shift * parts + column % parts)
        laid_ends = laid_ends + dot(chosen, here.astype(jnp.bfloat16))
    side = lane_iota((owned, every)) % (2 * parts) // parts
    for l in range(h):
        value = jnp.zeros((owned, every), jnp.float32)
        if l == h - 1:
            value = value + jnp.where(side == 1 - me % 2, laid_ends[:, :every], 0.0)
        if l == 0:
            value = value + jnp.where(side == me % 2, laid_ends[:, every:], 0.0)
        if every < LANES:
            value = jnp.concatenate([value, jnp.zeros((owned, LANES - every), jnp.float32)], axis=1)
        for m in range(end_weights.shape[0]):
            end_weights[m, pl.ds(l, owned, stride=h), :] = value[:, tile(m)]
    for copy in incoming:
        copy.wait()
    count = groups * (many // LANES)
    for f in range(ROWS // h):
        both = jnp.concatenate([weights[f * count + m] for m in range(count)], axis=1).astype(jnp.bfloat16)
        table[:, f * core : (f + 1) * core] = dot(both, merged[...])
    both = jnp.concatenate([end_weights[m] for m in range(end_weights.shape[0])], axis=1)[:, :every]
    table[:rows, :] += dot(both.astype(jnp.bfloat16), ends[...])
    lane = lane_iota((rows, LANES))
    low = lane < edge
    after = (lane // edge) * edge + (lane + 1) % edge
    before = (lane // edge) * edge + (lane + edge - 1) % edge

    def cut(slot, j):
        return table[slot * rows : (slot + 1) * rows, tile(j % columns)]

    pieces = sems.shape[0]
    copies = []
    up = swap_halves(cut(1, 0))
    down = swap_halves(cut(2, columns - 1))
    for j in range(columns):
        up_next, down_next = swap_halves(cut(1, j + 1)), swap_halves(cut(2, j))
        value = cut(0, j) + jnp.where(low, up, up_next) + jnp.where(low, down, down_next)
        value = value + pick_lanes(cut(3, j), after) + pick_lanes(cut(4, j), before)
        up, down = up_next, down_next
        for o in range(owned):
            out_ref[o, :, tile(j)] = value[o * h : (o + 1) * h, :]
        if (j + 1) % (columns // pieces) == 0:
            number = len(copies)
            part = pl.ds(number * (wide // pieces), wide // pieces)
            copies.append(
                pltpu.make_async_copy(out_ref.at[:, :, part], out_hbm.at[:, :, part], sems.at[number])
            )
            copies[-1].start()
    for copy in copies:
        copy.wait()


def in_vmem():
    return pl.BlockSpec(memory_space=pltpu.VMEM)


def anywhere():
    return pl.BlockSpec(memory_space=pl.ANY)


def per_device(particles, references, orient, allowed):
    edge = particles.shape[1]
    wide = edge * edge
    total = orient.shape[0]
    parts = lax.axis_size("dp")
    groups = lax.axis_size("ref")
    devices = parts * groups
    h = edge // parts
    planes = 2 * h
    rows = total * h
    owned = total // groups
    span = SLOTS * parts
    core_lanes, _, extra = lanes_of(edge, parts)
    payload = sum(lanes_of(edge, parts))
    scale = 3.0 / math.sqrt(edge**3)
    params = pltpu.CompilerParams(vmem_limit_bytes=VMEM_BYTES)
    f32, bf16 = jnp.float32, jnp.bfloat16
    array = jax.ShapeDtypeStruct
    turning = [
        pltpu.VMEM((ROWS, wide), f32),
        pltpu.VMEM((ROWS, wide), f32),
        pltpu.VMEM((planes * edge, LANES), f32),
        pltpu.VMEM((planes * edge, LANES), f32),
    ]
    far = lax.ppermute(references, "dp", [(i, parts - 1 - i) for i in range(parts)])
    sent, both = pl.pallas_call(
        functools.partial(pack_kernel, edge, parts),
        out_shape=(array((parts * ROWS, payload), bf16), array((2 * planes, wide), bf16)),
        in_specs=[anywhere()] * 2,
        out_specs=(in_vmem(), in_vmem()),
        scratch_shapes=[
            pltpu.VMEM((edge, wide), bf16),
            pltpu.VMEM(references.shape, bf16),
            pltpu.SemaphoreType.DMA((1 + edge // (2 * ROWS),)),
            pltpu.VMEM((edge + 2 * ROWS, wide), f32),
            pltpu.VMEM((parts * ROWS, payload), f32),
            *turning,
        ],
        compiler_params=pltpu.CompilerParams(vmem_limit_bytes=MOST_VMEM),
        name="pack",
    )(particles.reshape(edge, wide), references)
    own = pl.pallas_call(
        functools.partial(own_kernel, h, wide // LANES),
        out_shape=array((4 * wide // LANES, ROWS, LANES), f32),
        in_specs=[in_vmem()],
        out_specs=in_vmem(),
        compiler_params=params,
        cost_estimate=pl.CostEstimate(flops=0, bytes_accessed=16 * 1024 * 1024, transcendentals=0),
        name="own",
    )(both)
    got = lax.all_to_all(sent, "dp", 0, 0, tiled=True)
    got, own, far = lax.optimization_barrier((got, own, far))
    plane = array((parts, wide), bf16)
    core, outer, lacking = pl.pallas_call(
        functools.partial(trim_kernel, edge, parts),
        out_shape=(array((parts * ROWS, core_lanes), bf16), plane, plane),
        in_specs=[in_vmem()],
        out_specs=(in_vmem(),) * 3,
        compiler_params=params,
        name="trim",
    )(got)
    pairs = [(i, i ^ 1) for i in range(parts)]
    inner = lax.ppermute(lacking, "dp", pairs)
    steps = [[(i, (i + k) % groups) for i in range(groups)] for k in range(1, groups)]
    cores = [lax.ppermute(core, "ref", step) for step in steps]
    partial, base, bars = pl.pallas_call(
        functools.partial(logits_kernel, edge, parts, total),
        out_shape=(array((total, span), f32), array((rows, wide), bf16), array((total, span), f32)),
        in_specs=[anywhere()] * 2 + [in_vmem()] * 3,
        out_specs=(in_vmem(),) * 3,
        scratch_shapes=[
            pltpu.SMEM(orient.shape, jnp.int32),
            pltpu.SMEM(allowed.shape, jnp.int32),
            pltpu.SemaphoreType.DMA((2,)),
            *turning,
            pltpu.VMEM((extra // LANES, parts * ROWS, LANES), f32),
            pltpu.VMEM((planes * edge, LANES), f32),
            pltpu.VMEM((planes * edge, LANES), f32),
            pltpu.VMEM((24 * wide // LANES, ROWS, LANES), f32),
            pltpu.VMEM((len(FLAT) * rows, wide), bf16),
            pltpu.VMEM((len(FLAT) * rows, parts * ROWS), f32),
        ],
        compiler_params=params,
        name="logits",
    )(orient, allowed, got, own, far)
    partial = pl.pallas_call(
        functools.partial(finish_kernel, h, parts, devices, scale),
        out_shape=array((devices * total, span), f32),
        in_specs=[in_vmem()] * 5,
        out_specs=in_vmem(),
        scratch_shapes=[pltpu.VMEM((rows, LANES), f32)],
        compiler_params=params,
        name="finish",
    )(partial, base, bars, outer, inner)
    partial, outside = lax.optimization_barrier((partial, outer))
    logits = lax.all_to_all(partial, ("ref", "dp"), 0, 0, tiled=True)
    tables = [array((span, len(MOVES) * parts * ROWS), bf16)]
    pieces = [outer, inner]
    for core, step in zip(cores, steps, strict=True):
        lacking, *laid = pl.pallas_call(
            functools.partial(far_ends_kernel, h),
            out_shape=(plane, *tables),
            in_specs=[in_vmem()],
            out_specs=(in_vmem(),) * (1 + len(tables)),
            compiler_params=params,
            cost_estimate=pl.CostEstimate(flops=0, bytes_accessed=16 * 1024 * 1024, transcendentals=0),
            name="far_ends",
        )(core)
        spread = laid[0] if laid else spread
        pieces += [core, lax.ppermute(outside, "ref", step), lax.ppermute(lacking, "dp", pairs)]
        tables = []
    every = groups * 2 * parts
    sums, log_evidence = pl.pallas_call(
        functools.partial(sums_kernel, edge, parts, total, groups),
        out_shape=(array((owned, h, wide), f32), array((1, 1), f32)),
        in_specs=[in_vmem()] * 3 + [anywhere()] * len(pieces),
        out_specs=(anywhere(), in_vmem()),
        scratch_shapes=[
            pltpu.VMEM((owned, h, wide), f32),
            pltpu.SemaphoreType.DMA((4,)),
            pltpu.SemaphoreType.DMA((len(pieces),)),
            pltpu.VMEM((groups, total, span), f32),
            pltpu.VMEM((ROWS // h * groups * parts * ROWS // LANES, len(FLAT) * owned * h, LANES), f32),
            pltpu.VMEM((max(every // LANES, 1), owned * h, LANES), f32),
            pltpu.VMEM((len(FLAT) * owned * h, wide), f32),
            pltpu.VMEM((groups * parts * ROWS, core_lanes), bf16),
            pltpu.VMEM((every, wide), bf16),
        ],
        compiler_params=params,
        name="sums",
    )(logits, spread, got, *pieces)
    return (sums, log_evidence.reshape(1))


def solution(mesh):
    return jax.shard_map(
        per_device,
        mesh=mesh,
        in_specs=(P(("ref", "dp"), None, None), P(None, "dp", None), P(), P(("ref", "dp"), None)),
        out_specs=(P("ref", "dp", None), P(("ref", "dp"))),
        check_vma=False,
    )
```

time: 63.4 us -> 60.6 us (0.956)
  waiting for transfers between devices: 27.4 us -> 25.3 us
    ppermute x1, waiting for transfers between devices: 19.4 us -> 17.2 us  [per_device(): lax.ppermute(references, 'dp', [(i, parts - 1 - i) for i in range(parts)])]
    pallas_call x4 -> x5, Pallas kernels: 6.36 us -> 5.6 us  [the longest x1 3.83 us: per_device(): pl.pallas_call(functools.partial(logits_kernel, edge, parts, total), out_...]
    all_to_all x1, starting transfers between devices: 6.86 us -> 6.1 us  [per_device(): logits = lax.all_to_all(partial, ('ref', 'dp'), 0, 0, tiled=True)]
    ppermute x2 -> x3, starting transfers between devices: 1.9 us -> 2.52 us  [the longest x1 1.83 us: per_device(): lax.ppermute(outside, 'ref', step)]
    ppermute x2 -> x3, waiting for transfers between devices: 5.53 us -> 5.67 us  [the longest x1 5.66 us: per_device(): lax.ppermute(outside, 'ref', step)]
  transfers between devices with their start and end apart: 6 -> 7, of which waited for: 3 -> 3; matrix products, arithmetic and copies ran while one was open for 0% -> 0% of each run, Pallas kernels for 10% -> 9%
where the time goes in v4:
time: 60.6 us; the launch traced here: 60.3 us
  waiting for transfers between devices  25.3 us (42%)
  starting transfers between devices  22.2 us (37%)
  Pallas kernels  12 us (20%)
  between operations  0.73 us (1%)
    ppermute x1, waiting for transfers between devices, per_device(): lax.ppermute(references, 'dp', [(i, parts - 1 - i) for i in range(parts)])  17.2 us
    all_to_all x1, starting transfers between devices, per_device(): got = lax.all_to_all(sent, 'dp', 0, 0, tiled=True)  7.53 us
    all_to_all x1, starting transfers between devices, per_device(): logits = lax.all_to_all(partial, ('ref', 'dp'), 0, 0, tiled=True)  6.1 us
    ppermute x1, waiting for transfers between devices, per_device(): lax.ppermute(outside, 'ref', step)  5.66 us
    ppermute x1, starting transfers between devices, per_device(): lax.ppermute(references, 'dp', [(i, parts - 1 - i) for i in range(parts)])  4.44 us
    pallas_call x1, Pallas kernels, per_device(): pl.pallas_call(functools.partial(logits_kernel, edge, parts, total), out_...  3.83 us
    pallas_call x1, Pallas kernels, per_device(): pl.pallas_call(functools.partial(sums_kernel, edge, parts, total, groups)...  3.63 us
    pallas_call x1, Pallas kernels, per_device(): pl.pallas_call(functools.partial(pack_kernel, edge, parts), out_shape=(ar...  2.77 us
  transfers between devices with their start and end apart: 7, of which 3 were waited for; matrix products, arithmetic and copies ran while one was open for 0% of the time, Pallas kernels for 9%

profile of v4, /device:TPU:0, one launch (start us, length us, event | category | flops | bytes accessed | tf_op | source)
XLA Modules:
  0.0 60.3 jit_solution(17484440953286050352)
XLA Ops:
  0.6 2.8 %pack.1 = (bf16[128,3584]{1,0:T(8,128)(2,1)}, bf16[16,4096]{1,0:T(8,128)(2,1)}) custom-call(bf16[64,4096]{1,0:T(8,128)(2,1)} %bitcast.11, bf16[2,4,4096]{2,1,0:T(4,128)(2,1)} %refs_hbm.1), custom_call_target="tpu_custom_call" | custom-call | tf_op jit(solution)/shard_map/pack/pallas_call | solution.py:516
  3.4 0.0 copy-start.2
  3.4 0.0 copy-start
  3.4 7.5 %all-to-all-start = ((bf16[16,8,3584]{2,1,0:T(8,128)(2,1)}), bf16[16,8,3584]{2,1,0:T(8,128)(2,1)S(1)}, u32[]{:S(2)}, u32[]{:S(2)}) async-start(bf16[16,8,3584]{2,1,0:T(8,128)(2,1)} %bitcast.10), calls=%async_computation | async-start | bytes 1835008 | tf_op jit(solution)/shard_map/all_to_all | solution.py:541
  11.0 0.0 copy-done.2
  11.0 4.4 %collective-permute-start = (bf16[2,4,4096]{2,1,0:T(4,128)(2,1)S(1)}, bf16[2,4,4096]{2,1,0:T(4,128)(2,1)S(1)}, u32[]{:S(2)}, u32[]{:S(2)}) collective-permute-start(bf16[2,4,4096]{2,1,0:T(4,128)(2,1)S(1)} %copy-done.2), channel_id=1, source_target_pairs={{0,15},{1,14},{2,13},{3,12},{4,11},{5,10},{6,9},{7,8},{8,7},{9,6},... | collective-permute-start | bytes 196616 | tf_op jit(solution)/shard_map/ppermute | solution.py:515
  15.4 0.0 copy-done
  15.5 17.2 %collective-permute-done.far_ref = bf16[2,4,4096]{2,1,0:T(4,128)(2,1)S(1)} collective-permute-done((bf16[2,4,4096]{2,1,0:T(4,128)(2,1)S(1)}, bf16[2,4,4096]{2,1,0:T(4,128)(2,1)S(1)}, u32[]{:S(2)}, u32[]{:S(2)}) %collective-permute-start) | collective-permute-done | bytes 65568 | tf_op jit(solution)/shard_map/ppermute | solution.py:515
  32.7 0.0 all-to-all-done
  32.7 0.0 copy-start.3
  32.7 0.4 trim.1
  33.1 1.6 %collective-permute-start.2 = (bf16[128,2048]{1,0:T(8,128)(2,1)S(1)}, bf16[128,2048]{1,0:T(8,128)(2,1)S(1)}, u32[]{:S(2)}, u32[]{:S(2)}) collective-permute-start(bf16[128,2048]{1,0:T(8,128)(2,1)S(1)} %get-tuple-element.30), channel_id=1, source_target_pairs={{0,16},{16,0},{1,17},{17,1},{2,18},{18,2},{3,19},{19,3},{4,20},{20... | collective-permute-start | bytes 1572872 | tf_op jit(solution)/shard_map/ppermute | solution.py:555
  34.7 0.0 copy-start.1
  34.7 0.6 %collective-permute-start.1 = (bf16[16,4096]{1,0:T(8,128)(2,1)S(1)}, bf16[16,4096]{1,0:T(8,128)(2,1)S(1)}, u32[]{:S(2)}, u32[]{:S(2)}) collective-permute-start(bf16[16,4096]{1,0:T(8,128)(2,1)S(1)} %get-tuple-element.28), channel_id=1, source_target_pairs={{0,1},{1,0},{2,3},{3,2},{4,5},{5,4},{6,7},{7,6},{8,9},{9,8},{10,11... | collective-permute-start | bytes 393224 | tf_op jit(solution)/shard_map/ppermute | solution.py:553
  35.3 0.0 copy-done.3
  35.3 0.1 copy.6.orient_any
  35.4 0.0 copy-done.1
  35.4 3.8 %logits.1 = (f32[16,128]{1,0:T(8,128)S(1)}, bf16[64,4096]{1,0:T(8,128)(2,1)S(1)}, f32[16,128]{1,0:T(8,128)S(1)}) custom-call(s32[16,6]{1,0:T(8,128)S(1)} %copy.6.orient_any, s32[1,2]{1,0:T(1,128)S(1)} %copy-done.1, bf16[128,3584]{1,0:T(8,128)(2,1)S(1)} %bitcast.7, f32[128,8,128]{2,1,0:T(8,128)S(1)} %own.1.own_ref, ...), custom_call_target="tpu_custom_call" | custom-call | tf_op jit(solution)/shard_map/logits/pallas_call | solution.py:556
  39.2 0.0 collective-permute-done.1.inner_ref.refs_1_
  39.2 1.1 %finish.1 = f32[512,128]{1,0:T(8,128)} custom-call(f32[16,128]{1,0:T(8,128)S(1)} %get-tuple-element.24.part_ref, bf16[64,4096]{1,0:T(8,128)(2,1)S(1)} %get-tuple-element.25.base_ref, f32[16,128]{1,0:T(8,128)S(1)} %get-tuple-element.26.bar_ref, bf16[16,4096]{1,0:T(8,128)(2,1)S(1)} %get-tuple-element.32.outer_ref.refs_0_, ...), custom_call_target="tpu_custom_call" | custom-call | tf_op jit(solution)/shard_map/finish/pallas_call | solution.py:576
  40.3 6.1 %all-to-all-start.1 = ((f32[32,16,128]{2,1,0:T(8,128)}), f32[32,16,128]{2,1,0:T(8,128)S(1)}, u32[]{:S(2)}, u32[]{:S(2)}) async-start(f32[32,16,128]{2,1,0:T(8,128)} %bitcast.3), calls=%async_computation.1 | async-start | bytes 524288 | tf_op jit(solution)/shard_map/all_to_all | solution.py:586
  46.4 1.8 %collective-permute-start.3 = (bf16[16,4096]{1,0:T(8,128)(2,1)S(1)}, bf16[16,4096]{1,0:T(8,128)(2,1)S(1)}, u32[]{:S(2)}, u32[]{:S(2)}) collective-permute-start(bf16[16,4096]{1,0:T(8,128)(2,1)S(1)} %get-tuple-element.32.outer_ref.refs_0_), channel_id=1, source_target_pairs={{0,16},{16,0},{1,17},{17,1},{2,18},{18,2},{3,19},{19,3},{4,20},{20... | collective-permute-start | bytes 393224 | tf_op jit(solution)/shard_map/ppermute | solution.py:600
  48.2 0.0 collective-permute-done.2.core_ref.refs_2_
  48.2 0.3 far_ends.1
  48.5 0.1 collective-permute-start.4
  48.6 5.7 %collective-permute-done.3.refs_3_ = bf16[16,4096]{1,0:T(8,128)(2,1)S(1)} collective-permute-done((bf16[16,4096]{1,0:T(8,128)(2,1)S(1)}, bf16[16,4096]{1,0:T(8,128)(2,1)S(1)}, u32[]{:S(2)}, u32[]{:S(2)}) %collective-permute-start.3) | collective-permute-done | bytes 131104 | tf_op jit(solution)/shard_map/ppermute | solution.py:600
  54.3 2.4 %all-to-all-done.1 = f32[32,16,128]{2,1,0:T(8,128)S(1)} async-done(((f32[32,16,128]{2,1,0:T(8,128)}), f32[32,16,128]{2,1,0:T(8,128)S(1)}, u32[]{:S(2)}, u32[]{:S(2)}) %all-to-all-start.1) | async-done | bytes 262176 | tf_op jit(solution)/shard_map/all_to_all | solution.py:586
  56.7 0.0 collective-permute-done.4.refs_4_
  56.7 3.6 %sums.1 = (f32[8,4,4096]{2,1,0:T(4,128)}, f32[1,1]{1,0:T(1,128)}) custom-call(f32[512,128]{1,0:T(8,128)S(1)} %bitcast.9, bf16[128,896]{1,0:T(8,128)(2,1)S(1)} %get-tuple-element.31.spread_ref, bf16[128,3584]{1,0:T(8,128)(2,1)S(1)} %bitcast.8, bf16[16,4096]{1,0:T(8,128)(2,1)S(1)} %get-tuple-element.32.outer_ref.refs_0_, ...), custom_call_target="tpu_custom_call" | custom-call | tf_op jit(solution)/shard_map/sums/pallas_call | solution.py:603
  (1 shorter events, 0.0 us)
Async XLA Ops:
  3.4 7.6 %copy-start.2 = (bf16[2,4,4096]{2,1,0:T(4,128)(2,1)S(1)}, bf16[2,4,4096]{2,1,0:T(4,128)(2,1)}, u32[]{:S(2)}) copy-start(bf16[2,4,4096]{2,1,0:T(4,128)(2,1)} %refs_hbm.1) | copy-start | bytes 196612
  3.4 12.0 %copy-start = (bf16[16,4096]{1,0:T(8,128)(2,1)S(1)}, bf16[16,4096]{1,0:T(8,128)(2,1)}, u32[]{:S(2)}) copy-start(bf16[16,4096]{1,0:T(8,128)(2,1)} %get-tuple-element.20.both_ref) | copy-start | bytes 393220
  3.4 29.3 %all-to-all-start = ((bf16[16,8,3584]{2,1,0:T(8,128)(2,1)}), bf16[16,8,3584]{2,1,0:T(8,128)(2,1)S(1)}, u32[]{:S(2)}, u32[]{:S(2)}) async-start(bf16[16,8,3584]{2,1,0:T(8,128)(2,1)} %bitcast.10), calls=%async_computation | async-start | bytes 1835008 | tf_op jit(solution)/shard_map/all_to_all | solution.py:541
  11.0 21.7 %collective-permute-start = (bf16[2,4,4096]{2,1,0:T(4,128)(2,1)S(1)}, bf16[2,4,4096]{2,1,0:T(4,128)(2,1)S(1)}, u32[]{:S(2)}, u32[]{:S(2)}) collective-permute-start(bf16[2,4,4096]{2,1,0:T(4,128)(2,1)S(1)} %copy-done.2), channel_id=1, source_target_pairs={{0,15},{1,14},{2,13},{3,12},{4,11},{5,10},{6,9},{7,8},{8,7},{9,6},... | collective-permute-start | bytes 196616 | tf_op jit(solution)/shard_map/ppermute | solution.py:515
  32.7 2.6 %copy-start.3 = (s32[16,6]{0,1:T(8,128)S(1)}, s32[16,6]{0,1:T(8,128)}, u32[]{:S(2)}) copy-start(s32[16,6]{0,1:T(8,128)} %param.6) | copy-start | bytes 1156
  33.1 15.1 %collective-permute-start.2 = (bf16[128,2048]{1,0:T(8,128)(2,1)S(1)}, bf16[128,2048]{1,0:T(8,128)(2,1)S(1)}, u32[]{:S(2)}, u32[]{:S(2)}) collective-permute-start(bf16[128,2048]{1,0:T(8,128)(2,1)S(1)} %get-tuple-element.30), channel_id=1, source_target_pairs={{0,16},{16,0},{1,17},{17,1},{2,18},{18,2},{3,19},{19,3},{4,20},{20... | collective-permute-start | bytes 1572872 | tf_op jit(solution)/shard_map/ppermute | solution.py:555
  34.7 0.7 %copy-start.1 = (s32[1,2]{1,0:T(1,128)S(1)}, s32[1,2]{1,0:T(1,128)}, u32[]{:S(2)}) copy-start(s32[1,2]{1,0:T(1,128)} %allowed_any.1) | copy-start | bytes 28
  34.7 4.5 %collective-permute-start.1 = (bf16[16,4096]{1,0:T(8,128)(2,1)S(1)}, bf16[16,4096]{1,0:T(8,128)(2,1)S(1)}, u32[]{:S(2)}, u32[]{:S(2)}) collective-permute-start(bf16[16,4096]{1,0:T(8,128)(2,1)S(1)} %get-tuple-element.28), channel_id=1, source_target_pairs={{0,1},{1,0},{2,3},{3,2},{4,5},{5,4},{6,7},{7,6},{8,9},{9,8},{10,11... | collective-permute-start | bytes 393224 | tf_op jit(solution)/shard_map/ppermute | solution.py:553
  40.3 16.4 %all-to-all-start.1 = ((f32[32,16,128]{2,1,0:T(8,128)}), f32[32,16,128]{2,1,0:T(8,128)S(1)}, u32[]{:S(2)}, u32[]{:S(2)}) async-start(f32[32,16,128]{2,1,0:T(8,128)} %bitcast.3), calls=%async_computation.1 | async-start | bytes 524288 | tf_op jit(solution)/shard_map/all_to_all | solution.py:586
  46.4 7.9 %collective-permute-start.3 = (bf16[16,4096]{1,0:T(8,128)(2,1)S(1)}, bf16[16,4096]{1,0:T(8,128)(2,1)S(1)}, u32[]{:S(2)}, u32[]{:S(2)}) collective-permute-start(bf16[16,4096]{1,0:T(8,128)(2,1)S(1)} %get-tuple-element.32.outer_ref.refs_0_), channel_id=1, source_target_pairs={{0,16},{16,0},{1,17},{17,1},{2,18},{18,2},{3,19},{19,3},{4,20},{20... | collective-permute-start | bytes 393224 | tf_op jit(solution)/shard_map/ppermute | solution.py:600
  48.5 8.2 %collective-permute-start.4 = (bf16[16,4096]{1,0:T(8,128)(2,1)S(1)}, bf16[16,4096]{1,0:T(8,128)(2,1)S(1)}, u32[]{:S(2)}, u32[]{:S(2)}) collective-permute-start(bf16[16,4096]{1,0:T(8,128)(2,1)S(1)} %get-tuple-element.33), channel_id=1, source_target_pairs={{0,1},{1,0},{2,3},{3,2},{4,5},{5,4},{6,7},{7,6},{8,9},{9,8},{10,11... | collective-permute-start | bytes 393224 | tf_op jit(solution)/shard_map/ppermute | solution.py:600

commit v5 on v4

--- a/solution.py
+++ b/solution.py
@@ -49,15 +49,27 @@
 
 
 def turn_rows(edge, planes, x, z, flat, turned):
-    low = lane_iota((planes, LANES)) < edge
+    lay_rows(edge, planes, x, flat)
+    turn_planes(edge, planes, flat, turned)
+    gather_rows(edge, planes, turned, z)
+
+
+def lay_rows(edge, planes, x, flat):
     for m in range(edge // 2):
         piece = x[:planes, tile(m)]
         flat[pl.ds(2 * m, planes, stride=edge), :] = piece
         flat[pl.ds(2 * m + 1, planes, stride=edge), :] = swap_halves(piece)
+
+
+def turn_planes(edge, planes, flat, turned):
     for n in range(0, planes, 2):
         block = flat[n * edge : (n + 2) * edge, :].T[:edge, :]
         turned[n * edge : (n + 1) * edge, :] = block
         turned[(n + 1) * edge : (n + 2) * edge, :] = swap_halves(block)
+
+
+def gather_rows(edge, planes, turned, z):
+    low = lane_iota((planes, LANES)) < edge
     for m in range(edge // 2):
         even = turned[pl.ds(2 * m, planes, stride=edge), :]
         odd = turned[pl.ds(2 * m + 1, planes, stride=edge), :]
@@ -129,7 +141,7 @@
 
 def logits_kernel(
     edge, parts, total, orient_any, allowed_any, got_ref, own_ref, far_ref, out_ref, base_ref, bar_ref,
-    orient_ref, allowed_ref, sems, x, z, far_flat, far_turned, wide_f32, flat, turned, kinds, shifted, gram,
+    orient_ref, allowed_ref, sems, x, z, far_flat, far_turned, wide_f32, flats, turneds, kinds, shifted, gram,
 ):
     h = edge // parts
     wide = edge * edge
@@ -167,11 +179,9 @@
         far = far_ref[c].astype(jnp.float32)
         for l in range(h):
             x[c * h + l : c * h + l + 1, :] = far[h - 1 - l : h - l, :]
-    turn_rows(edge, planes, x, z, far_flat, far_turned)
-    for m in range(columns):
-        keep(2, 3, x[:planes, tile(m)], m)
-        keep(6, 7, z[:planes, tile(m)], m)
+    lay_rows(edge, planes, x, far_flat)
     for axis in (1, 2):
+        flat = flats.at[axis - 1]
         for c in range(2):
             for jl in range(h):
                 first = (axis - 1) * 2 * h * edge // LANES
@@ -186,12 +196,21 @@
                         else:
                             value = swap_halves(jnp.where(low, mirrored, plain))
                         flat[pl.ds((c * h + l) * edge + s * h + jl, ROWS, stride=h), :] = value
+    turn_planes(edge, planes, far_flat, far_turned)
+    for axis in (1, 2):
+        flat, turned = flats.at[axis - 1], turneds.at[axis - 1]
         for l in range(h):
             block = jnp.concatenate(
                 [flat[(c * h + l) * edge : (c * h + l + 1) * edge, :] for c in range(2)], axis=0
             ).T
             for side in range(2):
                 turned[(side * h + l) * edge : (side * h + l + 1) * edge, :] = block[side * edge : (side + 1) * edge, :]
+    gather_rows(edge, planes, far_turned, z)
+    for m in range(columns):
+        keep(2, 3, x[:planes, tile(m)], m)
+        keep(6, 7, z[:planes, tile(m)], m)
+    for axis in (1, 2):
+        flat, turned = flats.at[axis - 1], turneds.at[axis - 1]
         part = lane_iota((planes, LANES)) < edge
         for m in range(edge // 2):
             even = flat[pl.ds(2 * m, planes, stride=edge), :]
@@ -234,29 +253,40 @@
             found.append([pick_lanes(value, way) for way in index[b]])
         return [list(way) for way in zip(*found, strict=True)]
 
-    behind = column(columns - 1)[1]
+    many = parts * ROWS
+    fraction = lane_iota((len(FLAT) * rows, many)) % ROWS // h
+    blocks = []
+
+    def put(number, j, result):
+        at = j % columns
+        shifted[number * rows : (number + 1) * rows, tile(at)] = result
+        if number == 0:
+            base_ref[:, tile(at)] = result
+
+    def joined(result):
+        return jnp.concatenate(result, axis=0).astype(jnp.bfloat16)
+
+    def between(first, second):
+        return joined([jnp.where(lows, x, y) for x, y in zip(first[1], second[1], strict=True)])
+
     here = column(0)
+    put(1, 0, between(column(columns - 1), here))
     for j in range(columns):
         ahead = column((j + 1) % columns)
-        results = [
-            here[0],
-            [jnp.where(lows, x, y) for x, y in zip(behind, here[1], strict=True)],
-            [jnp.where(lows, x, y) for x, y in zip(here[1], ahead[1], strict=True)],
-            here[2],
-            here[3],
-        ]
-        for number, result in enumerate(results):
-            result = jnp.concatenate(result, axis=0).astype(jnp.bfloat16)
-            shifted[number * rows : (number + 1) * rows, tile(j)] = result
-            if number == 0:
-                base_ref[:, tile(j)] = result
-        behind, here = here[1], ahead
-    many = parts * ROWS
-    fraction = lane_iota((len(FLAT) * rows, many)) % ROWS // h
-    found = None
-    for f in range(ROWS // h):
-        block = rows_by_rows(shifted[:, f * core : (f + 1) * core], got_ref[:, :core])
-        found = block if found is None else jnp.where(fraction == f, block, found)
+        put(0, j, joined(here[0]))
+        put(3, j, joined(here[2]))
+        put(4, j, joined(here[3]))
+        middle = between(here, ahead)
+        put(2, j, middle)
+        if j + 1 < columns:
+            put(1, j + 1, middle)
+        here = ahead
+        f, rest = divmod((j + 1) * LANES, core)
+        if rest == 0:
+            blocks.append(rows_by_rows(shifted[:, (f - 1) * core : f * core], got_ref[:, :core]))
+    found = blocks[0]
+    for f in range(1, ROWS // h):
+        found = jnp.where(fraction == f, blocks[f], found)
     gram[...] = found
     place = lane_iota((total, many)) % h
     kept = []
@@ -362,7 +392,7 @@
 
 def sums_kernel(edge, parts, total, groups, logits_ref, spread_ref, got_ref, *refs):
     pieces, refs = refs[: 3 * groups - 1], refs[3 * groups - 1 :]
-    out_hbm, log_ref, out_ref, sems, in_sems, chances, weights, end_weights, table, merged, ends = refs
+    out_hbm, log_ref, out_ref, sems, chances, weights, end_weights, table, extra, merged, ends = refs
     h = edge // parts
     wide = edge * edge
     columns = wide // LANES
@@ -372,17 +402,14 @@
     many = parts * ROWS
     core, _, _ = lanes_of(edge, parts)
     mine, me = lax.axis_index("ref"), lax.axis_index("dp")
-    incoming = []
     at_core, at_end = many, 0
-    for number, piece in enumerate(pieces):
+    for piece in pieces:
         if piece.shape[0] == many:
-            target = merged.at[pl.ds(at_core, many)]
+            merged[at_core : at_core + many, :] = piece[...]
             at_core += many
         else:
-            target = ends.at[pl.ds(at_end, parts)]
+            ends[at_end : at_end + parts, :] = piece[...]
             at_end += parts
-        incoming.append(pltpu.make_async_copy(piece, target, in_sems.at[number]))
-        incoming[-1].start()
     merged[:many, :] = got_ref[:, :core]
     dot = functools.partial(jnp.dot, preferred_element_type=jnp.float32)
     lane = lane_iota((total, span))
@@ -442,14 +469,12 @@
             value = jnp.concatenate([value, jnp.zeros((owned, LANES - every), jnp.float32)], axis=1)
         for m in range(end_weights.shape[0]):
             end_weights[m, pl.ds(l, owned, stride=h), :] = value[:, tile(m)]
-    for copy in incoming:
-        copy.wait()
     count = groups * (many // LANES)
     for f in range(ROWS // h):
         both = jnp.concatenate([weights[f * count + m] for m in range(count)], axis=1).astype(jnp.bfloat16)
         table[:, f * core : (f + 1) * core] = dot(both, merged[...])
     both = jnp.concatenate([end_weights[m] for m in range(end_weights.shape[0])], axis=1)[:, :every]
-    table[:rows, :] += dot(both.astype(jnp.bfloat16), ends[...])
+    extra[...] = dot(both.astype(jnp.bfloat16), ends[...])
     lane = lane_iota((rows, LANES))
     low = lane < edge
     after = (lane // edge) * edge + (lane + 1) % edge
@@ -460,13 +485,10 @@
 
     pieces = sems.shape[0]
     copies = []
-    up = swap_halves(cut(1, 0))
-    down = swap_halves(cut(2, columns - 1))
     for j in range(columns):
-        up_next, down_next = swap_halves(cut(1, j + 1)), swap_halves(cut(2, j))
-        value = cut(0, j) + jnp.where(low, up, up_next) + jnp.where(low, down, down_next)
+        turned = swap_halves(jnp.where(low, cut(1, j + 1) + cut(2, j), cut(1, j) + cut(2, j - 1)))
+        value = cut(0, j) + extra[:, tile(j)] + turned
         value = value + pick_lanes(cut(3, j), after) + pick_lanes(cut(4, j), before)
-        up, down = up_next, down_next
         for o in range(owned):
             out_ref[o, :, tile(j)] = value[o * h : (o + 1) * h, :]
         if (j + 1) % (columns // pieces) == 0:
@@ -564,8 +586,8 @@
             pltpu.SemaphoreType.DMA((2,)),
             *turning,
             pltpu.VMEM((extra // LANES, parts * ROWS, LANES), f32),
-            pltpu.VMEM((planes * edge, LANES), f32),
-            pltpu.VMEM((planes * edge, LANES), f32),
+            pltpu.VMEM((2, planes * edge, LANES), f32),
+            pltpu.VMEM((2, planes * edge, LANES), f32),
             pltpu.VMEM((24 * wide // LANES, ROWS, LANES), f32),
             pltpu.VMEM((len(FLAT) * rows, wide), bf16),
             pltpu.VMEM((len(FLAT) * rows, parts * ROWS), f32),
@@ -603,16 +625,16 @@
     sums, log_evidence = pl.pallas_call(
         functools.partial(sums_kernel, edge, parts, total, groups),
         out_shape=(array((owned, h, wide), f32), array((1, 1), f32)),
-        in_specs=[in_vmem()] * 3 + [anywhere()] * len(pieces),
+        in_specs=[in_vmem()] * (3 + len(pieces)),
         out_specs=(anywhere(), in_vmem()),
         scratch_shapes=[
             pltpu.VMEM((owned, h, wide), f32),
-            pltpu.SemaphoreType.DMA((4,)),
-            pltpu.SemaphoreType.DMA((len(pieces),)),
+            pltpu.SemaphoreType.DMA((8,)),
             pltpu.VMEM((groups, total, span), f32),
             pltpu.VMEM((ROWS // h * groups * parts * ROWS // LANES, len(FLAT) * owned * h, LANES), f32),
             pltpu.VMEM((max(every // LANES, 1), owned * h, LANES), f32),
             pltpu.VMEM((len(FLAT) * owned * h, wide), f32),
+            pltpu.VMEM((owned * h, wide), f32),
             pltpu.VMEM((groups * parts * ROWS, core_lanes), bf16),
             pltpu.VMEM((every, wide), bf16),
         ],

time: 60.6 us -> 59.5 us (0.982)
  Pallas kernels: 12 us -> 10.9 us
    pallas_call x1, Pallas kernels: 3.63 us -> 2.72 us  [per_device(): pl.pallas_call(functools.partial(sums_kernel, edge, parts, total, groups)...]
where the time goes in v5:
time: 59.5 us; the launch traced here: 59.2 us
  waiting for transfers between devices  25.3 us (43%)
  starting transfers between devices  22.2 us (37%)
  Pallas kernels  10.9 us (18%)
  between operations  0.73 us (1%)
    ppermute x1, waiting for transfers between devices, per_device(): lax.ppermute(references, 'dp', [(i, parts - 1 - i) for i in range(parts)])  17.2 us
    all_to_all x1, starting transfers between devices, per_device(): got = lax.all_to_all(sent, 'dp', 0, 0, tiled=True)  7.53 us
    all_to_all x1, starting transfers between devices, per_device(): logits = lax.all_to_all(partial, ('ref', 'dp'), 0, 0, tiled=True)  6.1 us
    ppermute x1, waiting for transfers between devices, per_device(): lax.ppermute(outside, 'ref', step)  5.66 us
    ppermute x1, starting transfers between devices, per_device(): lax.ppermute(references, 'dp', [(i, parts - 1 - i) for i in range(parts)])  4.44 us
    pallas_call x1, Pallas kernels, per_device(): pl.pallas_call(functools.partial(logits_kernel, edge, parts, total), out_...  3.67 us
    pallas_call x1, Pallas kernels, per_device(): pl.pallas_call(functools.partial(pack_kernel, edge, parts), out_shape=(ar...  2.77 us
    pallas_call x1, Pallas kernels, per_device(): pl.pallas_call(functools.partial(sums_kernel, edge, parts, total, groups)...  2.72 us
  transfers between devices with their start and end apart: 7, of which 3 were waited for; matrix products, arithmetic and copies ran while one was open for 0% of the time, Pallas kernels for 9%

profile of v5, /device:TPU:0, one launch (start us, length us, event | category | flops | bytes accessed | tf_op | source)
XLA Modules:
  0.0 59.2 jit_solution(956827502579385633)
XLA Ops:
  0.6 2.8 %pack.1 = (bf16[128,3584]{1,0:T(8,128)(2,1)}, bf16[16,4096]{1,0:T(8,128)(2,1)}) custom-call(bf16[64,4096]{1,0:T(8,128)(2,1)} %bitcast.11, bf16[2,4,4096]{2,1,0:T(4,128)(2,1)} %refs_hbm.1), custom_call_target="tpu_custom_call" | custom-call | tf_op jit(solution)/shard_map/pack/pallas_call | solution.py:538
  3.4 0.0 copy-start.2
  3.4 0.0 copy-start
  3.4 7.5 %all-to-all-start = ((bf16[16,8,3584]{2,1,0:T(8,128)(2,1)}), bf16[16,8,3584]{2,1,0:T(8,128)(2,1)S(1)}, u32[]{:S(2)}, u32[]{:S(2)}) async-start(bf16[16,8,3584]{2,1,0:T(8,128)(2,1)} %bitcast.10), calls=%async_computation | async-start | bytes 1835008 | tf_op jit(solution)/shard_map/all_to_all | solution.py:563
  11.0 0.0 copy-done.2
  11.0 4.4 %collective-permute-start = (bf16[2,4,4096]{2,1,0:T(4,128)(2,1)S(1)}, bf16[2,4,4096]{2,1,0:T(4,128)(2,1)S(1)}, u32[]{:S(2)}, u32[]{:S(2)}) collective-permute-start(bf16[2,4,4096]{2,1,0:T(4,128)(2,1)S(1)} %copy-done.2), channel_id=1, source_target_pairs={{0,15},{1,14},{2,13},{3,12},{4,11},{5,10},{6,9},{7,8},{8,7},{9,6},... | collective-permute-start | bytes 196616 | tf_op jit(solution)/shard_map/ppermute | solution.py:537
  15.4 0.0 copy-done
  15.5 17.2 %collective-permute-done.far_ref = bf16[2,4,4096]{2,1,0:T(4,128)(2,1)S(1)} collective-permute-done((bf16[2,4,4096]{2,1,0:T(4,128)(2,1)S(1)}, bf16[2,4,4096]{2,1,0:T(4,128)(2,1)S(1)}, u32[]{:S(2)}, u32[]{:S(2)}) %collective-permute-start) | collective-permute-done | bytes 65568 | tf_op jit(solution)/shard_map/ppermute | solution.py:537
  32.7 0.0 all-to-all-done
  32.7 0.0 copy-start.3
  32.7 0.4 trim.1
  33.1 1.6 %collective-permute-start.2 = (bf16[128,2048]{1,0:T(8,128)(2,1)S(1)}, bf16[128,2048]{1,0:T(8,128)(2,1)S(1)}, u32[]{:S(2)}, u32[]{:S(2)}) collective-permute-start(bf16[128,2048]{1,0:T(8,128)(2,1)S(1)} %get-tuple-element.30), channel_id=1, source_target_pairs={{0,16},{16,0},{1,17},{17,1},{2,18},{18,2},{3,19},{19,3},{4,20},{20... | collective-permute-start | bytes 1572872 | tf_op jit(solution)/shard_map/ppermute | solution.py:577
  34.7 0.0 copy-start.1
  34.7 0.6 %collective-permute-start.1 = (bf16[16,4096]{1,0:T(8,128)(2,1)S(1)}, bf16[16,4096]{1,0:T(8,128)(2,1)S(1)}, u32[]{:S(2)}, u32[]{:S(2)}) collective-permute-start(bf16[16,4096]{1,0:T(8,128)(2,1)S(1)} %get-tuple-element.28), channel_id=1, source_target_pairs={{0,1},{1,0},{2,3},{3,2},{4,5},{5,4},{6,7},{7,6},{8,9},{9,8},{10,11... | collective-permute-start | bytes 393224 | tf_op jit(solution)/shard_map/ppermute | solution.py:575
  35.3 0.0 copy-done.3
  35.3 0.1 copy.6.orient_any
  35.4 0.0 copy-done.1
  35.4 3.7 %logits.1 = (f32[16,128]{1,0:T(8,128)S(1)}, bf16[64,4096]{1,0:T(8,128)(2,1)S(1)}, f32[16,128]{1,0:T(8,128)S(1)}) custom-call(s32[16,6]{1,0:T(8,128)S(1)} %copy.6.orient_any, s32[1,2]{1,0:T(1,128)S(1)} %copy-done.1, bf16[128,3584]{1,0:T(8,128)(2,1)S(1)} %bitcast.7, f32[128,8,128]{2,1,0:T(8,128)S(1)} %own.1.own_ref, ...), custom_call_target="tpu_custom_call" | custom-call | tf_op jit(solution)/shard_map/logits/pallas_call | solution.py:578
  39.0 0.0 collective-permute-done.1.inner_ref.refs_1_
  39.0 1.1 %finish.1 = f32[512,128]{1,0:T(8,128)} custom-call(f32[16,128]{1,0:T(8,128)S(1)} %get-tuple-element.24.part_ref, bf16[64,4096]{1,0:T(8,128)(2,1)S(1)} %get-tuple-element.25.base_ref, f32[16,128]{1,0:T(8,128)S(1)} %get-tuple-element.26.bar_ref, bf16[16,4096]{1,0:T(8,128)(2,1)S(1)} %get-tuple-element.32.outer_ref.refs_0_, ...), custom_call_target="tpu_custom_call" | custom-call | tf_op jit(solution)/shard_map/finish/pallas_call | solution.py:598
  40.1 6.1 %all-to-all-start.1 = ((f32[32,16,128]{2,1,0:T(8,128)}), f32[32,16,128]{2,1,0:T(8,128)S(1)}, u32[]{:S(2)}, u32[]{:S(2)}) async-start(f32[32,16,128]{2,1,0:T(8,128)} %bitcast.3), calls=%async_computation.1 | async-start | bytes 524288 | tf_op jit(solution)/shard_map/all_to_all | solution.py:608
  46.2 1.8 %collective-permute-start.3 = (bf16[16,4096]{1,0:T(8,128)(2,1)S(1)}, bf16[16,4096]{1,0:T(8,128)(2,1)S(1)}, u32[]{:S(2)}, u32[]{:S(2)}) collective-permute-start(bf16[16,4096]{1,0:T(8,128)(2,1)S(1)} %get-tuple-element.32.outer_ref.refs_0_), channel_id=1, source_target_pairs={{0,16},{16,0},{1,17},{17,1},{2,18},{18,2},{3,19},{19,3},{4,20},{20... | collective-permute-start | bytes 393224 | tf_op jit(solution)/shard_map/ppermute | solution.py:622
  48.1 0.0 collective-permute-done.2.core_ref.refs_2_
  48.1 0.3 far_ends.1
  48.4 0.1 collective-permute-start.4
  48.4 5.7 %collective-permute-done.3.refs_3_ = bf16[16,4096]{1,0:T(8,128)(2,1)S(1)} collective-permute-done((bf16[16,4096]{1,0:T(8,128)(2,1)S(1)}, bf16[16,4096]{1,0:T(8,128)(2,1)S(1)}, u32[]{:S(2)}, u32[]{:S(2)}) %collective-permute-start.3) | collective-permute-done | bytes 131104 | tf_op jit(solution)/shard_map/ppermute | solution.py:622
  54.1 2.4 %all-to-all-done.1 = f32[32,16,128]{2,1,0:T(8,128)S(1)} async-done(((f32[32,16,128]{2,1,0:T(8,128)}), f32[32,16,128]{2,1,0:T(8,128)S(1)}, u32[]{:S(2)}, u32[]{:S(2)}) %all-to-all-start.1) | async-done | bytes 262176 | tf_op jit(solution)/shard_map/all_to_all | solution.py:608
  56.5 0.0 collective-permute-done.4.refs_4_
  56.5 2.7 %sums.1 = (f32[8,4,4096]{2,1,0:T(4,128)}, f32[1,1]{1,0:T(1,128)}) custom-call(f32[512,128]{1,0:T(8,128)S(1)} %bitcast.9, bf16[128,896]{1,0:T(8,128)(2,1)S(1)} %get-tuple-element.31.spread_ref, bf16[128,3584]{1,0:T(8,128)(2,1)S(1)} %bitcast.8, bf16[16,4096]{1,0:T(8,128)(2,1)S(1)} %get-tuple-element.32.outer_ref.refs_0_, ...), custom_call_target="tpu_custom_call" | custom-call | tf_op jit(solution)/shard_map/sums/pallas_call | solution.py:625
  (1 shorter events, 0.0 us)
Async XLA Ops:
  3.4 7.6 %copy-start.2 = (bf16[2,4,4096]{2,1,0:T(4,128)(2,1)S(1)}, bf16[2,4,4096]{2,1,0:T(4,128)(2,1)}, u32[]{:S(2)}) copy-start(bf16[2,4,4096]{2,1,0:T(4,128)(2,1)} %refs_hbm.1) | copy-start | bytes 196612
  3.4 12.0 %copy-start = (bf16[16,4096]{1,0:T(8,128)(2,1)S(1)}, bf16[16,4096]{1,0:T(8,128)(2,1)}, u32[]{:S(2)}) copy-start(bf16[16,4096]{1,0:T(8,128)(2,1)} %get-tuple-element.20.both_ref) | copy-start | bytes 393220
  3.4 29.3 %all-to-all-start = ((bf16[16,8,3584]{2,1,0:T(8,128)(2,1)}), bf16[16,8,3584]{2,1,0:T(8,128)(2,1)S(1)}, u32[]{:S(2)}, u32[]{:S(2)}) async-start(bf16[16,8,3584]{2,1,0:T(8,128)(2,1)} %bitcast.10), calls=%async_computation | async-start | bytes 1835008 | tf_op jit(solution)/shard_map/all_to_all | solution.py:563
  11.0 21.7 %collective-permute-start = (bf16[2,4,4096]{2,1,0:T(4,128)(2,1)S(1)}, bf16[2,4,4096]{2,1,0:T(4,128)(2,1)S(1)}, u32[]{:S(2)}, u32[]{:S(2)}) collective-permute-start(bf16[2,4,4096]{2,1,0:T(4,128)(2,1)S(1)} %copy-done.2), channel_id=1, source_target_pairs={{0,15},{1,14},{2,13},{3,12},{4,11},{5,10},{6,9},{7,8},{8,7},{9,6},... | collective-permute-start | bytes 196616 | tf_op jit(solution)/shard_map/ppermute | solution.py:537
  32.7 2.6 %copy-start.3 = (s32[16,6]{0,1:T(8,128)S(1)}, s32[16,6]{0,1:T(8,128)}, u32[]{:S(2)}) copy-start(s32[16,6]{0,1:T(8,128)} %param.6) | copy-start | bytes 1156
  33.1 15.0 %collective-permute-start.2 = (bf16[128,2048]{1,0:T(8,128)(2,1)S(1)}, bf16[128,2048]{1,0:T(8,128)(2,1)S(1)}, u32[]{:S(2)}, u32[]{:S(2)}) collective-permute-start(bf16[128,2048]{1,0:T(8,128)(2,1)S(1)} %get-tuple-element.30), channel_id=1, source_target_pairs={{0,16},{16,0},{1,17},{17,1},{2,18},{18,2},{3,19},{19,3},{4,20},{20... | collective-permute-start | bytes 1572872 | tf_op jit(solution)/shard_map/ppermute | solution.py:577
  34.7 0.7 %copy-start.1 = (s32[1,2]{1,0:T(1,128)S(1)}, s32[1,2]{1,0:T(1,128)}, u32[]{:S(2)}) copy-start(s32[1,2]{1,0:T(1,128)} %allowed_any.1) | copy-start | bytes 28
  34.7 4.4 %collective-permute-start.1 = (bf16[16,4096]{1,0:T(8,128)(2,1)S(1)}, bf16[16,4096]{1,0:T(8,128)(2,1)S(1)}, u32[]{:S(2)}, u32[]{:S(2)}) collective-permute-start(bf16[16,4096]{1,0:T(8,128)(2,1)S(1)} %get-tuple-element.28), channel_id=1, source_target_pairs={{0,1},{1,0},{2,3},{3,2},{4,5},{5,4},{6,7},{7,6},{8,9},{9,8},{10,11... | collective-permute-start | bytes 393224 | tf_op jit(solution)/shard_map/ppermute | solution.py:575
  40.1 16.4 %all-to-all-start.1 = ((f32[32,16,128]{2,1,0:T(8,128)}), f32[32,16,128]{2,1,0:T(8,128)S(1)}, u32[]{:S(2)}, u32[]{:S(2)}) async-start(f32[32,16,128]{2,1,0:T(8,128)} %bitcast.3), calls=%async_computation.1 | async-start | bytes 524288 | tf_op jit(solution)/shard_map/all_to_all | solution.py:608
  46.2 7.9 %collective-permute-start.3 = (bf16[16,4096]{1,0:T(8,128)(2,1)S(1)}, bf16[16,4096]{1,0:T(8,128)(2,1)S(1)}, u32[]{:S(2)}, u32[]{:S(2)}) collective-permute-start(bf16[16,4096]{1,0:T(8,128)(2,1)S(1)} %get-tuple-element.32.outer_ref.refs_0_), channel_id=1, source_target_pairs={{0,16},{16,0},{1,17},{17,1},{2,18},{18,2},{3,19},{19,3},{4,20},{20... | collective-permute-start | bytes 393224 | tf_op jit(solution)/shard_map/ppermute | solution.py:622
  48.4 8.2 %collective-permute-start.4 = (bf16[16,4096]{1,0:T(8,128)(2,1)S(1)}, bf16[16,4096]{1,0:T(8,128)(2,1)S(1)}, u32[]{:S(2)}, u32[]{:S(2)}) collective-permute-start(bf16[16,4096]{1,0:T(8,128)(2,1)S(1)} %get-tuple-element.33), channel_id=1, source_target_pairs={{0,1},{1,0},{2,3},{3,2},{4,5},{5,4},{6,7},{7,6},{8,9},{9,8},{10,11... | collective-permute-start | bytes 393224 | tf_op jit(solution)/shard_map/ppermute | solution.py:622

commit v6 on v5

--- a/solution.py
+++ b/solution.py
@@ -392,7 +392,7 @@
 
 def sums_kernel(edge, parts, total, groups, logits_ref, spread_ref, got_ref, *refs):
     pieces, refs = refs[: 3 * groups - 1], refs[3 * groups - 1 :]
-    out_hbm, log_ref, out_ref, sems, chances, weights, end_weights, table, extra, merged, ends = refs
+    out_ref, log_ref, chances, weights, end_weights, table, extra, merged, ends = refs
     h = edge // parts
     wide = edge * edge
     columns = wide // LANES
@@ -483,23 +483,12 @@
     def cut(slot, j):
         return table[slot * rows : (slot + 1) * rows, tile(j % columns)]
 
-    pieces = sems.shape[0]
-    copies = []
     for j in range(columns):
         turned = swap_halves(jnp.where(low, cut(1, j + 1) + cut(2, j), cut(1, j) + cut(2, j - 1)))
         value = cut(0, j) + extra[:, tile(j)] + turned
         value = value + pick_lanes(cut(3, j), after) + pick_lanes(cut(4, j), before)
         for o in range(owned):
             out_ref[o, :, tile(j)] = value[o * h : (o + 1) * h, :]
-        if (j + 1) % (columns // pieces) == 0:
-            number = len(copies)
-            part = pl.ds(number * (wide // pieces), wide // pieces)
-            copies.append(
-                pltpu.make_async_copy(out_ref.at[:, :, part], out_hbm.at[:, :, part], sems.at[number])
-            )
-            copies[-1].start()
-    for copy in copies:
-        copy.wait()
 
 
 def in_vmem():
@@ -626,10 +615,8 @@
         functools.partial(sums_kernel, edge, parts, total, groups),
         out_shape=(array((owned, h, wide), f32), array((1, 1), f32)),
         in_specs=[in_vmem()] * (3 + len(pieces)),
-        out_specs=(anywhere(), in_vmem()),
+        out_specs=(in_vmem(), in_vmem()),
         scratch_shapes=[
-            pltpu.VMEM((owned, h, wide), f32),
-            pltpu.SemaphoreType.DMA((8,)),
             pltpu.VMEM((groups, total, span), f32),
             pltpu.VMEM((ROWS // h * groups * parts * ROWS // LANES, len(FLAT) * owned * h, LANES), f32),
             pltpu.VMEM((max(every // LANES, 1), owned * h, LANES), f32),

time: 59.5 us -> 59 us (level)
  no operation moved by 1% of the time
where the time goes in v6:
time: 59 us; the launch traced here: 58.7 us
  waiting for transfers between devices  25.3 us (43%)
  starting transfers between devices  22.2 us (38%)
  Pallas kernels  10.4 us (18%)
  between operations  0.73 us (1%)
    ppermute x1, waiting for transfers between devices, per_device(): lax.ppermute(references, 'dp', [(i, parts - 1 - i) for i in range(parts)])  17.2 us
    all_to_all x1, starting transfers between devices, per_device(): got = lax.all_to_all(sent, 'dp', 0, 0, tiled=True)  7.53 us
    all_to_all x1, starting transfers between devices, per_device(): logits = lax.all_to_all(partial, ('ref', 'dp'), 0, 0, tiled=True)  6.1 us
    ppermute x1, waiting for transfers between devices, per_device(): lax.ppermute(outside, 'ref', step)  5.66 us
    ppermute x1, starting transfers between devices, per_device(): lax.ppermute(references, 'dp', [(i, parts - 1 - i) for i in range(parts)])  4.44 us
    pallas_call x1, Pallas kernels, per_device(): pl.pallas_call(functools.partial(logits_kernel, edge, parts, total), out_...  3.66 us
    pallas_call x1, Pallas kernels, per_device(): pl.pallas_call(functools.partial(pack_kernel, edge, parts), out_shape=(ar...  2.77 us
    all_to_all x1, waiting for transfers between devices, per_device(): logits = lax.all_to_all(partial, ('ref', 'dp'), 0, 0, tiled=True)  2.41 us
  transfers between devices with their start and end apart: 7, of which 3 were waited for; matrix products, arithmetic and copies ran while one was open for 0% of the time, Pallas kernels for 9%

profile of v6, /device:TPU:0, one launch (start us, length us, event | category | flops | bytes accessed | tf_op | source)
XLA Modules:
  0.0 58.7 jit_solution(17887773895153275112)
XLA Ops:
  0.6 2.8 %pack.1 = (bf16[128,3584]{1,0:T(8,128)(2,1)}, bf16[16,4096]{1,0:T(8,128)(2,1)}) custom-call(bf16[64,4096]{1,0:T(8,128)(2,1)} %bitcast.11, bf16[2,4,4096]{2,1,0:T(4,128)(2,1)} %refs_hbm.1), custom_call_target="tpu_custom_call" | custom-call | tf_op jit(solution)/shard_map/pack/pallas_call | solution.py:527
  3.4 0.0 copy-start.2
  3.4 0.0 copy-start
  3.4 7.5 %all-to-all-start = ((bf16[16,8,3584]{2,1,0:T(8,128)(2,1)}), bf16[16,8,3584]{2,1,0:T(8,128)(2,1)S(1)}, u32[]{:S(2)}, u32[]{:S(2)}) async-start(bf16[16,8,3584]{2,1,0:T(8,128)(2,1)} %bitcast.10), calls=%async_computation | async-start | bytes 1835008 | tf_op jit(solution)/shard_map/all_to_all | solution.py:552
  11.0 0.0 copy-done.2
  11.0 4.4 %collective-permute-start = (bf16[2,4,4096]{2,1,0:T(4,128)(2,1)S(1)}, bf16[2,4,4096]{2,1,0:T(4,128)(2,1)S(1)}, u32[]{:S(2)}, u32[]{:S(2)}) collective-permute-start(bf16[2,4,4096]{2,1,0:T(4,128)(2,1)S(1)} %copy-done.2), channel_id=1, source_target_pairs={{0,15},{1,14},{2,13},{3,12},{4,11},{5,10},{6,9},{7,8},{8,7},{9,6},... | collective-permute-start | bytes 196616 | tf_op jit(solution)/shard_map/ppermute | solution.py:526
  15.4 0.0 copy-done
  15.5 17.2 %collective-permute-done.far_ref = bf16[2,4,4096]{2,1,0:T(4,128)(2,1)S(1)} collective-permute-done((bf16[2,4,4096]{2,1,0:T(4,128)(2,1)S(1)}, bf16[2,4,4096]{2,1,0:T(4,128)(2,1)S(1)}, u32[]{:S(2)}, u32[]{:S(2)}) %collective-permute-start) | collective-permute-done | bytes 65568 | tf_op jit(solution)/shard_map/ppermute | solution.py:526
  32.7 0.0 all-to-all-done
  32.7 0.0 copy-start.3
  32.7 0.4 trim.1
  33.1 1.6 %collective-permute-start.2 = (bf16[128,2048]{1,0:T(8,128)(2,1)S(1)}, bf16[128,2048]{1,0:T(8,128)(2,1)S(1)}, u32[]{:S(2)}, u32[]{:S(2)}) collective-permute-start(bf16[128,2048]{1,0:T(8,128)(2,1)S(1)} %get-tuple-element.30), channel_id=1, source_target_pairs={{0,16},{16,0},{1,17},{17,1},{2,18},{18,2},{3,19},{19,3},{4,20},{20... | collective-permute-start | bytes 1572872 | tf_op jit(solution)/shard_map/ppermute | solution.py:566
  34.7 0.0 copy-start.1
  34.7 0.6 %collective-permute-start.1 = (bf16[16,4096]{1,0:T(8,128)(2,1)S(1)}, bf16[16,4096]{1,0:T(8,128)(2,1)S(1)}, u32[]{:S(2)}, u32[]{:S(2)}) collective-permute-start(bf16[16,4096]{1,0:T(8,128)(2,1)S(1)} %get-tuple-element.28), channel_id=1, source_target_pairs={{0,1},{1,0},{2,3},{3,2},{4,5},{5,4},{6,7},{7,6},{8,9},{9,8},{10,11... | collective-permute-start | bytes 393224 | tf_op jit(solution)/shard_map/ppermute | solution.py:564
  35.3 0.0 copy-done.3
  35.3 0.1 copy.6.orient_any
  35.4 0.0 copy-done.1
  35.4 3.7 %logits.1 = (f32[16,128]{1,0:T(8,128)S(1)}, bf16[64,4096]{1,0:T(8,128)(2,1)S(1)}, f32[16,128]{1,0:T(8,128)S(1)}) custom-call(s32[16,6]{1,0:T(8,128)S(1)} %copy.6.orient_any, s32[1,2]{1,0:T(1,128)S(1)} %copy-done.1, bf16[128,3584]{1,0:T(8,128)(2,1)S(1)} %bitcast.7, f32[128,8,128]{2,1,0:T(8,128)S(1)} %own.1.own_ref, ...), custom_call_target="tpu_custom_call" | custom-call | tf_op jit(solution)/shard_map/logits/pallas_call | solution.py:567
  39.0 0.0 collective-permute-done.1.inner_ref.refs_1_
  39.0 1.1 %finish.1 = f32[512,128]{1,0:T(8,128)} custom-call(f32[16,128]{1,0:T(8,128)S(1)} %get-tuple-element.24.part_ref, bf16[64,4096]{1,0:T(8,128)(2,1)S(1)} %get-tuple-element.25.base_ref, f32[16,128]{1,0:T(8,128)S(1)} %get-tuple-element.26.bar_ref, bf16[16,4096]{1,0:T(8,128)(2,1)S(1)} %get-tuple-element.32.outer_ref.refs_0_, ...), custom_call_target="tpu_custom_call" | custom-call | tf_op jit(solution)/shard_map/finish/pallas_call | solution.py:587
  40.1 6.1 %all-to-all-start.1 = ((f32[32,16,128]{2,1,0:T(8,128)}), f32[32,16,128]{2,1,0:T(8,128)S(1)}, u32[]{:S(2)}, u32[]{:S(2)}) async-start(f32[32,16,128]{2,1,0:T(8,128)} %bitcast.3), calls=%async_computation.1 | async-start | bytes 524288 | tf_op jit(solution)/shard_map/all_to_all | solution.py:597
  46.2 1.8 %collective-permute-start.3 = (bf16[16,4096]{1,0:T(8,128)(2,1)S(1)}, bf16[16,4096]{1,0:T(8,128)(2,1)S(1)}, u32[]{:S(2)}, u32[]{:S(2)}) collective-permute-start(bf16[16,4096]{1,0:T(8,128)(2,1)S(1)} %get-tuple-element.32.outer_ref.refs_0_), channel_id=1, source_target_pairs={{0,16},{16,0},{1,17},{17,1},{2,18},{18,2},{3,19},{19,3},{4,20},{20... | collective-permute-start | bytes 393224 | tf_op jit(solution)/shard_map/ppermute | solution.py:611
  48.1 0.0 collective-permute-done.2.core_ref.refs_2_
  48.1 0.3 far_ends.1
  48.4 0.1 collective-permute-start.4
  48.4 5.7 %collective-permute-done.3.refs_3_ = bf16[16,4096]{1,0:T(8,128)(2,1)S(1)} collective-permute-done((bf16[16,4096]{1,0:T(8,128)(2,1)S(1)}, bf16[16,4096]{1,0:T(8,128)(2,1)S(1)}, u32[]{:S(2)}, u32[]{:S(2)}) %collective-permute-start.3) | collective-permute-done | bytes 131104 | tf_op jit(solution)/shard_map/ppermute | solution.py:611
  54.1 2.4 %all-to-all-done.1 = f32[32,16,128]{2,1,0:T(8,128)S(1)} async-done(((f32[32,16,128]{2,1,0:T(8,128)}), f32[32,16,128]{2,1,0:T(8,128)S(1)}, u32[]{:S(2)}, u32[]{:S(2)}) %all-to-all-start.1) | async-done | bytes 262176 | tf_op jit(solution)/shard_map/all_to_all | solution.py:597
  56.5 0.0 collective-permute-done.4.refs_4_
  56.5 2.2 %sums.1 = (f32[8,4,4096]{2,1,0:T(4,128)}, f32[1,1]{1,0:T(1,128)}) custom-call(f32[512,128]{1,0:T(8,128)S(1)} %bitcast.9, bf16[128,896]{1,0:T(8,128)(2,1)S(1)} %get-tuple-element.31.spread_ref, bf16[128,3584]{1,0:T(8,128)(2,1)S(1)} %bitcast.8, bf16[16,4096]{1,0:T(8,128)(2,1)S(1)} %get-tuple-element.32.outer_ref.refs_0_, ...), custom_call_target="tpu_custom_call" | custom-call | tf_op jit(solution)/shard_map/sums/pallas_call | solution.py:614
  (1 shorter events, 0.0 us)
Async XLA Ops:
  3.4 7.6 %copy-start.2 = (bf16[2,4,4096]{2,1,0:T(4,128)(2,1)S(1)}, bf16[2,4,4096]{2,1,0:T(4,128)(2,1)}, u32[]{:S(2)}) copy-start(bf16[2,4,4096]{2,1,0:T(4,128)(2,1)} %refs_hbm.1) | copy-start | bytes 196612
  3.4 12.0 %copy-start = (bf16[16,4096]{1,0:T(8,128)(2,1)S(1)}, bf16[16,4096]{1,0:T(8,128)(2,1)}, u32[]{:S(2)}) copy-start(bf16[16,4096]{1,0:T(8,128)(2,1)} %get-tuple-element.20.both_ref) | copy-start | bytes 393220
  3.4 29.3 %all-to-all-start = ((bf16[16,8,3584]{2,1,0:T(8,128)(2,1)}), bf16[16,8,3584]{2,1,0:T(8,128)(2,1)S(1)}, u32[]{:S(2)}, u32[]{:S(2)}) async-start(bf16[16,8,3584]{2,1,0:T(8,128)(2,1)} %bitcast.10), calls=%async_computation | async-start | bytes 1835008 | tf_op jit(solution)/shard_map/all_to_all | solution.py:552
  11.0 21.7 %collective-permute-start = (bf16[2,4,4096]{2,1,0:T(4,128)(2,1)S(1)}, bf16[2,4,4096]{2,1,0:T(4,128)(2,1)S(1)}, u32[]{:S(2)}, u32[]{:S(2)}) collective-permute-start(bf16[2,4,4096]{2,1,0:T(4,128)(2,1)S(1)} %copy-done.2), channel_id=1, source_target_pairs={{0,15},{1,14},{2,13},{3,12},{4,11},{5,10},{6,9},{7,8},{8,7},{9,6},... | collective-permute-start | bytes 196616 | tf_op jit(solution)/shard_map/ppermute | solution.py:526
  32.7 2.6 %copy-start.3 = (s32[16,6]{0,1:T(8,128)S(1)}, s32[16,6]{0,1:T(8,128)}, u32[]{:S(2)}) copy-start(s32[16,6]{0,1:T(8,128)} %param.6) | copy-start | bytes 1156
  33.1 15.0 %collective-permute-start.2 = (bf16[128,2048]{1,0:T(8,128)(2,1)S(1)}, bf16[128,2048]{1,0:T(8,128)(2,1)S(1)}, u32[]{:S(2)}, u32[]{:S(2)}) collective-permute-start(bf16[128,2048]{1,0:T(8,128)(2,1)S(1)} %get-tuple-element.30), channel_id=1, source_target_pairs={{0,16},{16,0},{1,17},{17,1},{2,18},{18,2},{3,19},{19,3},{4,20},{20... | collective-permute-start | bytes 1572872 | tf_op jit(solution)/shard_map/ppermute | solution.py:566
  34.7 0.7 %copy-start.1 = (s32[1,2]{1,0:T(1,128)S(1)}, s32[1,2]{1,0:T(1,128)}, u32[]{:S(2)}) copy-start(s32[1,2]{1,0:T(1,128)} %allowed_any.1) | copy-start | bytes 28
  34.7 4.4 %collective-permute-start.1 = (bf16[16,4096]{1,0:T(8,128)(2,1)S(1)}, bf16[16,4096]{1,0:T(8,128)(2,1)S(1)}, u32[]{:S(2)}, u32[]{:S(2)}) collective-permute-start(bf16[16,4096]{1,0:T(8,128)(2,1)S(1)} %get-tuple-element.28), channel_id=1, source_target_pairs={{0,1},{1,0},{2,3},{3,2},{4,5},{5,4},{6,7},{7,6},{8,9},{9,8},{10,11... | collective-permute-start | bytes 393224 | tf_op jit(solution)/shard_map/ppermute | solution.py:564
  40.1 16.4 %all-to-all-start.1 = ((f32[32,16,128]{2,1,0:T(8,128)}), f32[32,16,128]{2,1,0:T(8,128)S(1)}, u32[]{:S(2)}, u32[]{:S(2)}) async-start(f32[32,16,128]{2,1,0:T(8,128)} %bitcast.3), calls=%async_computation.1 | async-start | bytes 524288 | tf_op jit(solution)/shard_map/all_to_all | solution.py:597
  46.2 7.9 %collective-permute-start.3 = (bf16[16,4096]{1,0:T(8,128)(2,1)S(1)}, bf16[16,4096]{1,0:T(8,128)(2,1)S(1)}, u32[]{:S(2)}, u32[]{:S(2)}) collective-permute-start(bf16[16,4096]{1,0:T(8,128)(2,1)S(1)} %get-tuple-element.32.outer_ref.refs_0_), channel_id=1, source_target_pairs={{0,16},{16,0},{1,17},{17,1},{2,18},{18,2},{3,19},{19,3},{4,20},{20... | collective-permute-start | bytes 393224 | tf_op jit(solution)/shard_map/ppermute | solution.py:611
  48.4 8.2 %collective-permute-start.4 = (bf16[16,4096]{1,0:T(8,128)(2,1)S(1)}, bf16[16,4096]{1,0:T(8,128)(2,1)S(1)}, u32[]{:S(2)}, u32[]{:S(2)}) collective-permute-start(bf16[16,4096]{1,0:T(8,128)(2,1)S(1)} %get-tuple-element.33), channel_id=1, source_target_pairs={{0,1},{1,0},{2,3},{3,2},{4,5},{5,4},{6,7},{7,6},{8,9},{9,8},{10,11... | collective-permute-start | bytes 393224 | tf_op jit(solution)/shard_map/ppermute | solution.py:611

commit v7 on v6

--- a/solution.py
+++ b/solution.py
@@ -45,7 +45,7 @@
 
 def lanes_of(edge, parts):
     h = edge // parts
-    return edge * edge * h // ROWS, edge * edge // ROWS, 4 * h * edge
+    return edge * edge * h // ROWS, 4 * h * edge
 
 
 def turn_rows(edge, planes, x, z, flat, turned):
@@ -81,7 +81,7 @@
 ):
     h = edge // parts
     planes = 2 * h
-    core, outer, _ = lanes_of(edge, parts)
+    core, _ = lanes_of(edge, parts)
     chunk = 2 * ROWS
     refs_copy = pltpu.make_async_copy(refs_hbm, refs_ref, sems.at[0])
     refs_copy.start()
@@ -102,7 +102,7 @@
         top = s * ROWS
         mirror = parts - 1 - s
         for number, (array, place) in enumerate(((x, s), (x, mirror), (z, s), (z, mirror))):
-            left = core + outer + number * slab
+            left = core + number * slab
             stage[top : top + planes, left : left + slab] = array[:planes, place * slab : (place + 1) * slab]
     last = len(copies) - 1
     done = 0
@@ -120,15 +120,12 @@
                 top, first = s * ROWS, ROWS + h * s
                 for f in range(ROWS // h):
                     stage[top + f * h : top + (f + 1) * h, :core] = ring[first : first + h, f * core : (f + 1) * core]
-                end = first - 1 if s % 2 == 0 else first + h
-                for e in range(ROWS):
-                    stage[top + e : top + e + 1, core : core + outer] = ring[end : end + 1, e * outer : (e + 1) * outer]
             both = slice(done * ROWS, (done + 2) * ROWS)
             out_ref[both, :] = stage[both, :].astype(jnp.bfloat16)
             done += 2
 
 
-def own_kernel(h, columns, both_ref, out_ref):
+def own_kernel(h, columns, parts, allowed_ref, both_ref, out_ref, bar_ref):
     planes = 2 * h
     own = both_ref[...].astype(jnp.float32)
     for turn in range(2):
@@ -137,28 +134,29 @@
             for copy in range(ROWS // h):
                 for m in range(columns):
                     out_ref[(turn * 2 + c) * columns + m, copy * h : (copy + 1) * h, :] = own[top : top + h, tile(m)]
+    kin = row_iota(bar_ref.shape) // ORI
+    permit = jnp.zeros(bar_ref.shape, jnp.int32)
+    for c in range(bar_ref.shape[0] // ORI):
+        permit = jnp.where(kin == c, allowed_ref[0, c], permit)
+    barred = (lane_iota(bar_ref.shape) % parts == lax.axis_index("dp")) & (permit != 1)
+    bar_ref[...] = jnp.where(barred, jnp.float32(BARRED), jnp.float32(0.0))
 
 
 def logits_kernel(
-    edge, parts, total, orient_any, allowed_any, got_ref, own_ref, far_ref, out_ref, base_ref, bar_ref,
-    orient_ref, allowed_ref, sems, x, z, far_flat, far_turned, wide_f32, flats, turneds, kinds, shifted, gram,
+    edge, parts, total, orient_any, got_ref, own_ref, far_ref, out_ref, base_ref,
+    orient_ref, sem, x, z, far_flat, far_turned, wide_f32, flats, turneds, kinds, shifted, gram,
 ):
     h = edge // parts
     wide = edge * edge
     columns = wide // LANES
     rows = total * h
-    core, outer, extra = lanes_of(edge, parts)
+    core, extra = lanes_of(edge, parts)
     planes = 2 * h
-    me = lax.axis_index("dp")
-    scalars = [
-        pltpu.make_async_copy(orient_any, orient_ref, sems.at[0]),
-        pltpu.make_async_copy(allowed_any, allowed_ref, sems.at[1]),
-    ]
-    for copy in scalars:
-        copy.start()
+    scalars = pltpu.make_async_copy(orient_any, orient_ref, sem)
+    scalars.start()
     low = lane_iota((ROWS, LANES)) < edge
     for j in range(extra // LANES):
-        wide_f32[j] = got_ref[:, tile((core + outer) // LANES + j)].astype(jnp.float32)
+        wide_f32[j] = got_ref[:, tile(core // LANES + j)].astype(jnp.float32)
 
     def keep(first, second, value, m):
         if planes == ROWS:
@@ -221,8 +219,7 @@
             odd = turned[pl.ds(2 * m + 1, planes, stride=edge), :]
             keep(axis * 8 + 4, axis * 8 + 6, jnp.where(part, even, swap_halves(odd)), m)
             keep(axis * 8 + 5, axis * 8 + 7, jnp.where(part, swap_halves(even), odd), m)
-    for copy in scalars:
-        copy.wait()
+    scalars.wait()
     lane = lane_iota((ROWS, LANES))
     slot = row_iota((ROWS, LANES)) // h
     per = ROWS // h
@@ -316,12 +313,6 @@
         picker = (row_iota(shape) // ROWS == lane_iota(shape)).astype(jnp.float32)
         result = exactly(jnp.concatenate(kept, axis=1), picker)
     out_ref[...] = result
-    kin = row_iota(result.shape) // ORI
-    permit = jnp.zeros(result.shape, jnp.int32)
-    for c in range(total // ORI):
-        permit = jnp.where(kin == c, allowed_ref[0, c], permit)
-    barred = (lane_iota(result.shape) % parts == me) & (permit != 1)
-    bar_ref[...] = jnp.where(barred, jnp.float32(BARRED), jnp.float32(0.0))
 
 
 def exactly(a, b):
@@ -355,26 +346,25 @@
         out_ref[d * total : (d + 1) * total, :] = result
 
 
-def trim_kernel(edge, parts, got_ref, core_ref, outer_ref, lacking_ref):
+def trim_kernel(edge, parts, got_ref, core_ref, *lacking):
     h = edge // parts
-    core, outer, _ = lanes_of(edge, parts)
+    core, _ = lanes_of(edge, parts)
     core_ref[...] = got_ref[:, :core]
-    whole = got_ref[:, core : core + outer].reshape(parts, ROWS, outer)
-    for e in range(ROWS):
-        outer_ref[:, e * outer : (e + 1) * outer] = whole[:, e, :]
-    own_end(h, got_ref[:, :core].reshape(parts, ROWS, core), lacking_ref)
-
-
-def own_end(h, whole, out_ref):
+    whole = got_ref[:, :core].reshape(parts, ROWS, core)
+    for last_if, ref in enumerate(lacking):
+        own_end(h, whole, last_if, ref)
+
+
+def own_end(h, whole, last_if, out_ref):
     core = whole.shape[2]
-    even = lax.axis_index("dp") % 2 == 0
-
-    @pl.when(even)
+    last = lax.axis_index("dp") % 2 == last_if
+
+    @pl.when(last)
     def _():
         for f in range(ROWS // h):
             out_ref[:, f * core : (f + 1) * core] = whole[:, f * h + h - 1, :]
 
-    @pl.when(jnp.logical_not(even))
+    @pl.when(jnp.logical_not(last))
     def _():
         for f in range(ROWS // h):
             out_ref[:, f * core : (f + 1) * core] = whole[:, f * h, :]
@@ -382,7 +372,7 @@
 
 def far_ends_kernel(h, core_ref, out_ref, *tables):
     parts = core_ref.shape[0] // ROWS
-    own_end(h, core_ref[...].reshape(parts, ROWS, core_ref.shape[1]), out_ref)
+    own_end(h, core_ref[...].reshape(parts, ROWS, core_ref.shape[1]), 0, out_ref)
     for table in tables:
         many = parts * ROWS
         column = lane_iota(table.shape)
@@ -400,7 +390,7 @@
     rows = owned * h
     span = SLOTS * parts
     many = parts * ROWS
-    core, _, _ = lanes_of(edge, parts)
+    core, _ = lanes_of(edge, parts)
     mine, me = lax.axis_index("ref"), lax.axis_index("dp")
     at_core, at_end = many, 0
     for piece in pieces:
@@ -511,7 +501,7 @@
     rows = total * h
     owned = total // groups
     span = SLOTS * parts
-    core_lanes, _, extra = lanes_of(edge, parts)
+    core_lanes, extra = lanes_of(edge, parts)
     payload = sum(lanes_of(edge, parts))
     scale = 3.0 / math.sqrt(edge**3)
     params = pltpu.CompilerParams(vmem_limit_bytes=VMEM_BYTES)
@@ -540,19 +530,19 @@
         compiler_params=pltpu.CompilerParams(vmem_limit_bytes=MOST_VMEM),
         name="pack",
     )(particles.reshape(edge, wide), references)
-    own = pl.pallas_call(
-        functools.partial(own_kernel, h, wide // LANES),
-        out_shape=array((4 * wide // LANES, ROWS, LANES), f32),
-        in_specs=[in_vmem()],
-        out_specs=in_vmem(),
+    own, bars = pl.pallas_call(
+        functools.partial(own_kernel, h, wide // LANES, parts),
+        out_shape=(array((4 * wide // LANES, ROWS, LANES), f32), array((total, span), f32)),
+        in_specs=[pl.BlockSpec(memory_space=pltpu.SMEM), in_vmem()],
+        out_specs=(in_vmem(), in_vmem()),
         compiler_params=params,
         cost_estimate=pl.CostEstimate(flops=0, bytes_accessed=16 * 1024 * 1024, transcendentals=0),
         name="own",
-    )(both)
+    )(allowed, both)
     got = lax.all_to_all(sent, "dp", 0, 0, tiled=True)
-    got, own, far = lax.optimization_barrier((got, own, far))
+    got, own, bars, far = lax.optimization_barrier((got, own, bars, far))
     plane = array((parts, wide), bf16)
-    core, outer, lacking = pl.pallas_call(
+    core, lacking, beyond = pl.pallas_call(
         functools.partial(trim_kernel, edge, parts),
         out_shape=(array((parts * ROWS, core_lanes), bf16), plane, plane),
         in_specs=[in_vmem()],
@@ -561,18 +551,19 @@
         name="trim",
     )(got)
     pairs = [(i, i ^ 1) for i in range(parts)]
+    across = [(i, (i + 1 if i % 2 else i - 1) % parts) for i in range(parts)]
+    outer = lax.ppermute(beyond, "dp", across)
     inner = lax.ppermute(lacking, "dp", pairs)
     steps = [[(i, (i + k) % groups) for i in range(groups)] for k in range(1, groups)]
     cores = [lax.ppermute(core, "ref", step) for step in steps]
-    partial, base, bars = pl.pallas_call(
+    partial, base = pl.pallas_call(
         functools.partial(logits_kernel, edge, parts, total),
-        out_shape=(array((total, span), f32), array((rows, wide), bf16), array((total, span), f32)),
-        in_specs=[anywhere()] * 2 + [in_vmem()] * 3,
-        out_specs=(in_vmem(),) * 3,
+        out_shape=(array((total, span), f32), array((rows, wide), bf16)),
+        in_specs=[anywhere()] + [in_vmem()] * 3,
+        out_specs=(in_vmem(),) * 2,
         scratch_shapes=[
             pltpu.SMEM(orient.shape, jnp.int32),
-            pltpu.SMEM(allowed.shape, jnp.int32),
-            pltpu.SemaphoreType.DMA((2,)),
+            pltpu.SemaphoreType.DMA,
             *turning,
             pltpu.VMEM((extra // LANES, parts * ROWS, LANES), f32),
             pltpu.VMEM((2, planes * edge, LANES), f32),
@@ -583,7 +574,7 @@
         ],
         compiler_params=params,
         name="logits",
-    )(orient, allowed, got, own, far)
+    )(orient, got, own, far)
     partial = pl.pallas_call(
         functools.partial(finish_kernel, h, parts, devices, scale),
         out_shape=array((devices * total, span), f32),

time: 59 us -> 58.5 us (level)
  waiting for transfers between devices: 25.3 us -> 22.7 us
  starting transfers between devices: 22.2 us -> 23.8 us
    ppermute x0 -> x1, starting transfers between devices: none -> 4.66 us  [per_device(): outer = lax.ppermute(beyond, 'dp', across)]
    ppermute x1, waiting for transfers between devices: 17.2 us -> 14.6 us  [per_device(): lax.ppermute(references, 'dp', [(i, parts - 1 - i) for i in range(parts)])]
    all_to_all x1, starting transfers between devices: 6.1 us -> 3.69 us  [per_device(): logits = lax.all_to_all(partial, ('ref', 'dp'), 0, 0, tiled=True)]
    ppermute x1, starting transfers between devices: 0.62 us -> 0.01 us  [per_device(): inner = lax.ppermute(lacking, 'dp', pairs)]
  transfers between devices with their start and end apart: 7 -> 8, of which waited for: 3 -> 3; matrix products, arithmetic and copies ran while one was open for 0% -> 0% of each run, Pallas kernels for 9% -> 10%
where the time goes in v7:
time: 58.5 us; the launch traced here: 58.2 us
  starting transfers between devices  23.8 us (41%)
  waiting for transfers between devices  22.7 us (39%)
  Pallas kernels  10.9 us (19%)
  between operations  0.75 us (1%)
    ppermute x1, waiting for transfers between devices, per_device(): lax.ppermute(references, 'dp', [(i, parts - 1 - i) for i in range(parts)])  14.6 us
    all_to_all x1, starting transfers between devices, per_device(): got = lax.all_to_all(sent, 'dp', 0, 0, tiled=True)  7.53 us
    ppermute x1, waiting for transfers between devices, per_device(): lax.ppermute(outside, 'ref', step)  5.66 us
    ppermute x1, starting transfers between devices, per_device(): outer = lax.ppermute(beyond, 'dp', across)  4.66 us
    ppermute x1, starting transfers between devices, per_device(): lax.ppermute(references, 'dp', [(i, parts - 1 - i) for i in range(parts)])  4.44 us
    all_to_all x1, starting transfers between devices, per_device(): logits = lax.all_to_all(partial, ('ref', 'dp'), 0, 0, tiled=True)  3.69 us
    pallas_call x1, Pallas kernels, per_device(): pl.pallas_call(functools.partial(logits_kernel, edge, parts, total), out_...  3.64 us
    pallas_call x1, Pallas kernels, per_device(): pl.pallas_call(functools.partial(pack_kernel, edge, parts), out_shape=(ar...  2.64 us
  transfers between devices with their start and end apart: 8, of which 3 were waited for; matrix products, arithmetic and copies ran while one was open for 0% of the time, Pallas kernels for 10%

profile of v7, /device:TPU:0, one launch (start us, length us, event | category | flops | bytes accessed | tf_op | source)
XLA Modules:
  0.0 58.2 jit_solution(2052498717317645006)
XLA Ops:
  0.6 2.6 %pack.1 = (bf16[128,3072]{1,0:T(8,128)(2,1)}, bf16[16,4096]{1,0:T(8,128)(2,1)}) custom-call(bf16[64,4096]{1,0:T(8,128)(2,1)} %bitcast.11, bf16[2,4,4096]{2,1,0:T(4,128)(2,1)} %refs_hbm.1), custom_call_target="tpu_custom_call" | custom-call | tf_op jit(solution)/shard_map/pack/pallas_call | solution.py:517
  3.3 0.0 copy-start.2
  3.3 0.0 copy-start
  3.3 7.5 %all-to-all-start = ((bf16[16,8,3072]{2,1,0:T(8,128)(2,1)}), bf16[16,8,3072]{2,1,0:T(8,128)(2,1)S(1)}, u32[]{:S(2)}, u32[]{:S(2)}) async-start(bf16[16,8,3072]{2,1,0:T(8,128)(2,1)} %bitcast.10), calls=%async_computation | async-start | bytes 1572864 | tf_op jit(solution)/shard_map/all_to_all | solution.py:542
  10.8 0.0 copy-done.2
  10.8 0.0 copy-start.1
  10.9 4.4 %collective-permute-start = (bf16[2,4,4096]{2,1,0:T(4,128)(2,1)S(1)}, bf16[2,4,4096]{2,1,0:T(4,128)(2,1)S(1)}, u32[]{:S(2)}, u32[]{:S(2)}) collective-permute-start(bf16[2,4,4096]{2,1,0:T(4,128)(2,1)S(1)} %copy-done.2), channel_id=1, source_target_pairs={{0,15},{1,14},{2,13},{3,12},{4,11},{5,10},{6,9},{7,8},{8,7},{9,6},... | collective-permute-start | bytes 196616 | tf_op jit(solution)/shard_map/ppermute | solution.py:516
  15.3 0.0 copy-done
  15.3 0.0 copy-done.1
  15.3 0.6 own.1
  15.9 14.6 %collective-permute-done.far_ref = bf16[2,4,4096]{2,1,0:T(4,128)(2,1)S(1)} collective-permute-done((bf16[2,4,4096]{2,1,0:T(4,128)(2,1)S(1)}, bf16[2,4,4096]{2,1,0:T(4,128)(2,1)S(1)}, u32[]{:S(2)}, u32[]{:S(2)}) %collective-permute-start) | collective-permute-done | bytes 65568 | tf_op jit(solution)/shard_map/ppermute | solution.py:516
  30.5 0.0 all-to-all-done
  30.5 0.5 trim.1
  30.9 0.0 copy-start.3
  31.0 1.6 %collective-permute-start.3 = (bf16[128,2048]{1,0:T(8,128)(2,1)S(1)}, bf16[128,2048]{1,0:T(8,128)(2,1)S(1)}, u32[]{:S(2)}, u32[]{:S(2)}) collective-permute-start(bf16[128,2048]{1,0:T(8,128)(2,1)S(1)} %get-tuple-element.34), channel_id=1, source_target_pairs={{0,16},{16,0},{1,17},{17,1},{2,18},{18,2},{3,19},{19,3},{4,20},{20... | collective-permute-start | bytes 1572872 | tf_op jit(solution)/shard_map/ppermute | solution.py:558
  32.5 4.7 %collective-permute-start.1 = (bf16[16,4096]{1,0:T(8,128)(2,1)S(1)}, bf16[16,4096]{1,0:T(8,128)(2,1)S(1)}, u32[]{:S(2)}, u32[]{:S(2)}) collective-permute-start(bf16[16,4096]{1,0:T(8,128)(2,1)S(1)} %get-tuple-element.31), channel_id=1, source_target_pairs={{0,15},{1,2},{2,1},{3,4},{4,3},{5,6},{6,5},{7,8},{8,7},{9,10},{10,... | collective-permute-start | bytes 393224 | tf_op jit(solution)/shard_map/ppermute | solution.py:555
  37.2 0.0 collective-permute-start.2
  37.2 0.0 copy-done.3
  37.2 0.1 copy.6.orient_any
  37.3 3.6 %logits.1 = (f32[16,128]{1,0:T(8,128)S(1)}, bf16[64,4096]{1,0:T(8,128)(2,1)S(1)}) custom-call(s32[16,6]{1,0:T(8,128)S(1)} %copy.6.orient_any, bf16[128,3072]{1,0:T(8,128)(2,1)S(1)} %bitcast.7, f32[128,8,128]{2,1,0:T(8,128)S(1)} %get-tuple-element.26.own_ref, bf16[2,4,4096]{2,1,0:T(4,128)(2,1)S(1)} %collective-permute-done.far_ref), custom_call_target="tpu_custom_call" | custom-call | tf_op jit(solution)/shard_map/logits/pallas_call | solution.py:559
  40.9 0.0 collective-permute-done.1.outer_ref.refs_0_
  40.9 0.0 collective-permute-done.2.inner_ref.refs_1_
  40.9 1.1 %finish.1 = f32[512,128]{1,0:T(8,128)} custom-call(f32[16,128]{1,0:T(8,128)S(1)} %get-tuple-element.28.part_ref, bf16[64,4096]{1,0:T(8,128)(2,1)S(1)} %get-tuple-element.29.base_ref, f32[16,128]{1,0:T(8,128)S(1)} %get-tuple-element.30.bar_ref, bf16[16,4096]{1,0:T(8,128)(2,1)S(1)} %collective-permute-done.1.outer_ref.refs_0_, ...), custom_call_target="tpu_custom_call" | custom-call | tf_op jit(solution)/shard_map/finish/pallas_call | solution.py:578
  42.0 3.7 %all-to-all-start.1 = ((f32[32,16,128]{2,1,0:T(8,128)}), f32[32,16,128]{2,1,0:T(8,128)S(1)}, u32[]{:S(2)}, u32[]{:S(2)}) async-start(f32[32,16,128]{2,1,0:T(8,128)} %bitcast.3), calls=%async_computation.1 | async-start | bytes 524288 | tf_op jit(solution)/shard_map/all_to_all | solution.py:588
  45.7 1.8 %collective-permute-start.4 = (bf16[16,4096]{1,0:T(8,128)(2,1)S(1)}, bf16[16,4096]{1,0:T(8,128)(2,1)S(1)}, u32[]{:S(2)}, u32[]{:S(2)}) collective-permute-start(bf16[16,4096]{1,0:T(8,128)(2,1)S(1)} %collective-permute-done.1.outer_ref.refs_0_), channel_id=1, source_target_pairs={{0,16},{16,0},{1,17},{17,1},{2,18},{18,2},{3,19},{19,3},{4,20},{20... | collective-permute-start | bytes 393224 | tf_op jit(solution)/shard_map/ppermute | solution.py:602
  47.5 0.0 collective-permute-done.3.core_ref.refs_2_
  47.5 0.3 far_ends.1
  47.8 0.1 collective-permute-start.5
  47.9 5.7 %collective-permute-done.4.refs_3_ = bf16[16,4096]{1,0:T(8,128)(2,1)S(1)} collective-permute-done((bf16[16,4096]{1,0:T(8,128)(2,1)S(1)}, bf16[16,4096]{1,0:T(8,128)(2,1)S(1)}, u32[]{:S(2)}, u32[]{:S(2)}) %collective-permute-start.4) | collective-permute-done | bytes 131104 | tf_op jit(solution)/shard_map/ppermute | solution.py:602
  53.6 2.4 %all-to-all-done.1 = f32[32,16,128]{2,1,0:T(8,128)S(1)} async-done(((f32[32,16,128]{2,1,0:T(8,128)}), f32[32,16,128]{2,1,0:T(8,128)S(1)}, u32[]{:S(2)}, u32[]{:S(2)}) %all-to-all-start.1) | async-done | bytes 262176 | tf_op jit(solution)/shard_map/all_to_all | solution.py:588
  56.0 0.0 collective-permute-done.5.refs_4_
  56.0 2.2 %sums.1 = (f32[8,4,4096]{2,1,0:T(4,128)}, f32[1,1]{1,0:T(1,128)}) custom-call(f32[512,128]{1,0:T(8,128)S(1)} %bitcast.9, bf16[128,896]{1,0:T(8,128)(2,1)S(1)} %get-tuple-element.35.spread_ref, bf16[128,3072]{1,0:T(8,128)(2,1)S(1)} %bitcast.8, bf16[16,4096]{1,0:T(8,128)(2,1)S(1)} %collective-permute-done.1.outer_ref.refs_0_, ...), custom_call_target="tpu_custom_call" | custom-call | tf_op jit(solution)/shard_map/sums/pallas_call | solution.py:605
Async XLA Ops:
  3.3 7.6 %copy-start.2 = (bf16[2,4,4096]{2,1,0:T(4,128)(2,1)S(1)}, bf16[2,4,4096]{2,1,0:T(4,128)(2,1)}, u32[]{:S(2)}) copy-start(bf16[2,4,4096]{2,1,0:T(4,128)(2,1)} %refs_hbm.1) | copy-start | bytes 196612
  3.3 12.0 %copy-start = (bf16[16,4096]{1,0:T(8,128)(2,1)S(1)}, bf16[16,4096]{1,0:T(8,128)(2,1)}, u32[]{:S(2)}) copy-start(bf16[16,4096]{1,0:T(8,128)(2,1)} %get-tuple-element.22.both_ref) | copy-start | bytes 393220
  3.3 27.2 %all-to-all-start = ((bf16[16,8,3072]{2,1,0:T(8,128)(2,1)}), bf16[16,8,3072]{2,1,0:T(8,128)(2,1)S(1)}, u32[]{:S(2)}, u32[]{:S(2)}) async-start(bf16[16,8,3072]{2,1,0:T(8,128)(2,1)} %bitcast.10), calls=%async_computation | async-start | bytes 1572864 | tf_op jit(solution)/shard_map/all_to_all | solution.py:542
  10.8 4.5 %copy-start.1 = (s32[1,2]{1,0:T(1,128)S(1)}, s32[1,2]{1,0:T(1,128)}, u32[]{:S(2)}) copy-start(s32[1,2]{1,0:T(1,128)} %allowed_ref.1) | copy-start | bytes 28
  10.9 19.6 %collective-permute-start = (bf16[2,4,4096]{2,1,0:T(4,128)(2,1)S(1)}, bf16[2,4,4096]{2,1,0:T(4,128)(2,1)S(1)}, u32[]{:S(2)}, u32[]{:S(2)}) collective-permute-start(bf16[2,4,4096]{2,1,0:T(4,128)(2,1)S(1)} %copy-done.2), channel_id=1, source_target_pairs={{0,15},{1,14},{2,13},{3,12},{4,11},{5,10},{6,9},{7,8},{8,7},{9,6},... | collective-permute-start | bytes 196616 | tf_op jit(solution)/shard_map/ppermute | solution.py:516
  30.9 6.2 %copy-start.3 = (s32[16,6]{0,1:T(8,128)S(1)}, s32[16,6]{0,1:T(8,128)}, u32[]{:S(2)}) copy-start(s32[16,6]{0,1:T(8,128)} %param.6) | copy-start | bytes 1156
  31.0 16.6 %collective-permute-start.3 = (bf16[128,2048]{1,0:T(8,128)(2,1)S(1)}, bf16[128,2048]{1,0:T(8,128)(2,1)S(1)}, u32[]{:S(2)}, u32[]{:S(2)}) collective-permute-start(bf16[128,2048]{1,0:T(8,128)(2,1)S(1)} %get-tuple-element.34), channel_id=1, source_target_pairs={{0,16},{16,0},{1,17},{17,1},{2,18},{18,2},{3,19},{19,3},{4,20},{20... | collective-permute-start | bytes 1572872 | tf_op jit(solution)/shard_map/ppermute | solution.py:558
  32.5 8.4 %collective-permute-start.1 = (bf16[16,4096]{1,0:T(8,128)(2,1)S(1)}, bf16[16,4096]{1,0:T(8,128)(2,1)S(1)}, u32[]{:S(2)}, u32[]{:S(2)}) collective-permute-start(bf16[16,4096]{1,0:T(8,128)(2,1)S(1)} %get-tuple-element.31), channel_id=1, source_target_pairs={{0,15},{1,2},{2,1},{3,4},{4,3},{5,6},{6,5},{7,8},{8,7},{9,10},{10,... | collective-permute-start | bytes 393224 | tf_op jit(solution)/shard_map/ppermute | solution.py:555
  37.2 3.8 %collective-permute-start.2 = (bf16[16,4096]{1,0:T(8,128)(2,1)S(1)}, bf16[16,4096]{1,0:T(8,128)(2,1)S(1)}, u32[]{:S(2)}, u32[]{:S(2)}) collective-permute-start(bf16[16,4096]{1,0:T(8,128)(2,1)S(1)} %get-tuple-element.32), channel_id=1, source_target_pairs={{0,1},{1,0},{2,3},{3,2},{4,5},{5,4},{6,7},{7,6},{8,9},{9,8},{10,11... | collective-permute-start | bytes 393224 | tf_op jit(solution)/shard_map/ppermute | solution.py:556
  42.0 14.0 %all-to-all-start.1 = ((f32[32,16,128]{2,1,0:T(8,128)}), f32[32,16,128]{2,1,0:T(8,128)S(1)}, u32[]{:S(2)}, u32[]{:S(2)}) async-start(f32[32,16,128]{2,1,0:T(8,128)} %bitcast.3), calls=%async_computation.1 | async-start | bytes 524288 | tf_op jit(solution)/shard_map/all_to_all | solution.py:588
  45.7 7.9 %collective-permute-start.4 = (bf16[16,4096]{1,0:T(8,128)(2,1)S(1)}, bf16[16,4096]{1,0:T(8,128)(2,1)S(1)}, u32[]{:S(2)}, u32[]{:S(2)}) collective-permute-start(bf16[16,4096]{1,0:T(8,128)(2,1)S(1)} %collective-permute-done.1.outer_ref.refs_0_), channel_id=1, source_target_pairs={{0,16},{16,0},{1,17},{17,1},{2,18},{18,2},{3,19},{19,3},{4,20},{20... | collective-permute-start | bytes 393224 | tf_op jit(solution)/shard_map/ppermute | solution.py:602
  47.8 8.2 %collective-permute-start.5 = (bf16[16,4096]{1,0:T(8,128)(2,1)S(1)}, bf16[16,4096]{1,0:T(8,128)(2,1)S(1)}, u32[]{:S(2)}, u32[]{:S(2)}) collective-permute-start(bf16[16,4096]{1,0:T(8,128)(2,1)S(1)} %get-tuple-element.37), channel_id=1, source_target_pairs={{0,1},{1,0},{2,3},{3,2},{4,5},{5,4},{6,7},{7,6},{8,9},{9,8},{10,11... | collective-permute-start | bytes 393224 | tf_op jit(solution)/shard_map/ppermute | solution.py:602
